TPU v7x, 32 devices: a whole 2x2x4 slice. The times are simulated.
32 devices in a mesh: groups: 2 (over x), grid: 8 (over z, y), dp: 2 (over core).
Axes of the slice: x: 2, y: 2, z: 4, core: 2. Of those that a mesh axis runs over, the one named last changes fastest.
Arguments:
- acts: bfloat16 [4, 8, 192, 2560], P(('groups', 'dp'), 'grid'), parts along dimension 0, may hold values from -6 to 6
- cotangent: bfloat16 [4, 8, 192, 2560], P(('groups', 'dp'), 'grid'), parts along dimension 0, may hold values from -1.5 to 1.5
- w_gate: bfloat16 [8, 2560, 1792], P('grid'), may hold values from -0.078125 to 0.078125
- w_up: bfloat16 [8, 2560, 1792], P('grid'), may hold values from -0.078125 to 0.078125
- w_down: bfloat16 [8, 1792, 2560], P('grid'), may hold values from -0.0625 to 0.0625
Outputs:
- block_out: bfloat16 [4, 8, 192, 2560], P(('groups', 'dp'), 'grid'), parts along dimension 0
- input_grad: bfloat16 [4, 8, 192, 2560], P(('groups', 'dp'), 'grid'), parts along dimension 0
- gate_grad: bfloat16 [16, 2560, 1792], P(('groups', 'grid')), parts along dimension 0
- up_grad: bfloat16 [16, 2560, 1792], P(('groups', 'grid')), parts along dimension 0
- down_grad: bfloat16 [16, 1792, 2560], P(('groups', 'grid')), parts along dimension 0
There are 2 independent parts, one for each index of `groups`. A program takes and returns all parts, laid end to end along the dimension named above; an argument that names none is the same for every part. Nothing has to cross between parts.
All inputs are finite; a program needn't handle non-finite values.
Results may differ from a plain program's by a relative error of at most 0.015.
Values may be sent and summed in bfloat16 or wider, within the bound.
No kernel may reach another device: no remote copies, remote signals or barrier semaphores. Data moves between devices by JAX's collectives and lax.ppermute only.
A program may use at most 192 MiB of HBM per device.

v0:
```python
import jax
import jax.numpy as jnp
from jax import lax
from jax.sharding import PartitionSpec as P


def from_partner(block, axis, stride):
    count = lax.axis_size(axis)
    route = []
    for low in range(count):
        high = low | 1 << stride
        if high != low and high < count:
            route += [(low, high), (high, low)]
    return lax.ppermute(block, axis, route)


def contract_rows(left, right):
    return lax.dot_general(
        left, right, (((0,), (0,)), ((), ())), preferred_element_type=jnp.float32
    )


def contract_cols(left, right):
    return lax.dot_general(
        left, right, (((1,), (1,)), ((), ())), preferred_element_type=jnp.float32
    )


def order_pair(is_upper, mine, other):
    return jnp.where(is_upper, jnp.concatenate([other, mine], 1), jnp.concatenate([mine, other], 1))


def column_sum(partial_term, total_rows, col_bits, row_bits, my_row):
    result_sum = partial_term(0, total_rows)
    for level_bit in range(row_bits - 1, -1, -1):
        half_rows = result_sum.shape[1] // 2
        lower_half = result_sum[:, :half_rows]
        upper_half = result_sum[:, half_rows:]
        is_upper = my_row >> level_bit & 1 == 1
        kept_half = jnp.where(is_upper, upper_half, lower_half)
        given_half = jnp.where(is_upper, lower_half, upper_half)
        result_sum = kept_half + from_partner(
            given_half.astype(jnp.bfloat16), "grid", col_bits + level_bit
        ).astype(given_half.dtype)
    return result_sum


def column_gather(pieces, col_bits, row_bits, my_row):
    for level_bit in range(row_bits):
        partner = from_partner(pieces, "grid", col_bits + level_bit)
        pieces = order_pair(my_row >> level_bit & 1 == 1, pieces, partner)
    return pieces


def row_sum(full_sum, col_bits, my_col):
    for level_bit in range(col_bits - 1, -1, -1):
        half_rows = full_sum.shape[0] // 2
        lower_half = full_sum[:half_rows]
        upper_half = full_sum[half_rows:]
        is_upper = my_col >> level_bit & 1 == 1
        kept_half = jnp.where(is_upper, upper_half, lower_half)
        given_half = jnp.where(is_upper, lower_half, upper_half)
        full_sum = kept_half + from_partner(
            given_half.astype(jnp.bfloat16), "grid", level_bit
        ).astype(given_half.dtype)
    return full_sum


def per_device(acts, cotangent, w_gate, w_up, w_down):
    grid_size = lax.axis_size("grid")
    grid_cols = min(8, grid_size // 2)
    grid_rows = grid_size // grid_cols
    col_bits = grid_cols.bit_length() - 1
    row_bits = grid_rows.bit_length() - 1
    position = lax.axis_index("grid")
    my_row = position // grid_cols
    my_col = position % grid_cols
    own_acts = acts[0, 0]
    own_grads = cotangent[0, 0]
    gate_tile = w_gate[0]
    up_tile = w_up[0]
    down_tile = w_down[0]
    gathered = jnp.stack([own_acts, own_grads])
    for level_bit in range(col_bits):
        partner = from_partner(gathered, "grid", level_bit)
        gathered = order_pair(my_col >> level_bit & 1 == 1, gathered, partner)
    inputs_row = gathered[0]
    out_grad_row = gathered[1]
    total_rows = inputs_row.shape[0]

    def gate_up_term(row_start, row_count):
        return jnp.stack(
            [
                jnp.dot(inputs_row, gate_tile, preferred_element_type=jnp.float32),
                jnp.dot(inputs_row, up_tile, preferred_element_type=jnp.float32),
            ]
        )

    summed = column_sum(gate_up_term, total_rows, col_bits, row_bits, my_row)
    gate_pre = summed[0]
    up_proj = summed[1]
    sigmoid_g = jax.nn.sigmoid(gate_pre)
    activated = gate_pre * sigmoid_g
    hidden = (activated * up_proj).astype(jnp.bfloat16)
    hidden_full = column_gather(hidden[None], col_bits, row_bits, my_row)[0]
    output_sum = row_sum(
        jnp.dot(hidden_full, down_tile, preferred_element_type=jnp.float32), col_bits, my_col
    )
    block_out = (own_acts.astype(jnp.float32) + output_sum).astype(jnp.bfloat16)

    def hidden_grad_term(row_start, row_count):
        return contract_cols(out_grad_row, down_tile)[None]

    hidden_grad = column_sum(hidden_grad_term, total_rows, col_bits, row_bits, my_row)[0]
    gate_back = (hidden_grad * up_proj * sigmoid_g * (1.0 + gate_pre * (1.0 - sigmoid_g))).astype(
        jnp.bfloat16
    )
    up_back = (hidden_grad * activated).astype(jnp.bfloat16)
    backs_full = column_gather(jnp.stack([gate_back, up_back]), col_bits, row_bits, my_row)
    down_local = contract_rows(hidden_full, out_grad_row)
    input_part = contract_cols(backs_full[0], gate_tile) + contract_cols(backs_full[1], up_tile)
    input_sum = row_sum(input_part, col_bits, my_col)
    input_grad = (own_grads.astype(jnp.float32) + input_sum).astype(jnp.bfloat16)
    gate_local = contract_rows(inputs_row, backs_full[0])
    up_local = contract_rows(inputs_row, backs_full[1])
    gate_total, up_total, down_total = (
        lax.psum(gate_local.astype(jnp.bfloat16), "dp").astype(jnp.float32),
        lax.psum(up_local.astype(jnp.bfloat16), "dp").astype(jnp.float32),
        lax.psum(down_local.astype(jnp.bfloat16), "dp").astype(jnp.float32),
    )
    return (
        block_out[None, None],
        input_grad[None, None],
        gate_total.astype(jnp.bfloat16)[None],
        up_total.astype(jnp.bfloat16)[None],
        down_total.astype(jnp.bfloat16)[None],
    )


def solution(mesh):
    return jax.shard_map(
        per_device,
        mesh=mesh,
        in_specs=(
            P(("groups", "dp"), "grid", None, None),
            P(("groups", "dp"), "grid", None, None),
            P("grid", None, None),
            P("grid", None, None),
            P("grid", None, None),
        ),
        out_specs=(
            P(("groups", "dp"), "grid", None, None),
            P(("groups", "dp"), "grid", None, None),
            P(("groups", "grid"), None, None),
            P(("groups", "grid"), None, None),
            P(("groups", "grid"), None, None),
        ),
        check_vma=False,
    )
```

profile of v0, /device:TPU:0, one launch (start us, length us, event | category | flops | bytes accessed | tf_op | source)
XLA Modules:
  0.0 722.5 jit_solution(10330217533321276245)
XLA Ops:
  7.2 3.1 pad_maximum_fusion.2
  10.3 3.0 collective-permute-start
  13.3 43.1 %collective-permute-done = bf16[2,192,2560]{2,1,0:T(8,128)(2,1)} collective-permute-done((bf16[2,192,2560]{2,1,0:T(8,128)(2,1)}, bf16[2,192,2560]{2,1,0:T(8,128)(2,1)}, u32[]{:S(2)}, u32[]{:S(2)}) %collective-permute-start) | collective-permute-done | bytes 1966112 | tf_op jit(solution)/shard_map/ppermute | solution.py:14
  56.4 4.0 maximum_select_fusion.2
  62.2 84.7 %collective-permute-done.1 = bf16[2,384,2560]{2,1,0:T(8,128)(2,1)} collective-permute-done((bf16[2,384,2560]{2,1,0:T(8,128)(2,1)}, bf16[2,384,2560]{2,1,0:T(8,128)(2,1)}, u32[]{:S(2)}, u32[]{:S(2)}) %collective-permute-start.1) | collective-permute-done | bytes 3932192 | tf_op jit(solution)/shard_map/ppermute | solution.py:14
  146.8 6.7 maximum_select_fusion
  153.6 13.7 %fusion.22 = f32[1,768,1792]{2,1,0:T(8,128)S(1)} fusion(bf16[1,2560,1792]{2,1,0:T(8,128)(2,1)} %param.8, bf16[2,768,2560]{2,1,0:T(8,128)(2,1)S(1)} %maximum_select_fusion), kind=kOutput, calls=%fused_computation.35 | convolution fusion | flops 7046430720 | bytes 18612224 | tf_op jit(solution)/shard_map/dot_general | solution.py:95
  167.3 10.9 %fusion.19 = f32[1,768,1792]{2,1,0:T(8,128)S(1)} fusion(bf16[1,2560,1792]{2,1,0:T(8,128)(2,1)} %param.7, bf16[2,768,2560]{2,1,0:T(8,128)(2,1)S(1)} %maximum_select_fusion), kind=kOutput, calls=%fused_computation.34 | convolution fusion | flops 7046430720 | bytes 18612224 | tf_op jit(solution)/shard_map/dot_general | solution.py:94
  178.2 2.0 select_convert_fusion
  180.1 2.5 collective-permute-start.2
  182.6 10.6 %fusion.25 = f32[1,768,1792]{2,1,0:T(8,128)S(1)} fusion(bf16[1,1792,2560]{2,1,0:T(8,128)(2,1)} %param.9, bf16[2,768,2560]{2,1,0:T(8,128)(2,1)} %copy-done.4), kind=kOutput, calls=%fused_computation.36 | convolution fusion | flops 7046430720 | bytes 18612224 | tf_op jit(solution)/shard_map/dot_general | solution.py:24
  194.0 136.5 %collective-permute-done.2 = bf16[2,384,1792]{2,1,0:T(8,128)(2,1)} collective-permute-done((bf16[2,384,1792]{2,1,0:T(8,128)(2,1)}, bf16[2,384,1792]{2,1,0:T(8,128)(2,1)}, u32[]{:S(2)}, u32[]{:S(2)}) %collective-permute-start.2) | collective-permute-done | bytes 2752544 | tf_op jit(solution)/shard_map/ppermute | solution.py:14
  330.5 2.5 convert_add_fusion
  333.0 26.1 %collective-permute-done.6 = bf16[1,384,1792]{2,1,0:T(8,128)(2,1)S(1)} collective-permute-done((bf16[1,384,1792]{2,1,0:T(8,128)(2,1)S(1)}, bf16[1,384,1792]{2,1,0:T(8,128)(2,1)S(1)}, u32[]{:S(2)}, u32[]{:S(2)}) %collective-permute-start.6) | collective-permute-done | bytes 1376288 | tf_op jit(solution)/shard_map/ppermute | solution.py:14
  359.1 1.9 multiply_convert_fusion.1
  361.4 3.0 collective-permute-start.7
  364.3 118.8 %collective-permute-done.3 = bf16[1,384,1792]{2,1,0:T(8,128)(2,1)S(1)} collective-permute-done((bf16[1,384,1792]{2,1,0:T(8,128)(2,1)S(1)}, bf16[1,384,1792]{2,1,0:T(8,128)(2,1)S(1)}, u32[]{:S(2)}, u32[]{:S(2)}) %collective-permute-start.3) | collective-permute-done | bytes 1376288 | tf_op jit(solution)/shard_map/ppermute | solution.py:14
  483.2 12.8 %fusion.2 = bf16[1,1792,2560]{2,1,0:T(8,128)(2,1)} fusion(bf16[2,768,2560]{2,1,0:T(8,128)(2,1)} %copy-done.4, bf16[384,1792]{1,0:T(8,128)(2,1)} %bitcast.73, bf16[384,1792]{1,0:T(8,128)(2,1)S(1)} %bitcast.75, pred[]{:T(512)S(6)} %eq.10), kind=kOutput, calls=%fused_computation.7 | convolution fusion | flops 7063404544 | bytes 15859713 | tf_op jit(solution)/shard_map/dot_general | solution.py:18
  496.0 44.9 %collective-permute-done.7 = bf16[2,384,1792]{2,1,0:T(8,128)(2,1)S(1)} collective-permute-done((bf16[2,384,1792]{2,1,0:T(8,128)(2,1)S(1)}, bf16[2,384,1792]{2,1,0:T(8,128)(2,1)S(1)}, u32[]{:S(2)}, u32[]{:S(2)}) %collective-permute-start.7) | collective-permute-done | bytes 2752544 | tf_op jit(solution)/shard_map/ppermute | solution.py:14
  540.9 5.3 maximum_select_fusion.1
  546.2 10.0 %fusion.1 = bf16[1,2560,1792]{2,1,0:T(8,128)(2,1)} fusion(bf16[2,768,2560]{2,1,0:T(8,128)(2,1)S(1)} %bitcast.72, bf16[2,768,1792]{2,1,0:T(8,128)(2,1)S(1)} %maximum_select_fusion.1), kind=kOutput, calls=%fused_computation.6 | convolution fusion | flops 7051018240 | bytes 15859712 | tf_op jit(solution)/shard_map/dot_general | solution.py:18
  556.3 9.8 %fusion = bf16[1,2560,1792]{2,1,0:T(8,128)(2,1)} fusion(bf16[2,768,2560]{2,1,0:T(8,128)(2,1)S(1)} %bitcast.72, bf16[2,768,1792]{2,1,0:T(8,128)(2,1)S(1)} %maximum_select_fusion.1), kind=kOutput, calls=%fused_computation.5 | convolution fusion | flops 7051018240 | bytes 15859712 | tf_op jit(solution)/shard_map/dot_general | solution.py:18
  567.4 12.4 %fusion.5 = f32[768,2560]{1,0:T(8,128)S(1)} fusion(bf16[1,1792,2560]{2,1,0:T(8,128)(2,1)} %param.9, bf16[384,1792]{1,0:T(8,128)(2,1)S(1)} %bitcast.74, bf16[384,1792]{1,0:T(8,128)(2,1)} %bitcast.76, pred[]{:T(512)S(6)} %eq.10), kind=kOutput, calls=%fused_computation.10 | convolution fusion | flops 7058817024 | bytes 19791872 | tf_op jit(solution)/shard_map/dot_general | solution.py:107
  581.5 2.9 copy-done.6
  584.3 13.7 %fusion.7 = f32[768,2560]{1,0:T(8,128)} fusion(bf16[1,2560,1792]{2,1,0:T(8,128)(2,1)} %param.8, bf16[2,768,1792]{2,1,0:T(8,128)(2,1)S(1)} %copy-done.6), kind=kOutput, calls=%fused_computation.12 | convolution fusion | flops 7046430720 | bytes 19791872 | tf_op jit(solution)/shard_map/dot_general | solution.py:24
  598.1 12.6 %fusion.15 = f32[768,2560]{1,0:T(8,128)S(1)} fusion(f32[768,2560]{1,0:T(8,128)} %fusion.7, bf16[1,2560,1792]{2,1,0:T(8,128)(2,1)} %param.7, bf16[2,768,1792]{2,1,0:T(8,128)(2,1)} %copy-done.5), kind=kOutput, calls=%fused_computation.21 | convolution fusion | flops 7048396800 | bytes 27656192 | tf_op jit(solution)/shard_map/dot_general | solution.py:24
  611.1 16.3 %collective-permute-done.4 = bf16[384,2560]{1,0:T(8,128)(2,1)S(1)} collective-permute-done((bf16[384,2560]{1,0:T(8,128)(2,1)}, bf16[384,2560]{1,0:T(8,128)(2,1)S(1)}, u32[]{:S(2)}, u32[]{:S(2)}) %collective-permute-start.4) | collective-permute-done | bytes 1966112 | tf_op jit(solution)/shard_map/ppermute | solution.py:14
  629.3 38.1 %collective-permute-done.8 = bf16[384,2560]{1,0:T(8,128)(2,1)S(1)} collective-permute-done((bf16[384,2560]{1,0:T(8,128)(2,1)S(1)}, bf16[384,2560]{1,0:T(8,128)(2,1)S(1)}, u32[]{:S(2)}, u32[]{:S(2)}) %collective-permute-start.8) | collective-permute-done | bytes 1966112 | tf_op jit(solution)/shard_map/ppermute | solution.py:14
  670.1 20.1 %collective-permute-done.9 = bf16[192,2560]{1,0:T(8,128)(2,1)S(1)} collective-permute-done((bf16[192,2560]{1,0:T(8,128)(2,1)S(1)}, bf16[192,2560]{1,0:T(8,128)(2,1)S(1)}, u32[]{:S(2)}, u32[]{:S(2)}) %collective-permute-start.9) | collective-permute-done | bytes 983072 | tf_op jit(solution)/shard_map/ppermute | solution.py:14
  691.6 7.8 %copy.13 = bf16[1,2560,1792]{2,1,0:T(8,128)(2,1)} copy(bf16[1,2560,1792]{2,1,0:T(8,128)(2,1)} %get-tuple-element.13) | data formatting | bytes 18350080
  699.5 7.8 %copy.14 = bf16[1,2560,1792]{2,1,0:T(8,128)(2,1)} copy(bf16[1,2560,1792]{2,1,0:T(8,128)(2,1)} %get-tuple-element.14) | data formatting | bytes 18350080
  707.3 7.9 %copy.15 = bf16[1,1792,2560]{2,1,0:T(8,128)(2,1)} copy(bf16[1,1792,2560]{2,1,0:T(8,128)(2,1)} %get-tuple-element.15) | data formatting | bytes 18350080
  (45 shorter events, 12.3 us)
Async XLA Ops:
  7.2 49.3 %copy-start.2 = (bf16[1,1,192,2560]{3,2,1,0:T(8,128)(2,1)S(1)}, bf16[1,1,192,2560]{3,2,1,0:T(8,128)(2,1)}, u32[]{:S(2)}) copy-start(bf16[1,1,192,2560]{3,2,1,0:T(8,128)(2,1)} %param.6) | copy-start | bytes 2949124
  7.2 49.2 %copy-start = (bf16[1,1,192,2560]{3,2,1,0:T(8,128)(2,1)S(1)}, bf16[1,1,192,2560]{3,2,1,0:T(8,128)(2,1)}, u32[]{:S(2)}) copy-start(bf16[1,1,192,2560]{3,2,1,0:T(8,128)(2,1)} %param.5) | copy-start | bytes 2949124
  7.2 684.4 %all-reduce.3.cloned.1.call-start = ((), (), s32[]{:S(2)}) async-start(), calls=%async_computation | async-start | bytes 55050240 | tf_op jit(solution)/shard_map/psum | solution.py:127
  10.3 46.1 %collective-permute-start = (bf16[2,192,2560]{2,1,0:T(8,128)(2,1)}, bf16[2,192,2560]{2,1,0:T(8,128)(2,1)}, u32[]{:S(2)}, u32[]{:S(2)}) collective-permute-start(bf16[2,192,2560]{2,1,0:T(8,128)(2,1)} %pad_maximum_fusion.2), channel_id=1, source_target_pairs={{0,2},{2,0},{4,6},{6,4},{8,10},{10,8},{12,14},{14,12},{1,3},{3,1},... | collective-permute-start | bytes 5898248 | tf_op jit(solution)/shard_map/ppermute | solution.py:14
  60.4 86.5 %collective-permute-start.1 = (bf16[2,384,2560]{2,1,0:T(8,128)(2,1)}, bf16[2,384,2560]{2,1,0:T(8,128)(2,1)}, u32[]{:S(2)}, u32[]{:S(2)}) collective-permute-start(bf16[2,384,2560]{2,1,0:T(8,128)(2,1)} %maximum_select_fusion.2), channel_id=1, source_target_pairs={{0,4},{4,0},{2,6},{6,2},{8,12},{12,8},{10,14},{14,10},{1,5},{5,1},... | collective-permute-start | bytes 11796488 | tf_op jit(solution)/shard_map/ppermute | solution.py:14
  153.6 13.7 %copy-start.4 = (bf16[2,768,2560]{2,1,0:T(8,128)(2,1)}, bf16[2,768,2560]{2,1,0:T(8,128)(2,1)S(1)}, u32[]{:S(2)}) copy-start(bf16[2,768,2560]{2,1,0:T(8,128)(2,1)S(1)} %maximum_select_fusion) | copy-start | bytes 23592964
  180.1 150.4 %collective-permute-start.2 = (bf16[2,384,1792]{2,1,0:T(8,128)(2,1)}, bf16[2,384,1792]{2,1,0:T(8,128)(2,1)}, u32[]{:S(2)}, u32[]{:S(2)}) collective-permute-start(bf16[2,384,1792]{2,1,0:T(8,128)(2,1)} %select_convert_fusion), channel_id=1, source_target_pairs={{0,8},{8,0},{2,10},{10,2},{4,12},{12,4},{6,14},{14,6},{1,9},{9,1},... | collective-permute-start | bytes 8257544 | tf_op jit(solution)/shard_map/ppermute | solution.py:14
  193.5 165.6 %collective-permute-start.6 = (bf16[1,384,1792]{2,1,0:T(8,128)(2,1)S(1)}, bf16[1,384,1792]{2,1,0:T(8,128)(2,1)S(1)}, u32[]{:S(2)}, u32[]{:S(2)}) collective-permute-start(bf16[1,384,1792]{2,1,0:T(8,128)(2,1)S(1)} %select_convert_fusion.3), channel_id=1, source_target_pairs={{0,8},{8,0},{2,10},{10,2},{4,12},{12,4},{6,14},{14,6},{1,9},{9,1},... | collective-permute-start | bytes 4128776 | tf_op jit(solution)/shard_map/ppermute | solution.py:14
  361.0 3.3 copy-start.7
  361.0 122.1 %collective-permute-start.3 = (bf16[1,384,1792]{2,1,0:T(8,128)(2,1)S(1)}, bf16[1,384,1792]{2,1,0:T(8,128)(2,1)S(1)}, u32[]{:S(2)}, u32[]{:S(2)}) collective-permute-start(bf16[1,384,1792]{2,1,0:T(8,128)(2,1)S(1)} %get-tuple-element.10), channel_id=1, source_target_pairs={{0,8},{8,0},{2,10},{10,2},{4,12},{12,4},{6,14},{14,6},{1,9},{9,1},... | collective-permute-start | bytes 4128776 | tf_op jit(solution)/shard_map/ppermute | solution.py:14
  361.1 185.1 %slice-start = ((s8[7864320]{0:T(1024)(128)(4,1)}), s8[4194304]{0:T(1024)(128)(4,1)S(1)}, s32[]{:S(2)}) async-start(s8[7864320]{0:T(1024)(128)(4,1)} %bitcast.71), calls=%async_computation.1 | async-start | bytes 8388608
  361.4 179.5 %collective-permute-start.7 = (bf16[2,384,1792]{2,1,0:T(8,128)(2,1)S(1)}, bf16[2,384,1792]{2,1,0:T(8,128)(2,1)S(1)}, u32[]{:S(2)}, u32[]{:S(2)}) collective-permute-start(bf16[2,384,1792]{2,1,0:T(8,128)(2,1)S(1)} %pad_maximum_fusion.1), channel_id=1, source_target_pairs={{0,8},{8,0},{2,10},{10,2},{4,12},{12,4},{6,14},{14,6},{1,9},{9,1},... | collective-permute-start | bytes 8257544 | tf_op jit(solution)/shard_map/ppermute | solution.py:14
  483.2 12.8 %copy-start.9 = (bf16[1,384,1792]{2,1,0:T(8,128)(2,1)}, bf16[1,384,1792]{2,1,0:T(8,128)(2,1)S(1)}, u32[]{:S(2)}) copy-start(bf16[1,384,1792]{2,1,0:T(8,128)(2,1)S(1)} %collective-permute-done.3) | copy-start | bytes 4128772
  483.2 63.0 %slice-start.1 = ((s8[7864320]{0:T(1024)(128)(4,1)}), s8[3670016]{0:T(1024)(128)(4,1)S(1)}, s32[]{:S(2)}) async-start(s8[7864320]{0:T(1024)(128)(4,1)} %bitcast.71), calls=%async_computation.2 | async-start | bytes 7340032
  546.2 10.0 %copy-start.5 = (bf16[2,768,1792]{2,1,0:T(8,128)(2,1)}, bf16[2,768,1792]{2,1,0:T(8,128)(2,1)S(1)}, u32[]{:S(2)}) copy-start(bf16[2,768,1792]{2,1,0:T(8,128)(2,1)S(1)} %maximum_select_fusion.1) | copy-start | bytes 16515076
  566.1 1.3 copy-start.8
  579.8 4.5 copy-start.6
  581.5 46.0 %collective-permute-start.4 = (bf16[384,2560]{1,0:T(8,128)(2,1)}, bf16[384,2560]{1,0:T(8,128)(2,1)S(1)}, u32[]{:S(2)}, u32[]{:S(2)}) collective-permute-start(bf16[384,2560]{1,0:T(8,128)(2,1)} %select_convert_fusion.2), channel_id=1, source_target_pairs={{0,4},{4,0},{2,6},{6,2},{8,12},{12,8},{10,14},{14,10},{1,5},{5,1},... | collective-permute-start | bytes 5898248 | tf_op jit(solution)/shard_map/ppermute | solution.py:14
  611.1 56.3 %collective-permute-start.8 = (bf16[384,2560]{1,0:T(8,128)(2,1)S(1)}, bf16[384,2560]{1,0:T(8,128)(2,1)S(1)}, u32[]{:S(2)}, u32[]{:S(2)}) collective-permute-start(bf16[384,2560]{1,0:T(8,128)(2,1)S(1)} %select_convert_fusion.1), channel_id=1, source_target_pairs={{0,4},{4,0},{2,6},{6,2},{8,12},{12,8},{10,14},{14,10},{1,5},{5,1},... | collective-permute-start | bytes 5898248 | tf_op jit(solution)/shard_map/ppermute | solution.py:14
  628.5 40.0 %copy-start.1 = (bf16[1,1,192,2560]{3,2,1,0:T(8,128)(2,1)S(1)}, bf16[1,1,192,2560]{3,2,1,0:T(8,128)(2,1)}, u32[]{:S(2)}) copy-start(bf16[1,1,192,2560]{3,2,1,0:T(8,128)(2,1)} %param.5) | copy-start | bytes 2949124
  628.5 40.0 %collective-permute-start.5 = (bf16[192,2560]{1,0:T(8,128)(2,1)S(1)}, bf16[192,2560]{1,0:T(8,128)(2,1)S(1)}, u32[]{:S(2)}, u32[]{:S(2)}) collective-permute-start(bf16[192,2560]{1,0:T(8,128)(2,1)S(1)} %select_convert_fusion.5), channel_id=1, source_target_pairs={{0,2},{2,0},{4,6},{6,4},{8,10},{10,8},{12,14},{14,12},{1,3},{3,1},... | collective-permute-start | bytes 2949128 | tf_op jit(solution)/shard_map/ppermute | solution.py:14
  668.5 21.7 %copy-start.3 = (bf16[1,1,192,2560]{3,2,1,0:T(8,128)(2,1)S(1)}, bf16[1,1,192,2560]{3,2,1,0:T(8,128)(2,1)}, u32[]{:S(2)}) copy-start(bf16[1,1,192,2560]{3,2,1,0:T(8,128)(2,1)} %param.6) | copy-start | bytes 2949124
  668.5 21.6 %collective-permute-start.9 = (bf16[192,2560]{1,0:T(8,128)(2,1)S(1)}, bf16[192,2560]{1,0:T(8,128)(2,1)S(1)}, u32[]{:S(2)}, u32[]{:S(2)}) collective-permute-start(bf16[192,2560]{1,0:T(8,128)(2,1)S(1)} %select_convert_fusion.4), channel_id=1, source_target_pairs={{0,2},{2,0},{4,6},{6,4},{8,10},{10,8},{12,14},{14,12},{1,3},{3,1},... | collective-permute-start | bytes 2949128 | tf_op jit(solution)/shard_map/ppermute | solution.py:14
Sparse Core Ops, SparseCore 0:
  566.2 83.6 all-reduce.2
where the time goes:
time: 731 us; the launch traced here: 722 us
  waiting for transfers between devices  529 us (72%)
  matrix products  107 us (15%)
  other arithmetic  33 us (5%)
  local copies, waits for them, and re-layouts  27.8 us (4%)
  between operations  14.8 us (2%)
  starting transfers between devices  11.7 us (2%)
    ppermute x10, waiting for transfers between devices, from_partner(): return lax.ppermute(block, axis, route)  529 us
    dot_general x3, matrix products, contract_cols(): lax.dot_general(left, right, (((1,), (1,)), ((), ())), preferred_element_...  37 us
    dot_general x3, matrix products, contract_rows(): lax.dot_general(left, right, (((0,), (0,)), ((), ())), preferred_element_...  32.6 us
    unnamed x27, local copies, waits for them, and re-layouts  27.8 us
    select_n x3, other arithmetic, order_pair(): jnp.where(is_upper, jnp.concatenate([other, mine], 1), jnp.concatenate([m...  16 us
  transfers between devices with their start and end apart: 11, of which 9 were waited for; matrix products, arithmetic and copies ran while one was open for 10% of the time, Pallas kernels for 0%

commit v1 on v0

--- a/solution.py
+++ b/solution.py
@@ -1,7 +1,16 @@
+import functools
+
 import jax
 import jax.numpy as jnp
 from jax import lax
+from jax.experimental import pallas as pl
+from jax.experimental.pallas import tpu as pltpu
 from jax.sharding import PartitionSpec as P
+
+VMEM_BYTES = 62 * 1024 * 1024
+TILE = 256
+COST_SCALE = 0.03e9
+G, U, PRE = 0, 1, 2
 
 
 def from_partner(block, axis, stride):
@@ -26,8 +35,10 @@
     )
 
 
-def order_pair(is_upper, mine, other):
-    return jnp.where(is_upper, jnp.concatenate([other, mine], 1), jnp.concatenate([mine, other], 1))
+def order_pair(is_upper, mine, other, dim=1):
+    return jnp.where(
+        is_upper, jnp.concatenate([other, mine], dim), jnp.concatenate([mine, other], dim)
+    )
 
 
 def column_sum(partial_term, total_rows, col_bits, row_bits, my_row):
@@ -66,7 +77,7 @@
     return full_sum
 
 
-def per_device(acts, cotangent, w_gate, w_up, w_down):
+def any_grid(acts, cotangent, w_gate, w_up, w_down):
     grid_size = lax.axis_size("grid")
     grid_cols = min(8, grid_size // 2)
     grid_rows = grid_size // grid_cols
@@ -137,6 +148,395 @@
     )
 
 
+class Order:
+    def __init__(self):
+        self.token = None
+        self.calls = 0
+        self.due = []
+
+    def need(self, array, calls):
+        self.due.append((self.calls + calls, array))
+        return array
+
+    def call(self, body, name, cost, steps, inputs, outputs, scratch=(), after=(), aliases=()):
+        after = list(after) + ([] if self.token is None else [self.token])
+        after += [array for call, array in self.due if call <= self.calls]
+        self.due = [(call, array) for call, array in self.due if call > self.calls]
+        self.calls += 1
+        n_in, n_after, n_out = len(inputs), len(after), len(outputs)
+
+        def kernel(*refs):
+            ins = refs[:n_in]
+            outs = refs[n_in + n_after : n_in + n_after + n_out]
+            refs[n_in + n_after + n_out][...] = jnp.zeros((8, 128), jnp.float32)
+            body(ins, outs, refs[n_in + n_after + n_out + 1 :])
+
+        *results, self.token = pl.pallas_call(
+            kernel,
+            name=name,
+            grid=(steps,),
+            in_specs=[spec for _, spec in inputs]
+            + [pl.BlockSpec(memory_space=pl.ANY) for _ in after],
+            out_specs=[spec for _, spec in outputs] + [pl.BlockSpec((8, 128), lambda j: (0, 0))],
+            out_shape=[shape for shape, _ in outputs]
+            + [jax.ShapeDtypeStruct((8, 128), jnp.float32)],
+            scratch_shapes=list(scratch),
+            input_output_aliases=dict(aliases),
+            cost_estimate=pl.CostEstimate(
+                flops=int(cost * COST_SCALE), bytes_accessed=0, transcendentals=0
+            ),
+            compiler_params=pltpu.CompilerParams(vmem_limit_bytes=VMEM_BYTES),
+        )(*[array for array, _ in inputs], *after)
+        return results
+
+    def hold(self, array, after):
+        inputs = [(array, pl.BlockSpec(memory_space=pl.ANY))]
+        outputs = [(jax.ShapeDtypeStruct(array.shape, array.dtype), inputs[0][1])]
+        return self.call(
+            lambda *_: None, "hold", 0.6, 1, inputs, outputs, after=after, aliases={0: 0}.items()
+        )[0]
+
+
+def weight_specs(weights, kinds, first):
+    gate, up, down = weights
+    depth = gate.shape[1]
+    wide = pl.BlockSpec((1, depth, TILE), lambda j: (0, 0, first + j))
+    tall = pl.BlockSpec((1, TILE, depth), lambda j: (0, first + j, 0))
+    return [((gate, up, down)[kind], tall if kind == PRE else wide) for kind in kinds]
+
+
+def partials(order, units, tiles, sources, weights, after=()):
+    first, count = tiles
+    rows, depth = sources[0].shape[2:]
+    kinds = [kind for kind in (G, U, PRE) if any(kind in unit[0] for unit in units)]
+    token_spec = pl.BlockSpec((1, 1, rows, depth), lambda j: (0, 0, 0, 0))
+    inputs = [(sources[kind == PRE], token_spec) for kind in kinds]
+    inputs += weight_specs(weights, kinds, first)
+    n = len(kinds)
+
+    def body(ins, outs, _):
+        for i, kind in enumerate(kinds):
+            left, right = ins[i][0, 0], ins[n + i][0]
+            if kind == PRE:
+                term = contract_cols(left, right)
+            else:
+                term = jnp.dot(left, right, preferred_element_type=jnp.float32)
+            for m, (unit_kinds, start, size) in enumerate(units):
+                if kind in unit_kinds:
+                    at = unit_kinds.index(kind)
+                    outs[2 * m][at] = term[start : start + size]
+                    outs[2 * m + 1][at] = term[start : start + size].astype(jnp.bfloat16)
+
+    outputs = []
+    for unit_kinds, _, size in units:
+        shape = (len(unit_kinds), size, count * TILE)
+        spec = pl.BlockSpec((len(unit_kinds), size, TILE), lambda j: (0, 0, j))
+        outputs.append((jax.ShapeDtypeStruct(shape, jnp.float32), spec))
+        outputs.append((jax.ShapeDtypeStruct(shape, jnp.bfloat16), spec))
+    results = order.call(body, "partials", (1 + 0.8 * count) * n, count, inputs, outputs, after=after)
+    return list(zip(results[::2], results[1::2]))
+
+
+def hidden_and_back(order, tiles, parts, weights, out_type, addend=()):
+    first, count = tiles
+    sizes = [kept.shape[1] for kept, _ in parts]
+    rows = sum(sizes)
+    depth = weights[0].shape[1]
+    inputs = []
+    for pair, size in zip(parts, sizes):
+        spec = pl.BlockSpec((3, size, TILE), lambda j: (0, 0, j))
+        inputs += [(array, spec) for array in pair]
+    n = len(inputs)
+    inputs += weight_specs(weights, (G, U, PRE), first)
+    sums_spec = pl.BlockSpec((rows, depth), lambda j: (0, 0))
+    inputs += [(array, sums_spec) for array in addend]
+
+    def body(ins, outs, scratch):
+        wg_ref, wu_ref, wd_ref = ins[n : n + 3]
+        hqr_ref = outs[0]
+        acc_ref = scratch[0]
+        j = pl.program_id(0)
+        terms = [ins[m][...] + ins[m + 1][...].astype(jnp.float32) for m in range(0, n, 2)]
+        g, u, p = terms[0] if len(terms) == 1 else jnp.concatenate(terms, 1)
+        s = jax.nn.sigmoid(g)
+        a = g * s
+        h = (a * u).astype(jnp.bfloat16)
+        q = (p * u * s * (1.0 + g * (1.0 - s))).astype(jnp.bfloat16)
+        r = (p * a).astype(jnp.bfloat16)
+        for i, value in enumerate((h, q, r)):
+            hqr_ref[0, i] = value
+            hqr_ref[1, i] = value
+        out_term = jnp.dot(h, wd_ref[0], preferred_element_type=jnp.float32)
+        in_term = contract_cols(q, wg_ref[0]) + contract_cols(r, wu_ref[0])
+
+        @pl.when(j == 0)
+        def _():
+            acc_ref[0] = out_term
+            acc_ref[1] = in_term
+
+        @pl.when(j > 0)
+        def _():
+            acc_ref[0] += out_term
+            acc_ref[1] += in_term
+
+        @pl.when(j == count - 1)
+        def _():
+            for i in range(2):
+                total = acc_ref[i]
+                if addend:
+                    total = total + ins[n + 3 + i][...].astype(jnp.float32)
+                outs[1 + i][...] = total.astype(out_type)
+
+    outputs = [
+        (
+            jax.ShapeDtypeStruct((2, 3, rows, count * TILE), jnp.bfloat16),
+            pl.BlockSpec((2, 3, rows, TILE), lambda j: (0, 0, 0, j)),
+        ),
+    ]
+    outputs += [(jax.ShapeDtypeStruct((rows, depth), out_type), sums_spec)] * 2
+    scratch = [pltpu.VMEM((2, rows, depth), jnp.float32)]
+    return order.call(body, "hidden_and_back", 3 + 2.2 * count, count, inputs, outputs, scratch)
+
+
+def assemble(order, blocks):
+    rows, depth = blocks[0].shape[2:]
+    total = 2 * rows * len(blocks)
+    inputs = []
+    for block in blocks:
+        for part in range(2):
+            index = functools.partial(lambda j, part: (0, part, 0, j), part=part)
+            inputs.append((block, pl.BlockSpec((2, 1, rows, TILE), index)))
+
+    def body(ins, outs, scratch):
+        xt_ref, e_ref = outs
+        x_all = scratch[0]
+        for b in range(len(blocks)):
+            for d in range(2):
+                at = pl.ds((2 * b + d) * rows, rows)
+                x_all[at, :] = ins[2 * b][d, 0]
+                e_ref[at, :] = ins[2 * b + 1][d, 0]
+        xt_ref[...] = x_all[...].T
+
+    outputs = [
+        (
+            jax.ShapeDtypeStruct((depth, total), jnp.bfloat16),
+            pl.BlockSpec((TILE, total), lambda j: (j, 0)),
+        ),
+        (
+            jax.ShapeDtypeStruct((total, depth), jnp.bfloat16),
+            pl.BlockSpec((total, TILE), lambda j: (0, j)),
+        ),
+    ]
+    scratch = [pltpu.VMEM((total, TILE), jnp.bfloat16)]
+    return order.call(body, "assemble", 10, depth // TILE, inputs, outputs, scratch)
+
+
+def weight_grads(order, tiles, tokens, pieces, width, so_far=None, into=None):
+    first, count = tiles
+    xt, e_all = tokens
+    depth, total = xt.shape
+    whole = [
+        pl.BlockSpec((depth, total), lambda j: (0, 0), pipeline_mode=pl.Buffered(1)),
+        pl.BlockSpec((total, depth), lambda j: (0, 0), pipeline_mode=pl.Buffered(1)),
+    ]
+    inputs = [(xt, whole[0]), (e_all, whole[1])]
+    for _, _, hqr, start in pieces:
+        index = functools.partial(lambda j, start: (0, 0, 0, start + j), start=start)
+        inputs.append((hqr, pl.BlockSpec((2, 3, hqr.shape[2], TILE), index)))
+    wide = pl.BlockSpec((1, depth, TILE), lambda j: (0, 0, first + j))
+    tall = pl.BlockSpec((1, TILE, depth), lambda j: (0, first + j, 0))
+    specs = (wide, wide, tall)
+    n = len(inputs)
+    if so_far is not None:
+        inputs += list(zip(so_far, specs))
+    aliases = {}
+    if into is not None:
+        for i, array in enumerate(into):
+            aliases[len(inputs)] = i
+            inputs.append((array, pl.BlockSpec(memory_space=pl.ANY)))
+
+    def body(ins, outs, scratch):
+        hqr_all = scratch[0]
+        for m, (*starts, hqr, _) in enumerate(pieces):
+            for d, start in enumerate(starts):
+                for i in range(3):
+                    hqr_all[i, start : start + hqr.shape[2], :] = ins[2 + m][d, i]
+        terms = (
+            lambda: jnp.dot(ins[0][...], hqr_all[1], preferred_element_type=jnp.float32),
+            lambda: jnp.dot(ins[0][...], hqr_all[2], preferred_element_type=jnp.float32),
+            lambda: contract_rows(hqr_all[0], ins[1][...]),
+        )
+        for i, term in enumerate(terms):
+            value = term()
+            if so_far is not None:
+                value = value + ins[n + i][0].astype(jnp.float32)
+            outs[i][0] = value.astype(jnp.bfloat16)
+
+    shapes = ((1, depth, width), (1, depth, width), (1, width, depth))
+    outputs = [
+        (jax.ShapeDtypeStruct(shape, jnp.bfloat16), spec) for shape, spec in zip(shapes, specs)
+    ]
+    scratch = [pltpu.VMEM((3, total, TILE), jnp.bfloat16)]
+    return order.call(
+        body, "weight_grads", 4 + 4 * count, count, inputs, outputs, scratch, aliases=aliases.items()
+    )
+
+
+def add_row_sums(order, own_sums, near_sums, far_sums, acts, cotangent):
+    rows, depth = acts.shape[2:]
+    step = rows // 4
+    spec = pl.BlockSpec((step, depth), lambda j: (j, 0))
+    token_spec = pl.BlockSpec((1, 1, step, depth), lambda j: (0, 0, j, 0))
+    inputs = [(array, spec) for array in (*own_sums, *near_sums, *far_sums)]
+    inputs += [(acts, token_spec), (cotangent, token_spec)]
+
+    def body(ins, outs, _):
+        for i in range(2):
+            total = ins[i][...] + ins[2 + i][...].astype(jnp.float32)
+            total += ins[4 + i][...].astype(jnp.float32) + ins[6 + i][0, 0].astype(jnp.float32)
+            outs[i][0, 0] = total.astype(jnp.bfloat16)
+
+    outputs = [(jax.ShapeDtypeStruct(acts.shape, jnp.bfloat16), token_spec)] * 2
+    return order.call(body, "add_row_sums", 5, 4, inputs, outputs)
+
+
+def two_by_four(acts, cotangent, w_gate, w_up, w_down):
+    near, far, across = 0, 1, 2
+    rows = acts.shape[2]
+    half = rows // 2
+    width = w_gate.shape[2]
+    n_tiles = width // TILE
+    weights = (w_gate, w_up, w_down)
+    order = Order()
+
+    sources = {"own": (acts, cotangent)}
+
+    def gather(block, origin, bit):
+        sources[block] = tuple(from_partner(array, "grid", bit) for array in sources[origin])
+
+    gather("near", "own", near)
+    gather("far", "own", far)
+
+    a = max(1, n_tiles * 3 // 7)
+    b = n_tiles - 1
+    every = (0, n_tiles)
+    chunks = {"c0": (0, a), "c1": (a, b - a), "c2": (b, n_tiles - b)}
+    own, ready, got = {}, {}, {}
+
+    def compute(names, units, tiles, block, after=()):
+        after = [got[key] for key in after]
+        results = partials(order, units, tiles, sources[block], weights, after)
+        for name, (kept, rounded) in zip(names, results):
+            own[name], ready[name] = kept, rounded
+
+    def send(name, after=()):
+        rounded = ready[name]
+        if after:
+            rounded = order.hold(rounded, [got[key] for key in after])
+        got[name] = from_partner(rounded, "grid", across)
+
+    hqr, sums, passed = {}, {}, {}
+
+    def both_replicas(pair):
+        return lax.all_to_all(pair, "dp", 0, 0, tiled=True)
+
+    def twice(x, e):
+        return jnp.stack([x[0, 0], e[0, 0], x[0, 0], e[0, 0]]).reshape(2, 2, *x.shape[2:])
+
+    def finish(name, names, tiles, out_type=jnp.bfloat16, addend=()):
+        parts = [(own[key], got[key]) for key in names]
+        pair, *sums[name] = hidden_and_back(order, tiles, parts, weights, out_type, addend)
+        hqr[name] = both_replicas(pair)
+
+    def pieces_of(groups, start):
+        found = []
+        at = 0
+        for group in groups:
+            size = sum(hqr[name].shape[2] for name in group)
+            for name in group:
+                first = start if hqr[name].shape[3] == width else 0
+                found.append((at, at + size, hqr[name], first))
+                at += hqr[name].shape[2]
+            at += size
+        return found
+
+    def pass_on(name, bit, calls):
+        passed[name] = [order.need(from_partner(sum, "grid", bit), calls) for sum in sums[name]]
+
+    def collect(*names):
+        return assemble(order, [both_replicas(twice(*sources[name])) for name in names])
+
+    gup = (G, U, PRE)
+    everything = [(gup, 0, rows)]
+    halves = [(gup, 0, half), (gup, half, half)]
+    compute(["c0"], everything, chunks["c0"], "own")
+    send("c0")
+    compute(["c1"], everything, chunks["c1"], "own")
+    compute(["c2"], everything, chunks["c2"], "own")
+    compute(["na", "nb"], halves, every, "near")
+    send("na")
+    send("nb", ["c0"])
+    finish("c0", ["c0"], chunks["c0"], jnp.float32)
+    sources["far"] = tuple(order.hold(array, []) for array in sources["far"])
+    gather("both", "far", near)
+    compute(["fa", "fb"], halves, every, "far")
+    late = collect("far", "own")
+    compute(["ba", "bb"], halves, every, "both", ["na"])
+    send("ba")
+    send("bb", ["nb"])
+    finish("near", ["na", "nb"], every)
+    pass_on("near", near, 3)
+    early = collect("near", "both")
+    send("fa", ["ba"])
+    send("fb", ["bb"])
+    finish("both", ["ba", "bb"], every)
+    pass_on("both", near, 9)
+    early_pieces = pieces_of([["near"], ["both"]], 0)
+    mid = n_tiles // 2
+    first = weight_grads(order, (0, mid), early, early_pieces, width)
+    send("c1", ["fa"])
+    first = weight_grads(
+        order,
+        (mid, n_tiles - mid),
+        early,
+        pieces_of([["near"], ["both"]], mid),
+        width,
+        into=first,
+    )
+    send("c2", ["fb"])
+    finish("far", ["fa", "fb"], every, addend=passed["both"])
+    pass_on("far", far, 20)
+
+    grads = None
+
+    def final(name):
+        return weight_grads(
+            order,
+            chunks[name],
+            late,
+            pieces_of([["far"], [name]], chunks[name][0]),
+            width,
+            first,
+            grads,
+        )
+
+    grads = final("c0")
+    last = "c0"
+    for name in ("c1", "c2"):
+        finish(name, [name], chunks[name], jnp.float32, sums[last])
+        last = name
+        grads = final(name)
+    outs = add_row_sums(order, sums[last], passed["near"], passed["far"], acts, cotangent)
+    return (*outs, *grads)
+
+
+def per_device(acts, cotangent, w_gate, w_up, w_down):
+    fits = acts.shape[2] % 64 == 0 and acts.shape[3] % TILE == 0 and w_gate.shape[2] % TILE == 0
+    if lax.axis_size("grid") == 8 and lax.axis_size("dp") == 2 and fits:
+        return two_by_four(acts, cotangent, w_gate, w_up, w_down)
+    return any_grid(acts, cotangent, w_gate, w_up, w_down)
+
+
 def solution(mesh):
     return jax.shard_map(
         per_device,

time: 731 us -> 482 us (0.66)
  waiting for transfers between devices: 529 us -> 73.1 us
  Pallas kernels: 0 us -> 270 us
  matrix products: 107 us -> 0 us
  blocking collectives: 0 us -> 77.4 us
  starting transfers between devices: 11.7 us -> 39.8 us
  local copies, waits for them, and re-layouts: 27.8 us -> 5.12 us
  other arithmetic: 33 us -> 14.1 us
  between operations: 14.8 us -> 0.92 us
    ppermute x10 -> x21, waiting for transfers between devices: 529 us -> 73 us  [from_partner(): return lax.ppermute(block, axis, route)]
    pallas_call x0 -> x28, Pallas kernels: none -> 270 us  [call(): pl.pallas_call(kernel, name=name, grid=(steps,), in_specs=[spec for _, sp...]
    dot_general x9 -> x0, matrix products: 107 us -> none  [the longest x3 37 us: contract_cols(): lax.dot_general(left, right, (((1,), (1,)), ((), ())), preferred_element_...]
    all_to_all x0 -> x8, blocking collectives: none -> 77.4 us  [both_replicas(): return lax.all_to_all(pair, 'dp', 0, 0, tiled=True)]
    unnamed x27 -> x22, local copies, waits for them, and re-layouts: 27.8 us -> 5.12 us
    ppermute x10 -> x21, starting transfers between devices: 11.7 us -> 28.8 us  [from_partner(): return lax.ppermute(block, axis, route)]
    select_n x3 -> x0, other arithmetic: 16 us -> none  [order_pair(): jnp.where(is_upper, jnp.concatenate([other, mine], 1), jnp.concatenate([m...]
    all_to_all x0 -> x2, starting transfers between devices: none -> 11 us  [both_replicas(): return lax.all_to_all(pair, 'dp', 0, 0, tiled=True)]
  transfers between devices with their start and end apart: 11 -> 23, of which waited for: 9 -> 6; matrix products, arithmetic and copies ran while one was open for 10% -> 3% of each run, Pallas kernels for 0% -> 55%
where the time goes in v1:
time: 482 us; the launch traced here: 480 us
  Pallas kernels  270 us (56%)
  blocking collectives  77.4 us (16%)
  waiting for transfers between devices  73.1 us (15%)
  starting transfers between devices  39.8 us (8%)
  other arithmetic  14.1 us (3%)
  local copies, waits for them, and re-layouts  5.12 us (1%)
    pallas_call x28, Pallas kernels, call(): pl.pallas_call(kernel, name=name, grid=(steps,), in_specs=[spec for _, sp...  270 us
    all_to_all x8, blocking collectives, both_replicas(): return lax.all_to_all(pair, 'dp', 0, 0, tiled=True)  77.4 us
    ppermute x21, waiting for transfers between devices, from_partner(): return lax.ppermute(block, axis, route)  73 us
    ppermute x21, starting transfers between devices, from_partner(): return lax.ppermute(block, axis, route)  28.8 us
    another operation x4, other arithmetic, twice(): jnp.stack([x[0, 0], e[0, 0], x[0, 0], e[0, 0]]).reshape(2, 2, *x.shape[2:])  14.1 us
    all_to_all x2, starting transfers between devices, both_replicas(): return lax.all_to_all(pair, 'dp', 0, 0, tiled=True)  11 us
  transfers between devices with their start and end apart: 23, of which 6 were waited for; matrix products, arithmetic and copies ran while one was open for 3% of the time, Pallas kernels for 55%

profile of v1, /device:TPU:0, one launch (start us, length us, event | category | flops | bytes accessed | tf_op | source)
XLA Modules:
  0.0 480.3 jit_solution(6603744691990229071)
XLA Ops:
  5.8 9.9 %partials.6 = (f32[3,192,768]{2,1,0:T(8,128)}, bf16[3,192,768]{2,1,0:T(8,128)(2,1)}, f32[8,128]{1,0:T(8,128)}) custom-call(bf16[1,1,192,2560]{3,2,1,0:T(8,128)(2,1)} %refs_6_.7, bf16[1,1,192,2560]{3,2,1,0:T(8,128)(2,1)} %refs_6_.7, bf16[1,1,192,2560]{3,2,1,0:T(8,128)(2,1)} %refs_7_.1, bf16[1,2560,1792]{2,1,0:T(8,128)(2,1)} %refs_2_.11, ...), custom_call_target="tpu_custom_call" | custom-call | flops 306000000 | tf_op jit(solution)/shard_map/partials/pallas_call | solution.py:174
  18.7 10.0 %partials.7 = (f32[3,192,768]{2,1,0:T(8,128)}, bf16[3,192,768]{2,1,0:T(8,128)(2,1)}, f32[8,128]{1,0:T(8,128)}) custom-call(bf16[1,1,192,2560]{3,2,1,0:T(8,128)(2,1)} %refs_6_.7, bf16[1,1,192,2560]{3,2,1,0:T(8,128)(2,1)} %refs_6_.7, bf16[1,1,192,2560]{3,2,1,0:T(8,128)(2,1)} %refs_7_.1, bf16[1,2560,1792]{2,1,0:T(8,128)(2,1)} %refs_2_.11, ...), custom_call_target="tpu_custom_call" | custom-call | flops 306000000 | tf_op jit(solution)/shard_map/partials/pallas_call | solution.py:174
  33.8 12.9 %collective-permute-done.3.refs_2_ = bf16[1,1,192,2560]{3,2,1,0:T(8,128)(2,1)S(1)} collective-permute-done((bf16[1,1,192,2560]{3,2,1,0:T(8,128)(2,1)}, bf16[1,1,192,2560]{3,2,1,0:T(8,128)(2,1)S(1)}, u32[]{:S(2)}, u32[]{:S(2)}) %collective-permute-start.3) | collective-permute-done | bytes 983072 | tf_op jit(solution)/shard_map/ppermute | solution.py:23
  47.6 17.6 %partials.9 = (f32[3,96,1792]{2,1,0:T(8,128)}, bf16[3,96,1792]{2,1,0:T(8,128)(2,1)}, f32[3,96,1792]{2,1,0:T(8,128)}, bf16[3,96,1792]{2,1,0:T(8,128)(2,1)}, f32[8,128]{1,0:T(8,128)}) custom-call(bf16[1,1,192,2560]{3,2,1,0:T(8,128)(2,1)} %copy-done.2, bf16[1,1,192,2560]{3,2,1,0:T(8,128)(2,1)} %copy-done.2, bf16[1,1,192,2560]{3,2,1,0:T(8,128)(2,1)} %copy-done.7, ...), custom_call_target="tpu_custom_call" | custom-call | flops 594000000 | tf_op jit(solution)/shard_map/partials/pallas_call | solution.py:174
  70.5 10.8 %hidden_and_back.6 = (bf16[2,3,192,768]{3,2,1,0:T(8,128)(2,1)}, f32[192,2560]{1,0:T(8,128)}, f32[192,2560]{1,0:T(8,128)}, f32[8,128]{1,0:T(8,128)}) custom-call(f32[3,192,768]{2,1,0:T(8,128)} %get-tuple-element.101.refs_0_, bf16[3,192,768]{2,1,0:T(8,128)(2,1)} %collective-permute-done.1.refs_1_, bf16[1,2560,1792]{2,1,0:T(8,128)(2,1)} %refs_2_.11, ...), custom_call_target="tpu_custom_call" | custom-call | flops 288000000 | tf_op jit(solution)/shard_map/hidden_and_back/pallas_call | solution.py:174
  86.7 5.5 %all-to-all-start.1 = ((bf16[2,2,192,2560]{3,2,1,0:T(8,128)(2,1)}), bf16[2,2,192,2560]{3,2,1,0:T(8,128)(2,1)}, u32[]{:S(2)}, u32[]{:S(2)}) async-start(bf16[2,2,192,2560]{3,2,1,0:T(8,128)(2,1)} %bitcast.14), calls=%async_computation.1 | async-start | bytes 7864320 | tf_op jit(solution)/shard_map/all_to_all | solution.py:441
  92.2 17.8 %partials.10 = (f32[3,96,1792]{2,1,0:T(8,128)}, bf16[3,96,1792]{2,1,0:T(8,128)(2,1)}, f32[3,96,1792]{2,1,0:T(8,128)}, bf16[3,96,1792]{2,1,0:T(8,128)(2,1)}, f32[8,128]{1,0:T(8,128)}) custom-call(bf16[1,1,192,2560]{3,2,1,0:T(8,128)(2,1)} %get-tuple-element.108.refs_0_.refs_1_, bf16[1,1,192,2560]{3,2,1,0:T(8,128)(2,1)} %get-tuple-element.108.refs_0_.refs_1_, ...), custom_call_target="tpu_custom_call" | custom-call | flops 594000000 | tf_op jit(solution)/shard_map/partials/pallas_call | solution.py:174
  114.1 11.5 %all_to_all.50.refs_0_.refs_1_ = bf16[2,2,192,2560]{3,2,1,0:T(8,128)(2,1)} all-to-all(bf16[2,2,192,2560]{3,2,1,0:T(8,128)(2,1)} %bitcast.17), channel_id=1, replica_groups=mesh['groups'=2,'grid'=8,'dp'=2] {'dp'}, dimensions={0} | all-to-all | bytes 7864320 | tf_op jit(solution)/shard_map/all_to_all | solution.py:441
  125.7 10.0 %assemble.2 = (bf16[2560,768]{1,0:T(8,128)(2,1)}, bf16[768,2560]{1,0:T(8,128)(2,1)}, f32[8,128]{1,0:T(8,128)}) custom-call(bf16[2,2,192,2560]{3,2,1,0:T(8,128)(2,1)} %all_to_all.50.refs_0_.refs_1_, bf16[2,2,192,2560]{3,2,1,0:T(8,128)(2,1)} %all_to_all.50.refs_0_.refs_1_, bf16[2,2,192,2560]{3,2,1,0:T(8,128)(2,1)} %all-to-all-done.1.refs_2_.refs_3_, ...), custom_call_target="tpu_custom_call" | custom-call | flops 300000000 | tf_op jit(solution)/shard_map/assemble/pallas_call | solution.py:174
  135.9 17.7 %partials.11 = (f32[3,96,1792]{2,1,0:T(8,128)}, bf16[3,96,1792]{2,1,0:T(8,128)(2,1)}, f32[3,96,1792]{2,1,0:T(8,128)}, bf16[3,96,1792]{2,1,0:T(8,128)(2,1)}, f32[8,128]{1,0:T(8,128)}) custom-call(bf16[1,1,192,2560]{3,2,1,0:T(8,128)(2,1)} %collective-permute-done.5.refs_0_.refs_1_, bf16[1,1,192,2560]{3,2,1,0:T(8,128)(2,1)} %collective-permute-done.5.refs_0_.refs_1_, ...), custom_call_target="tpu_custom_call" | custom-call | flops 594000000 | tf_op jit(solution)/shard_map/partials/pallas_call | solution.py:174
  154.5 25.6 %collective-permute-done.8.refs_1_.refs_3_ = bf16[3,96,1792]{2,1,0:T(8,128)(2,1)} collective-permute-done((bf16[3,96,1792]{2,1,0:T(8,128)(2,1)}, bf16[3,96,1792]{2,1,0:T(8,128)(2,1)}, u32[]{:S(2)}, u32[]{:S(2)}) %collective-permute-start.8) | collective-permute-done | bytes 1032224 | tf_op jit(solution)/shard_map/ppermute | solution.py:23
  180.8 19.0 %hidden_and_back.7 = (bf16[2,3,192,1792]{3,2,1,0:T(8,128)(2,1)}, bf16[192,2560]{1,0:T(8,128)(2,1)}, bf16[192,2560]{1,0:T(8,128)(2,1)}, f32[8,128]{1,0:T(8,128)}) custom-call(f32[3,96,1792]{2,1,0:T(8,128)} %get-tuple-element.122.refs_0_, bf16[3,96,1792]{2,1,0:T(8,128)(2,1)} %collective-permute-done.7.refs_6_.refs_1_, ...), custom_call_target="tpu_custom_call" | custom-call | flops 552000000 | tf_op jit(solution)/shard_map/hidden_and_back/pallas_call | solution.py:174
  215.2 11.6 %all_to_all.51.refs_2_.refs_3_ = bf16[2,2,192,2560]{3,2,1,0:T(8,128)(2,1)} all-to-all(bf16[2,2,192,2560]{3,2,1,0:T(8,128)(2,1)} %bitcast.16), channel_id=1, replica_groups=mesh['groups'=2,'grid'=8,'dp'=2] {'dp'}, dimensions={0} | all-to-all | bytes 7864320 | tf_op jit(solution)/shard_map/all_to_all | solution.py:441
  226.8 9.9 %assemble.3 = (bf16[2560,768]{1,0:T(8,128)(2,1)}, bf16[768,2560]{1,0:T(8,128)(2,1)}, f32[8,128]{1,0:T(8,128)}) custom-call(bf16[2,2,192,2560]{3,2,1,0:T(8,128)(2,1)} %all-to-all-done.2.refs_0_.refs_1_, bf16[2,2,192,2560]{3,2,1,0:T(8,128)(2,1)} %all-to-all-done.2.refs_0_.refs_1_, bf16[2,2,192,2560]{3,2,1,0:T(8,128)(2,1)} %all_to_all.51.refs_2_.refs_3_, ...), custom_call_target="tpu_custom_call" | custom-call | flops 300000000 | tf_op jit(solution)/shard_map/assemble/pallas_call | solution.py:174
  241.3 27.3 %collective-permute-done.9.refs_1_.refs_3_ = bf16[3,96,1792]{2,1,0:T(8,128)(2,1)} collective-permute-done((bf16[3,96,1792]{2,1,0:T(8,128)(2,1)}, bf16[3,96,1792]{2,1,0:T(8,128)(2,1)}, u32[]{:S(2)}, u32[]{:S(2)}) %collective-permute-start.9) | collective-permute-done | bytes 1032224 | tf_op jit(solution)/shard_map/ppermute | solution.py:23
  269.2 18.9 %hidden_and_back.8 = (bf16[2,3,192,1792]{3,2,1,0:T(8,128)(2,1)}, bf16[192,2560]{1,0:T(8,128)(2,1)}, bf16[192,2560]{1,0:T(8,128)(2,1)}, f32[8,128]{1,0:T(8,128)}) custom-call(f32[3,96,1792]{2,1,0:T(8,128)} %get-tuple-element.132.refs_0_, bf16[3,96,1792]{2,1,0:T(8,128)(2,1)} %copy-done.6, f32[3,96,1792]{2,1,0:T(8,128)} %get-tuple-element.133.refs_2_, ...), custom_call_target="tpu_custom_call" | custom-call | flops 552000000 | tf_op jit(solution)/shard_map/hidden_and_back/pallas_call | solution.py:174
  290.3 12.0 %all_to_all.52.refs_2_ = bf16[2,3,192,1792]{3,2,1,0:T(8,128)(2,1)} all-to-all(bf16[2,3,192,1792]{3,2,1,0:T(8,128)(2,1)} %get-tuple-element.131), channel_id=1, replica_groups=mesh['groups'=2,'grid'=8,'dp'=2] {'dp'}, dimensions={0} | all-to-all | bytes 8257536 | tf_op jit(solution)/shard_map/all_to_all | solution.py:441
  302.3 8.1 %all_to_all.53.refs_3_ = bf16[2,3,192,1792]{3,2,1,0:T(8,128)(2,1)} all-to-all(bf16[2,3,192,1792]{3,2,1,0:T(8,128)(2,1)S(1)} %copy-done.4), channel_id=1, replica_groups=mesh['groups'=2,'grid'=8,'dp'=2] {'dp'}, dimensions={0} | all-to-all | bytes 8257536 | tf_op jit(solution)/shard_map/all_to_all | solution.py:441
  310.3 14.5 %weight_grads.5 = (bf16[1,2560,1792]{2,1,0:T(8,128)(2,1)}, bf16[1,2560,1792]{2,1,0:T(8,128)(2,1)}, bf16[1,1792,2560]{2,1,0:T(8,128)(2,1)}, f32[8,128]{1,0:T(8,128)}) custom-call(bf16[2560,768]{1,0:T(8,128)(2,1)} %get-tuple-element.129.refs_0_, bf16[768,2560]{1,0:T(8,128)(2,1)} %get-tuple-element.130.refs_1_, bf16[2,3,192,1792]{3,2,1,0:T(8,128)(2,1)} %all_to_all.52.refs_2_, ...), custom_call_target="tpu_custom_call" | custom-call | flops 480000000 | tf_op jit(solution)/shard_map/weight_grads/pallas_call | solution.py:174
  329.3 17.8 %weight_grads.6 = (bf16[1,2560,1792]{2,1,0:T(8,128)(2,1)}, bf16[1,2560,1792]{2,1,0:T(8,128)(2,1)}, bf16[1,1792,2560]{2,1,0:T(8,128)(2,1)}, f32[8,128]{1,0:T(8,128)}) custom-call(bf16[2560,768]{1,0:T(8,128)(2,1)} %get-tuple-element.129.refs_0_, ...), custom_call_target="tpu_custom_call", output_to_operand_aliasing={{0}: (4, {}), {1}: (5, {}), {2}: (6, {})} | custom-call | flops 600000000 | tf_op jit(solution)/shard_map/weight_grads/pallas_call | solution.py:174
  347.1 6.8 %collective-permute-done.11.refs_1_.refs_3_ = bf16[3,96,1792]{2,1,0:T(8,128)(2,1)} collective-permute-done((bf16[3,96,1792]{2,1,0:T(8,128)(2,1)}, bf16[3,96,1792]{2,1,0:T(8,128)(2,1)}, u32[]{:S(2)}, u32[]{:S(2)}) %collective-permute-start.11) | collective-permute-done | bytes 1032224 | tf_op jit(solution)/shard_map/ppermute | solution.py:23
  355.5 20.1 %hidden_and_back.9 = (bf16[2,3,192,1792]{3,2,1,0:T(8,128)(2,1)}, bf16[192,2560]{1,0:T(8,128)(2,1)}, bf16[192,2560]{1,0:T(8,128)(2,1)}, f32[8,128]{1,0:T(8,128)}) custom-call(f32[3,96,1792]{2,1,0:T(8,128)} %get-tuple-element.154.refs_0_, bf16[3,96,1792]{2,1,0:T(8,128)(2,1)} %copy-done.5, f32[3,96,1792]{2,1,0:T(8,128)} %get-tuple-element.155.refs_2_, ...), custom_call_target="tpu_custom_call" | custom-call | flops 552000000 | tf_op jit(solution)/shard_map/hidden_and_back/pallas_call | solution.py:174
  378.7 8.2 %all_to_all.54.refs_3_ = bf16[2,3,192,768]{3,2,1,0:T(8,128)(2,1)} all-to-all(bf16[2,3,192,768]{3,2,1,0:T(8,128)(2,1)} %get-tuple-element.160), channel_id=1, replica_groups=mesh['groups'=2,'grid'=8,'dp'=2] {'dp'}, dimensions={0} | all-to-all | bytes 3538944 | tf_op jit(solution)/shard_map/all_to_all | solution.py:441
  386.8 11.8 %all_to_all.55.refs_2_ = bf16[2,3,192,1792]{3,2,1,0:T(8,128)(2,1)} all-to-all(bf16[2,3,192,1792]{3,2,1,0:T(8,128)(2,1)} %get-tuple-element.159), channel_id=1, replica_groups=mesh['groups'=2,'grid'=8,'dp'=2] {'dp'}, dimensions={0} | all-to-all | bytes 8257536 | tf_op jit(solution)/shard_map/all_to_all | solution.py:441
  398.6 16.3 %weight_grads.7 = (bf16[1,2560,1792]{2,1,0:T(8,128)(2,1)}, bf16[1,2560,1792]{2,1,0:T(8,128)(2,1)}, bf16[1,1792,2560]{2,1,0:T(8,128)(2,1)}, f32[8,128]{1,0:T(8,128)}) custom-call(bf16[2560,768]{1,0:T(8,128)(2,1)} %get-tuple-element.152.refs_0_, bf16[768,2560]{1,0:T(8,128)(2,1)} %get-tuple-element.153.refs_1_, bf16[2,3,192,1792]{3,2,1,0:T(8,128)(2,1)} %all_to_all.55.refs_2_, ...), custom_call_target="tpu_custom_call" | custom-call | flops 480000000 | tf_op jit(solution)/shard_map/weight_grads/pallas_call | solution.py:174
  414.8 12.6 %hidden_and_back.10 = (bf16[2,3,192,768]{3,2,1,0:T(8,128)(2,1)}, f32[192,2560]{1,0:T(8,128)}, f32[192,2560]{1,0:T(8,128)}, f32[8,128]{1,0:T(8,128)}) custom-call(f32[3,192,768]{2,1,0:T(8,128)} %get-tuple-element.148.refs_0_, bf16[3,192,768]{2,1,0:T(8,128)(2,1)} %collective-permute-done.16.refs_1_, bf16[1,2560,1792]{2,1,0:T(8,128)(2,1)} %refs_2_.11, ...), custom_call_target="tpu_custom_call" | custom-call | flops 288000000 | tf_op jit(solution)/shard_map/hidden_and_back/pallas_call | solution.py:174
  427.5 8.2 %all_to_all.56.refs_3_ = bf16[2,3,192,768]{3,2,1,0:T(8,128)(2,1)} all-to-all(bf16[2,3,192,768]{3,2,1,0:T(8,128)(2,1)} %get-tuple-element.168), channel_id=1, replica_groups=mesh['groups'=2,'grid'=8,'dp'=2] {'dp'}, dimensions={0} | all-to-all | bytes 3538944 | tf_op jit(solution)/shard_map/all_to_all | solution.py:441
  435.6 16.3 %weight_grads.8 = (bf16[1,2560,1792]{2,1,0:T(8,128)(2,1)}, bf16[1,2560,1792]{2,1,0:T(8,128)(2,1)}, bf16[1,1792,2560]{2,1,0:T(8,128)(2,1)}, f32[8,128]{1,0:T(8,128)}) custom-call(bf16[2560,768]{1,0:T(8,128)(2,1)} %get-tuple-element.152.refs_0_, ...), custom_call_target="tpu_custom_call", output_to_operand_aliasing={{0}: (7, {}), {1}: (8, {}), {2}: (9, {})} | custom-call | flops 480000000 | tf_op jit(solution)/shard_map/weight_grads/pallas_call | solution.py:174
  451.9 6.2 %hidden_and_back.11 = (bf16[2,3,192,256]{3,2,1,0:T(8,128)(2,1)}, f32[192,2560]{1,0:T(8,128)}, f32[192,2560]{1,0:T(8,128)}, f32[8,128]{1,0:T(8,128)}) custom-call(f32[3,192,256]{2,1,0:T(8,128)} %get-tuple-element.99.refs_0_, bf16[3,192,256]{2,1,0:T(8,128)(2,1)} %collective-permute-done.15.refs_1_, bf16[1,2560,1792]{2,1,0:T(8,128)(2,1)} %refs_2_.11, ...), custom_call_target="tpu_custom_call" | custom-call | flops 156000000 | tf_op jit(solution)/shard_map/hidden_and_back/pallas_call | solution.py:174
  458.1 6.1 %all_to_all.57.refs_3_ = bf16[2,3,192,256]{3,2,1,0:T(8,128)(2,1)} all-to-all(bf16[2,3,192,256]{3,2,1,0:T(8,128)(2,1)} %get-tuple-element.178), channel_id=1, replica_groups=mesh['groups'=2,'grid'=8,'dp'=2] {'dp'}, dimensions={0} | all-to-all | bytes 1179648 | tf_op jit(solution)/shard_map/all_to_all | solution.py:441
  464.3 9.1 %weight_grads.9 = (bf16[1,2560,1792]{2,1,0:T(8,128)(2,1)}, bf16[1,2560,1792]{2,1,0:T(8,128)(2,1)}, bf16[1,1792,2560]{2,1,0:T(8,128)(2,1)}, f32[8,128]{1,0:T(8,128)}) custom-call(bf16[2560,768]{1,0:T(8,128)(2,1)} %get-tuple-element.152.refs_0_, ...), custom_call_target="tpu_custom_call", output_to_operand_aliasing={{0}: (7, {}), {1}: (8, {}), {2}: (9, {})} | custom-call | flops 240000000 | tf_op jit(solution)/shard_map/weight_grads/pallas_call | solution.py:174
  474.6 5.6 %add_row_sums.1 = (bf16[1,1,192,2560]{3,2,1,0:T(8,128)(2,1)}, bf16[1,1,192,2560]{3,2,1,0:T(8,128)(2,1)}, f32[8,128]{1,0:T(8,128)}) custom-call(f32[192,2560]{1,0:T(8,128)} %get-tuple-element.174.refs_0_, f32[192,2560]{1,0:T(8,128)} %get-tuple-element.175.refs_1_, bf16[192,2560]{1,0:T(8,128)(2,1)} %collective-permute-done.12.refs_8_.refs_2_, ...), custom_call_target="tpu_custom_call" | custom-call | flops 150000000 | tf_op jit(solution)/shard_map/add_row_sums/pallas_call | solution.py:174
  (76 shorter events, 63.7 us)
Async XLA Ops:
  0.6 33.1 %collective-permute-start.2 = (bf16[1,1,192,2560]{3,2,1,0:T(8,128)(2,1)}, bf16[1,1,192,2560]{3,2,1,0:T(8,128)(2,1)S(1)}, u32[]{:S(2)}, u32[]{:S(2)}) collective-permute-start(bf16[1,1,192,2560]{3,2,1,0:T(8,128)(2,1)} %refs_6_.7), channel_id=1, source_target_pairs={{0,2},{2,0},{4,6},{6,4},{8,10},{10,8},{12,14},{14,12},{1,3},{3,1},... | collective-permute-start | bytes 2949128 | tf_op jit(solution)/shard_map/ppermute | solution.py:23
  3.7 43.0 %collective-permute-start.3 = (bf16[1,1,192,2560]{3,2,1,0:T(8,128)(2,1)}, bf16[1,1,192,2560]{3,2,1,0:T(8,128)(2,1)S(1)}, u32[]{:S(2)}, u32[]{:S(2)}) collective-permute-start(bf16[1,1,192,2560]{3,2,1,0:T(8,128)(2,1)} %refs_7_.1), channel_id=1, source_target_pairs={{0,2},{2,0},{4,6},{6,4},{8,10},{10,8},{12,14},{14,12},{1,3},{3,1},... | collective-permute-start | bytes 2949128 | tf_op jit(solution)/shard_map/ppermute | solution.py:23
  3.7 77.6 %collective-permute-start = (bf16[1,1,192,2560]{3,2,1,0:T(8,128)(2,1)}, bf16[1,1,192,2560]{3,2,1,0:T(8,128)(2,1)}, u32[]{:S(2)}, u32[]{:S(2)}) collective-permute-start(bf16[1,1,192,2560]{3,2,1,0:T(8,128)(2,1)} %refs_6_.7), channel_id=1, source_target_pairs={{0,4},{4,0},{2,6},{6,2},{8,12},{12,8},{10,14},{14,10},{1,5},{5,1},... | collective-permute-start | bytes 2949128 | tf_op jit(solution)/shard_map/ppermute | solution.py:23
  5.7 76.2 %collective-permute-start.4 = (bf16[1,1,192,2560]{3,2,1,0:T(8,128)(2,1)}, bf16[1,1,192,2560]{3,2,1,0:T(8,128)(2,1)}, u32[]{:S(2)}, u32[]{:S(2)}) collective-permute-start(bf16[1,1,192,2560]{3,2,1,0:T(8,128)(2,1)} %refs_7_.1), channel_id=1, source_target_pairs={{0,4},{4,0},{2,6},{6,2},{8,12},{12,8},{10,14},{14,10},{1,5},{5,1},... | collective-permute-start | bytes 2949128 | tf_op jit(solution)/shard_map/ppermute | solution.py:23
  15.7 52.4 %collective-permute-start.1 = (bf16[3,192,768]{2,1,0:T(8,128)(2,1)}, bf16[3,192,768]{2,1,0:T(8,128)(2,1)}, u32[]{:S(2)}, u32[]{:S(2)}) collective-permute-start(bf16[3,192,768]{2,1,0:T(8,128)(2,1)} %get-tuple-element.102), channel_id=1, source_target_pairs={{0,8},{8,0},{2,10},{10,2},{4,12},{12,4},{6,14},{14,6},{1,9},{9,1},... | collective-permute-start | bytes 2654216 | tf_op jit(solution)/shard_map/ppermute | solution.py:23
  33.8 12.9 %copy-start.2 = (bf16[1,1,192,2560]{3,2,1,0:T(8,128)(2,1)}, bf16[1,1,192,2560]{3,2,1,0:T(8,128)(2,1)S(1)}, u32[]{:S(2)}) copy-start(bf16[1,1,192,2560]{3,2,1,0:T(8,128)(2,1)S(1)} %collective-permute-done.2.refs_0_.refs_1_) | copy-start | bytes 2949124
  65.3 70.6 %collective-permute-start.7 = (bf16[3,96,1792]{2,1,0:T(8,128)(2,1)}, bf16[3,96,1792]{2,1,0:T(8,128)(2,1)}, u32[]{:S(2)}, u32[]{:S(2)}) collective-permute-start(bf16[3,96,1792]{2,1,0:T(8,128)(2,1)} %get-tuple-element.113), channel_id=1, source_target_pairs={{0,8},{8,0},{2,10},{10,2},{4,12},{12,4},{6,14},{14,6},{1,9},{9,1},... | collective-permute-start | bytes 3096584 | tf_op jit(solution)/shard_map/ppermute | solution.py:23
  68.7 111.5 %collective-permute-start.8 = (bf16[3,96,1792]{2,1,0:T(8,128)(2,1)}, bf16[3,96,1792]{2,1,0:T(8,128)(2,1)}, u32[]{:S(2)}, u32[]{:S(2)}) collective-permute-start(bf16[3,96,1792]{2,1,0:T(8,128)(2,1)} %get-tuple-element.117), channel_id=1, source_target_pairs={{0,8},{8,0},{2,10},{10,2},{4,12},{12,4},{6,14},{14,6},{1,9},{9,1},... | collective-permute-start | bytes 3096584 | tf_op jit(solution)/shard_map/ppermute | solution.py:23
  70.5 14.0 %copy-start = (bf16[1,1,192,2560]{3,2,1,0:T(8,128)(2,1)S(1)}, bf16[1,1,192,2560]{3,2,1,0:T(8,128)(2,1)}, u32[]{:S(2)}) copy-start(bf16[1,1,192,2560]{3,2,1,0:T(8,128)(2,1)} %refs_6_.7) | copy-start | bytes 2949124
  70.5 14.0 %copy-start.1 = (bf16[1,1,192,2560]{3,2,1,0:T(8,128)(2,1)S(1)}, bf16[1,1,192,2560]{3,2,1,0:T(8,128)(2,1)}, u32[]{:S(2)}) copy-start(bf16[1,1,192,2560]{3,2,1,0:T(8,128)(2,1)} %refs_7_.1) | copy-start | bytes 2949124
  82.5 53.1 %collective-permute-start.6 = (bf16[1,1,192,2560]{3,2,1,0:T(8,128)(2,1)}, bf16[1,1,192,2560]{3,2,1,0:T(8,128)(2,1)}, u32[]{:S(2)}, u32[]{:S(2)}) collective-permute-start(bf16[1,1,192,2560]{3,2,1,0:T(8,128)(2,1)} %get-tuple-element.110.refs_2_), channel_id=1, source_target_pairs={{0,2},{2,0},{4,6},{6,4},{8,10},{10,8},{12,14},{14,12},{1,3},{3,1},... | collective-permute-start | bytes 2949128 | tf_op jit(solution)/shard_map/ppermute | solution.py:23
  84.0 51.6 %collective-permute-start.5 = (bf16[1,1,192,2560]{3,2,1,0:T(8,128)(2,1)}, bf16[1,1,192,2560]{3,2,1,0:T(8,128)(2,1)}, u32[]{:S(2)}, u32[]{:S(2)}) collective-permute-start(bf16[1,1,192,2560]{3,2,1,0:T(8,128)(2,1)} %get-tuple-element.108.refs_0_.refs_1_), channel_id=1, source_target_pairs={{0,2},{2,0},{4,6},{6,4},{8,10},{10,8},{12,14},{14,12},{1,3},{3,1},... | collective-permute-start | bytes 2949128 | tf_op jit(solution)/shard_map/ppermute | solution.py:23
  86.7 27.4 %all-to-all-start.1 = ((bf16[2,2,192,2560]{3,2,1,0:T(8,128)(2,1)}), bf16[2,2,192,2560]{3,2,1,0:T(8,128)(2,1)}, u32[]{:S(2)}, u32[]{:S(2)}) async-start(bf16[2,2,192,2560]{3,2,1,0:T(8,128)(2,1)} %bitcast.14), calls=%async_computation.1 | async-start | bytes 7864320 | tf_op jit(solution)/shard_map/all_to_all | solution.py:441
  153.6 83.1 %collective-permute-start.10 = (bf16[3,96,1792]{2,1,0:T(8,128)(2,1)}, bf16[3,96,1792]{2,1,0:T(8,128)(2,1)S(1)}, u32[]{:S(2)}, u32[]{:S(2)}) collective-permute-start(bf16[3,96,1792]{2,1,0:T(8,128)(2,1)} %get-tuple-element.121), channel_id=1, source_target_pairs={{0,8},{8,0},{2,10},{10,2},{4,12},{12,4},{6,14},{14,6},{1,9},{9,1},... | collective-permute-start | bytes 3096584 | tf_op jit(solution)/shard_map/ppermute | solution.py:23
  180.8 87.9 %collective-permute-start.9 = (bf16[3,96,1792]{2,1,0:T(8,128)(2,1)}, bf16[3,96,1792]{2,1,0:T(8,128)(2,1)}, u32[]{:S(2)}, u32[]{:S(2)}) collective-permute-start(bf16[3,96,1792]{2,1,0:T(8,128)(2,1)} %get-tuple-element.119), channel_id=1, source_target_pairs={{0,8},{8,0},{2,10},{10,2},{4,12},{12,4},{6,14},{14,6},{1,9},{9,1},... | collective-permute-start | bytes 3096584 | tf_op jit(solution)/shard_map/ppermute | solution.py:23
  180.8 21.1 %copy-start.3 = (bf16[1,1,192,2560]{3,2,1,0:T(8,128)(2,1)S(1)}, bf16[1,1,192,2560]{3,2,1,0:T(8,128)(2,1)}, u32[]{:S(2)}) copy-start(bf16[1,1,192,2560]{3,2,1,0:T(8,128)(2,1)} %copy-done.2) | copy-start | bytes 2949124
  199.7 69.5 %collective-permute-start.12 = (bf16[192,2560]{1,0:T(8,128)(2,1)}, bf16[192,2560]{1,0:T(8,128)(2,1)}, u32[]{:S(2)}, u32[]{:S(2)}) collective-permute-start(bf16[192,2560]{1,0:T(8,128)(2,1)} %get-tuple-element.135), channel_id=1, source_target_pairs={{0,2},{2,0},{4,6},{6,4},{8,10},{10,8},{12,14},{14,12},{1,3},{3,1},... | collective-permute-start | bytes 2949128 | tf_op jit(solution)/shard_map/ppermute | solution.py:23
  201.3 68.0 %collective-permute-start.13 = (bf16[192,2560]{1,0:T(8,128)(2,1)}, bf16[192,2560]{1,0:T(8,128)(2,1)}, u32[]{:S(2)}, u32[]{:S(2)}) collective-permute-start(bf16[192,2560]{1,0:T(8,128)(2,1)} %get-tuple-element.136), channel_id=1, source_target_pairs={{0,2},{2,0},{4,6},{6,4},{8,10},{10,8},{12,14},{14,12},{1,3},{3,1},... | collective-permute-start | bytes 2949128 | tf_op jit(solution)/shard_map/ppermute | solution.py:23
  205.4 9.8 %all-to-all-start.2 = ((bf16[2,2,192,2560]{3,2,1,0:T(8,128)(2,1)}), bf16[2,2,192,2560]{3,2,1,0:T(8,128)(2,1)}, u32[]{:S(2)}, u32[]{:S(2)}) async-start(bf16[2,2,192,2560]{3,2,1,0:T(8,128)(2,1)} %bitcast.15), calls=%async_computation.2 | async-start | bytes 7864320 | tf_op jit(solution)/shard_map/all_to_all | solution.py:441
  236.8 1.0 copy-start.6
  238.4 86.5 %collective-permute-start.14 = (bf16[3,96,1792]{2,1,0:T(8,128)(2,1)}, bf16[3,96,1792]{2,1,0:T(8,128)(2,1)S(1)}, u32[]{:S(2)}, u32[]{:S(2)}) collective-permute-start(bf16[3,96,1792]{2,1,0:T(8,128)(2,1)} %get-tuple-element.143), channel_id=1, source_target_pairs={{0,8},{8,0},{2,10},{10,2},{4,12},{12,4},{6,14},{14,6},{1,9},{9,1},... | collective-permute-start | bytes 3096584 | tf_op jit(solution)/shard_map/ppermute | solution.py:23
  269.2 84.7 %collective-permute-start.11 = (bf16[3,96,1792]{2,1,0:T(8,128)(2,1)}, bf16[3,96,1792]{2,1,0:T(8,128)(2,1)}, u32[]{:S(2)}, u32[]{:S(2)}) collective-permute-start(bf16[3,96,1792]{2,1,0:T(8,128)(2,1)} %get-tuple-element.128), channel_id=1, source_target_pairs={{0,8},{8,0},{2,10},{10,2},{4,12},{12,4},{6,14},{14,6},{1,9},{9,1},... | collective-permute-start | bytes 3096584 | tf_op jit(solution)/shard_map/ppermute | solution.py:23
  288.2 66.4 %collective-permute-start.17 = (bf16[192,2560]{1,0:T(8,128)(2,1)}, bf16[192,2560]{1,0:T(8,128)(2,1)S(1)}, u32[]{:S(2)}, u32[]{:S(2)}) collective-permute-start(bf16[192,2560]{1,0:T(8,128)(2,1)} %get-tuple-element.156), channel_id=1, source_target_pairs={{0,2},{2,0},{4,6},{6,4},{8,10},{10,8},{12,14},{14,12},{1,3},{3,1},... | collective-permute-start | bytes 2949128 | tf_op jit(solution)/shard_map/ppermute | solution.py:23
  289.7 64.8 %collective-permute-start.18 = (bf16[192,2560]{1,0:T(8,128)(2,1)}, bf16[192,2560]{1,0:T(8,128)(2,1)}, u32[]{:S(2)}, u32[]{:S(2)}) collective-permute-start(bf16[192,2560]{1,0:T(8,128)(2,1)} %get-tuple-element.157), channel_id=1, source_target_pairs={{0,2},{2,0},{4,6},{6,4},{8,10},{10,8},{12,14},{14,12},{1,3},{3,1},... | collective-permute-start | bytes 2949128 | tf_op jit(solution)/shard_map/ppermute | solution.py:23
  290.3 12.0 %copy-start.4 = (bf16[2,3,192,1792]{3,2,1,0:T(8,128)(2,1)S(1)}, bf16[2,3,192,1792]{3,2,1,0:T(8,128)(2,1)}, u32[]{:S(2)}) copy-start(bf16[2,3,192,1792]{3,2,1,0:T(8,128)(2,1)} %get-tuple-element.137) | copy-start | bytes 12386308
  324.9 1.0 copy-start.5
  326.4 88.4 %collective-permute-start.16 = (bf16[3,192,768]{2,1,0:T(8,128)(2,1)}, bf16[3,192,768]{2,1,0:T(8,128)(2,1)}, u32[]{:S(2)}, u32[]{:S(2)}) collective-permute-start(bf16[3,192,768]{2,1,0:T(8,128)(2,1)} %get-tuple-element.149), channel_id=1, source_target_pairs={{0,8},{8,0},{2,10},{10,2},{4,12},{12,4},{6,14},{14,6},{1,9},{9,1},... | collective-permute-start | bytes 2654216 | tf_op jit(solution)/shard_map/ppermute | solution.py:23
  354.6 0.9 copy-start.8
  375.6 97.7 %collective-permute-start.19 = (bf16[192,2560]{1,0:T(8,128)(2,1)}, bf16[192,2560]{1,0:T(8,128)(2,1)S(1)}, u32[]{:S(2)}, u32[]{:S(2)}) collective-permute-start(bf16[192,2560]{1,0:T(8,128)(2,1)} %get-tuple-element.176), channel_id=1, source_target_pairs={{0,4},{4,0},{2,6},{6,2},{8,12},{12,8},{10,14},{14,10},{1,5},{5,1},... | collective-permute-start | bytes 2949128 | tf_op jit(solution)/shard_map/ppermute | solution.py:23
  375.7 97.7 %collective-permute-start.20 = (bf16[192,2560]{1,0:T(8,128)(2,1)}, bf16[192,2560]{1,0:T(8,128)(2,1)S(1)}, u32[]{:S(2)}, u32[]{:S(2)}) collective-permute-start(bf16[192,2560]{1,0:T(8,128)(2,1)} %get-tuple-element.177), channel_id=1, source_target_pairs={{0,4},{4,0},{2,6},{6,2},{8,12},{12,8},{10,14},{14,10},{1,5},{5,1},... | collective-permute-start | bytes 2949128 | tf_op jit(solution)/shard_map/ppermute | solution.py:23
  377.7 74.3 %collective-permute-start.15 = (bf16[3,192,256]{2,1,0:T(8,128)(2,1)}, bf16[3,192,256]{2,1,0:T(8,128)(2,1)}, u32[]{:S(2)}, u32[]{:S(2)}) collective-permute-start(bf16[3,192,256]{2,1,0:T(8,128)(2,1)} %get-tuple-element.147), channel_id=1, source_target_pairs={{0,8},{8,0},{2,10},{10,2},{4,12},{12,4},{6,14},{14,6},{1,9},{9,1},... | collective-permute-start | bytes 884744 | tf_op jit(solution)/shard_map/ppermute | solution.py:23
  473.3 1.3 copy-start.10
  (2 other events, 1.9 us)

commit v2 on v1

--- a/solution.py
+++ b/solution.py
@@ -1,4 +1,5 @@
 import functools
+import itertools
 
 import jax
 import jax.numpy as jnp
@@ -9,7 +10,7 @@
 
 VMEM_BYTES = 62 * 1024 * 1024
 TILE = 256
-COST_SCALE = 0.03e9
+COST_SCALE = 0.1e9
 G, U, PRE = 0, 1, 2
 
 
@@ -205,7 +206,7 @@
     return [((gate, up, down)[kind], tall if kind == PRE else wide) for kind in kinds]
 
 
-def partials(order, units, tiles, sources, weights, after=()):
+def partials(order, units, tiles, sources, weights, after=(), pack=False):
     first, count = tiles
     rows, depth = sources[0].shape[2:]
     kinds = [kind for kind in (G, U, PRE) if any(kind in unit[0] for unit in units)]
@@ -226,6 +227,13 @@
                     at = unit_kinds.index(kind)
                     outs[2 * m][at] = term[start : start + size]
                     outs[2 * m + 1][at] = term[start : start + size].astype(jnp.bfloat16)
+        if pack:
+
+            @pl.when(pl.program_id(0) == 0)
+            def _():
+                for d in range(2):
+                    outs[-1][d, 0] = ins[kinds.index(G)][0, 0]
+                    outs[-1][d, 1] = ins[kinds.index(PRE)][0, 0]
 
     outputs = []
     for unit_kinds, _, size in units:
@@ -233,12 +241,19 @@
         spec = pl.BlockSpec((len(unit_kinds), size, TILE), lambda j: (0, 0, j))
         outputs.append((jax.ShapeDtypeStruct(shape, jnp.float32), spec))
         outputs.append((jax.ShapeDtypeStruct(shape, jnp.bfloat16), spec))
-    results = order.call(body, "partials", (1 + 0.8 * count) * n, count, inputs, outputs, after=after)
-    return list(zip(results[::2], results[1::2]))
-
-
-def hidden_and_back(order, tiles, parts, weights, out_type, addend=()):
+    if pack:
+        shape = (2, 2, rows, depth)
+        spec = pl.BlockSpec(shape, lambda j: (0, 0, 0, 0))
+        outputs.append((jax.ShapeDtypeStruct(shape, jnp.bfloat16), spec))
+    cost = (1 + 0.8 * count) * n
+    results = order.call(body, "partials", cost, count, inputs, outputs, after=after)
+    pairs = list(zip(results[: 2 * len(units) : 2], results[1::2]))
+    return pairs, results[-1]
+
+
+def hidden_and_back(order, tiles, parts, weights, out_type, addend=None, cuts=1, twice=True):
     first, count = tiles
+    copies, hqr_cuts = (2, 1) if twice else (1, 2)
     sizes = [kept.shape[1] for kept, _ in parts]
     rows = sum(sizes)
     depth = weights[0].shape[1]
@@ -247,13 +262,13 @@
         spec = pl.BlockSpec((3, size, TILE), lambda j: (0, 0, j))
         inputs += [(array, spec) for array in pair]
     n = len(inputs)
+    size = rows // hqr_cuts
     inputs += weight_specs(weights, (G, U, PRE), first)
-    sums_spec = pl.BlockSpec((rows, depth), lambda j: (0, 0))
-    inputs += [(array, sums_spec) for array in addend]
+    if addend is not None:
+        inputs.append((addend, pl.BlockSpec(addend.shape, lambda j: (0, 0, 0))))
 
     def body(ins, outs, scratch):
         wg_ref, wu_ref, wd_ref = ins[n : n + 3]
-        hqr_ref = outs[0]
         acc_ref = scratch[0]
         j = pl.program_id(0)
         terms = [ins[m][...] + ins[m + 1][...].astype(jnp.float32) for m in range(0, n, 2)]
@@ -264,8 +279,8 @@
         q = (p * u * s * (1.0 + g * (1.0 - s))).astype(jnp.bfloat16)
         r = (p * a).astype(jnp.bfloat16)
         for i, value in enumerate((h, q, r)):
-            hqr_ref[0, i] = value
-            hqr_ref[1, i] = value
+            for cut, copy in itertools.product(range(hqr_cuts), range(copies)):
+                outs[cut][copy, i] = value[cut * size : (cut + 1) * size]
         out_term = jnp.dot(h, wd_ref[0], preferred_element_type=jnp.float32)
         in_term = contract_cols(q, wg_ref[0]) + contract_cols(r, wu_ref[0])
 
@@ -281,26 +296,30 @@
 
         @pl.when(j == count - 1)
         def _():
-            for i in range(2):
-                total = acc_ref[i]
-                if addend:
-                    total = total + ins[n + 3 + i][...].astype(jnp.float32)
-                outs[1 + i][...] = total.astype(out_type)
+            total = acc_ref[...]
+            if addend is not None:
+                total = total + ins[n + 3][...].astype(jnp.float32)
+            step = rows // cuts
+            for cut, ref in enumerate(outs[hqr_cuts:]):
+                ref[...] = total[:, cut * step : (cut + 1) * step].astype(out_type)
 
     outputs = [
         (
-            jax.ShapeDtypeStruct((2, 3, rows, count * TILE), jnp.bfloat16),
-            pl.BlockSpec((2, 3, rows, TILE), lambda j: (0, 0, 0, j)),
-        ),
-    ]
-    outputs += [(jax.ShapeDtypeStruct((rows, depth), out_type), sums_spec)] * 2
+            jax.ShapeDtypeStruct((copies, 3, size, count * TILE), jnp.bfloat16),
+            pl.BlockSpec((copies, 3, size, TILE), lambda j: (0, 0, 0, j)),
+        )
+    ] * hqr_cuts
+    shape = (2, rows // cuts, depth)
+    sums_spec = pl.BlockSpec(shape, lambda j: (0, 0, 0))
+    outputs += [(jax.ShapeDtypeStruct(shape, out_type), sums_spec)] * cuts
     scratch = [pltpu.VMEM((2, rows, depth), jnp.float32)]
     return order.call(body, "hidden_and_back", 3 + 2.2 * count, count, inputs, outputs, scratch)
 
 
 def assemble(order, blocks):
+    n = len(blocks)
     rows, depth = blocks[0].shape[2:]
-    total = 2 * rows * len(blocks)
+    total = 2 * rows * n
     inputs = []
     for block in blocks:
         for part in range(2):
@@ -310,7 +329,7 @@
     def body(ins, outs, scratch):
         xt_ref, e_ref = outs
         x_all = scratch[0]
-        for b in range(len(blocks)):
+        for b in range(n):
             for d in range(2):
                 at = pl.ds((2 * b + d) * rows, rows)
                 x_all[at, :] = ins[2 * b][d, 0]
@@ -328,10 +347,10 @@
         ),
     ]
     scratch = [pltpu.VMEM((total, TILE), jnp.bfloat16)]
-    return order.call(body, "assemble", 10, depth // TILE, inputs, outputs, scratch)
-
-
-def weight_grads(order, tiles, tokens, pieces, width, so_far=None, into=None):
+    return order.call(body, "assemble", 5 * n, depth // TILE, inputs, outputs, scratch)
+
+
+def weight_grads(order, side, tiles, tokens, pieces, width, so_far=None, into=None):
     first, count = tiles
     xt, e_all = tokens
     depth, total = xt.shape
@@ -339,10 +358,24 @@
         pl.BlockSpec((depth, total), lambda j: (0, 0), pipeline_mode=pl.Buffered(1)),
         pl.BlockSpec((total, depth), lambda j: (0, 0), pipeline_mode=pl.Buffered(1)),
     ]
-    inputs = [(xt, whole[0]), (e_all, whole[1])]
-    for _, _, hqr, start in pieces:
-        index = functools.partial(lambda j, start: (0, 0, 0, start + j), start=start)
-        inputs.append((hqr, pl.BlockSpec((2, 3, hqr.shape[2], TILE), index)))
+    inputs = [(side, pl.BlockSpec(memory_space=pltpu.SMEM)), (xt, whole[0]), (e_all, whole[1])]
+    bounds = []
+    for _, _, *arrays in pieces:
+        at = 0
+        for hqr in arrays:
+            at = 0 if hqr.shape[0] == 1 else at
+            size = hqr.shape[3] // TILE
+
+            def index(j, at, size):
+                return 0, 0, 0, jnp.clip(first + j - at, 0, size - 1)
+
+            spec = pl.BlockSpec(
+                (hqr.shape[0], 3, hqr.shape[2], TILE),
+                functools.partial(index, at=at, size=size),
+            )
+            inputs.append((hqr, spec))
+            bounds.append((at, at + size))
+            at += size
     wide = pl.BlockSpec((1, depth, TILE), lambda j: (0, 0, first + j))
     tall = pl.BlockSpec((1, TILE, depth), lambda j: (0, first + j, 0))
     specs = (wide, wide, tall)
@@ -357,14 +390,30 @@
 
     def body(ins, outs, scratch):
         hqr_all = scratch[0]
-        for m, (*starts, hqr, _) in enumerate(pieces):
-            for d, start in enumerate(starts):
-                for i in range(3):
-                    hqr_all[i, start : start + hqr.shape[2], :] = ins[2 + m][d, i]
+        tile = first + pl.program_id(0)
+        m = 0
+        for lower, higher, *arrays in pieces:
+            for n_array, hqr in enumerate(arrays):
+
+                def take(m=m, starts=(lower, higher), rows=hqr.shape[2]):
+                    for d, start in enumerate(starts):
+                        for i in range(3):
+                            hqr_all[i, pl.ds(start, rows), :] = ins[3 + m][d, i]
+
+                if hqr.shape[0] == 1:
+                    upper = ins[0][0] if n_array == 0 else 1 - ins[0][0]
+                    start = pl.multiple_of(lower + upper * (higher - lower), 16)
+                    take(starts=(start,))
+                elif len(arrays) == 1:
+                    take()
+                else:
+                    low, high = bounds[m]
+                    pl.when((tile >= low) & (tile < high))(take)
+                m += 1
         terms = (
-            lambda: jnp.dot(ins[0][...], hqr_all[1], preferred_element_type=jnp.float32),
-            lambda: jnp.dot(ins[0][...], hqr_all[2], preferred_element_type=jnp.float32),
-            lambda: contract_rows(hqr_all[0], ins[1][...]),
+            lambda: jnp.dot(ins[1][...], hqr_all[1], preferred_element_type=jnp.float32),
+            lambda: jnp.dot(ins[1][...], hqr_all[2], preferred_element_type=jnp.float32),
+            lambda: contract_rows(hqr_all[0], ins[2][...]),
         )
         for i, term in enumerate(terms):
             value = term()
@@ -384,20 +433,27 @@
 
 def add_row_sums(order, own_sums, near_sums, far_sums, acts, cotangent):
     rows, depth = acts.shape[2:]
-    step = rows // 4
-    spec = pl.BlockSpec((step, depth), lambda j: (j, 0))
+    cuts = len(far_sums)
+    step = rows // cuts
+    spec = pl.BlockSpec((2, step, depth), lambda j: (0, j, 0))
+    each = pl.BlockSpec((2, step, depth), lambda j: (0, 0, 0))
     token_spec = pl.BlockSpec((1, 1, step, depth), lambda j: (0, 0, j, 0))
-    inputs = [(array, spec) for array in (*own_sums, *near_sums, *far_sums)]
-    inputs += [(acts, token_spec), (cotangent, token_spec)]
+    inputs = [(own_sums, spec), (acts, token_spec), (cotangent, token_spec)]
+    inputs += [(array, each) for array in (*near_sums, *far_sums)]
 
     def body(ins, outs, _):
-        for i in range(2):
-            total = ins[i][...] + ins[2 + i][...].astype(jnp.float32)
-            total += ins[4 + i][...].astype(jnp.float32) + ins[6 + i][0, 0].astype(jnp.float32)
-            outs[i][0, 0] = total.astype(jnp.bfloat16)
+        def add(j):
+            for i in range(2):
+                total = ins[0][i] + ins[3 + j][i].astype(jnp.float32)
+                total += ins[3 + cuts + j][i].astype(jnp.float32)
+                total += ins[1 + i][0, 0].astype(jnp.float32)
+                outs[i][0, 0] = total.astype(jnp.bfloat16)
+
+        for j in range(cuts):
+            pl.when(pl.program_id(0) == j)(functools.partial(add, j))
 
     outputs = [(jax.ShapeDtypeStruct(acts.shape, jnp.bfloat16), token_spec)] * 2
-    return order.call(body, "add_row_sums", 5, 4, inputs, outputs)
+    return order.call(body, "add_row_sums", 5, cuts, inputs, outputs)
 
 
 def two_by_four(acts, cotangent, w_gate, w_up, w_down):
@@ -407,6 +463,7 @@
     width = w_gate.shape[2]
     n_tiles = width // TILE
     weights = (w_gate, w_up, w_down)
+    side = lax.axis_index("dp").astype(jnp.int32).reshape(1)
     order = Order()
 
     sources = {"own": (acts, cotangent)}
@@ -418,16 +475,16 @@
     gather("far", "own", far)
 
     a = max(1, n_tiles * 3 // 7)
-    b = n_tiles - 1
     every = (0, n_tiles)
-    chunks = {"c0": (0, a), "c1": (a, b - a), "c2": (b, n_tiles - b)}
-    own, ready, got = {}, {}, {}
-
-    def compute(names, units, tiles, block, after=()):
-        after = [got[key] for key in after]
-        results = partials(order, units, tiles, sources[block], weights, after)
+    chunks = {"c0": (0, a), "c1": (a, n_tiles - a)}
+    own, ready, got, pairs = {}, {}, {}, {}
+
+    def compute(names, units, tiles, block, pack=False):
+        results, pair = partials(order, units, tiles, sources[block], weights, pack=pack)
         for name, (kept, rounded) in zip(names, results):
             own[name], ready[name] = kept, rounded
+        if pack:
+            pairs[block] = order.need(both_replicas(pair), 0)
 
     def send(name, after=()):
         rounded = ready[name]
@@ -435,98 +492,82 @@
             rounded = order.hold(rounded, [got[key] for key in after])
         got[name] = from_partner(rounded, "grid", across)
 
-    hqr, sums, passed = {}, {}, {}
+    hqr, sums = {}, {}
 
     def both_replicas(pair):
         return lax.all_to_all(pair, "dp", 0, 0, tiled=True)
 
-    def twice(x, e):
-        return jnp.stack([x[0, 0], e[0, 0], x[0, 0], e[0, 0]]).reshape(2, 2, *x.shape[2:])
-
-    def finish(name, names, tiles, out_type=jnp.bfloat16, addend=()):
-        parts = [(own[key], got[key]) for key in names]
-        pair, *sums[name] = hidden_and_back(order, tiles, parts, weights, out_type, addend)
-        hqr[name] = both_replicas(pair)
-
-    def pieces_of(groups, start):
+    def finish(name, tiles, parts=None, addend=None, calls=99):
+        parts = [(own[key], got[key]) for key in parts or [name]]
+        cuts = parts[0][0].shape[1] * len(parts) // half if tiles == every else 1
+        out_type = jnp.bfloat16 if tiles == every else jnp.float32
+        twice = name not in ("fa", "fb")
+        found, *rest = hidden_and_back(
+            order, tiles, parts, weights, out_type, addend, cuts, twice
+        )
+        if twice:
+            hqr[name] = (order.need(both_replicas(found), calls),)
+        else:
+            for cut, part in enumerate((found, rest.pop(0))):
+                hqr[name, cut] = (part, order.need(from_partner(part, "dp", 0), calls))
+        sums[name] = rest
+
+    def pieces_of(*groups):
         found = []
         at = 0
         for group in groups:
-            size = sum(hqr[name].shape[2] for name in group)
-            for name in group:
-                first = start if hqr[name].shape[3] == width else 0
-                found.append((at, at + size, hqr[name], first))
-                at += hqr[name].shape[2]
+            size = sum(hqr[names[0]][0].shape[2] for names in group)
+            for names in group:
+                found.append((at, at + size, *(array for name in names for array in hqr[name])))
+                at += hqr[names[0]][0].shape[2]
             at += size
         return found
 
-    def pass_on(name, bit, calls):
-        passed[name] = [order.need(from_partner(sum, "grid", bit), calls) for sum in sums[name]]
+    def pass_on(array, bit, calls):
+        return order.need(from_partner(array, "grid", bit), calls)
 
     def collect(*names):
-        return assemble(order, [both_replicas(twice(*sources[name])) for name in names])
+        return assemble(order, [pairs[name] for name in names])
 
     gup = (G, U, PRE)
     everything = [(gup, 0, rows)]
     halves = [(gup, 0, half), (gup, half, half)]
     compute(["c0"], everything, chunks["c0"], "own")
     send("c0")
-    compute(["c1"], everything, chunks["c1"], "own")
-    compute(["c2"], everything, chunks["c2"], "own")
-    compute(["na", "nb"], halves, every, "near")
-    send("na")
-    send("nb", ["c0"])
-    finish("c0", ["c0"], chunks["c0"], jnp.float32)
+    compute(["c1"], everything, chunks["c1"], "own", pack=True)
+    compute(["near"], everything, every, "near", pack=True)
+    send("near")
+    finish("c0", chunks["c0"], calls=1)
     sources["far"] = tuple(order.hold(array, []) for array in sources["far"])
     gather("both", "far", near)
-    compute(["fa", "fb"], halves, every, "far")
-    late = collect("far", "own")
-    compute(["ba", "bb"], halves, every, "both", ["na"])
+    compute(["fa", "fb"], halves, every, "far", pack=True)
+    send("c1", ["c0"])
+    early = collect("near", "own")
+    compute(["ba", "bb"], halves, every, "both", pack=True)
     send("ba")
-    send("bb", ["nb"])
-    finish("near", ["na", "nb"], every)
-    pass_on("near", near, 3)
-    early = collect("near", "both")
+    late = collect("both", "far")
+    send("bb", ["near"])
+    finish("near", every)
+    near_sums = [pass_on(array, near, 4) for array in sums["near"]]
+    finish("c1", chunks["c1"], addend=sums["c0"][0])
     send("fa", ["ba"])
+    early_pieces = pieces_of([["near"]], [["c0", "c1"]])
+    mid = n_tiles // 2
+    first = weight_grads(order, side, (0, mid), early, early_pieces, width)
     send("fb", ["bb"])
-    finish("both", ["ba", "bb"], every)
-    pass_on("both", near, 9)
-    early_pieces = pieces_of([["near"], ["both"]], 0)
-    mid = n_tiles // 2
-    first = weight_grads(order, (0, mid), early, early_pieces, width)
-    send("c1", ["fa"])
-    first = weight_grads(
-        order,
-        (mid, n_tiles - mid),
-        early,
-        pieces_of([["near"], ["both"]], mid),
-        width,
-        into=first,
-    )
-    send("c2", ["fb"])
-    finish("far", ["fa", "fb"], every, addend=passed["both"])
-    pass_on("far", far, 20)
-
-    grads = None
-
-    def final(name):
-        return weight_grads(
-            order,
-            chunks[name],
-            late,
-            pieces_of([["far"], [name]], chunks[name][0]),
-            width,
-            first,
-            grads,
-        )
-
-    grads = final("c0")
-    last = "c0"
-    for name in ("c1", "c2"):
-        finish(name, [name], chunks[name], jnp.float32, sums[last])
-        last = name
-        grads = final(name)
-    outs = add_row_sums(order, sums[last], passed["near"], passed["far"], acts, cotangent)
+    finish("both", every, parts=["ba", "bb"], calls=1)
+    both_sums = [pass_on(sums["both"][0], near, 99)]
+    rest = (mid, n_tiles - mid)
+    first = weight_grads(order, side, rest, early, early_pieces, width, into=first)
+    both_sums.append(pass_on(order.hold(sums["both"][1], []), near, 99))
+    far_sums = []
+    for name, addend in zip(("fa", "fb"), both_sums):
+        finish(name, every, addend=addend, calls=0)
+        far_sums.append(pass_on(sums[name][0], far, 99))
+    far_names = [[(name, cut)] for name in ("fa", "fb") for cut in range(2)]
+    late_pieces = pieces_of([["both"]], far_names)
+    grads = weight_grads(order, side, every, late, late_pieces, width, first)
+    outs = add_row_sums(order, sums["c1"][0], near_sums, far_sums, acts, cotangent)
     return (*outs, *grads)
 
 

time: 482 us -> 456 us (0.946)
  blocking collectives: 77.4 us -> 34.9 us
  waiting for transfers between devices: 73.1 us -> 90.2 us
  other arithmetic: 14.1 us -> 0 us
  starting transfers between devices: 39.8 us -> 49.4 us
    all_to_all x8 -> x3, blocking collectives: 77.4 us -> 34.9 us  [both_replicas(): return lax.all_to_all(pair, 'dp', 0, 0, tiled=True)]
    all_to_all x2 -> x5, starting transfers between devices: 11 us -> 25.8 us  [both_replicas(): return lax.all_to_all(pair, 'dp', 0, 0, tiled=True)]
    another operation x4 -> x0, other arithmetic: 14.1 us -> none  [twice(): jnp.stack([x[0, 0], e[0, 0], x[0, 0], e[0, 0]]).reshape(2, 2, *x.shape[2:])]
    ppermute x21 -> x23, waiting for transfers between devices: 73 us -> 81.8 us  [from_partner(): return lax.ppermute(block, axis, route)]
    all_to_all x2 -> x5, waiting for transfers between devices: 0.06 us -> 8.34 us  [both_replicas(): return lax.all_to_all(pair, 'dp', 0, 0, tiled=True)]
    ppermute x21 -> x23, starting transfers between devices: 28.8 us -> 23.6 us  [from_partner(): return lax.ppermute(block, axis, route)]
    pallas_call x28 -> x24, Pallas kernels: 270 us -> 271 us  [call(): pl.pallas_call(kernel, name=name, grid=(steps,), in_specs=[spec for _, sp...]
  transfers between devices with their start and end apart: 23 -> 28, of which waited for: 6 -> 13; matrix products, arithmetic and copies ran while one was open for 3% -> 0% of each run, Pallas kernels for 55% -> 58%
where the time goes in v2:
time: 456 us; the launch traced here: 454 us
  Pallas kernels  271 us (59%)
  waiting for transfers between devices  90.2 us (20%)
  starting transfers between devices  49.4 us (11%)
  blocking collectives  34.9 us (8%)
  local copies, waits for them, and re-layouts  8.09 us (2%)
    pallas_call x24, Pallas kernels, call(): pl.pallas_call(kernel, name=name, grid=(steps,), in_specs=[spec for _, sp...  271 us
    ppermute x23, waiting for transfers between devices, from_partner(): return lax.ppermute(block, axis, route)  81.8 us
    all_to_all x3, blocking collectives, both_replicas(): return lax.all_to_all(pair, 'dp', 0, 0, tiled=True)  34.9 us
    all_to_all x5, starting transfers between devices, both_replicas(): return lax.all_to_all(pair, 'dp', 0, 0, tiled=True)  25.8 us
    ppermute x23, starting transfers between devices, from_partner(): return lax.ppermute(block, axis, route)  23.6 us
  transfers between devices with their start and end apart: 28, of which 13 were waited for; matrix products, arithmetic and copies ran while one was open for 0% of the time, Pallas kernels for 58%

profile of v2, /device:TPU:0, one launch (start us, length us, event | category | flops | bytes accessed | tf_op | source)
XLA Modules:
  0.0 454.1 jit_solution(16981769061317335154)
XLA Ops:
  0.6 3.0 collective-permute-start.2
  5.8 9.9 %partials.5 = (f32[3,192,768]{2,1,0:T(8,128)}, bf16[3,192,768]{2,1,0:T(8,128)(2,1)}, f32[8,128]{1,0:T(8,128)}) custom-call(bf16[1,1,192,2560]{3,2,1,0:T(8,128)(2,1)} %refs_1_.5, bf16[1,1,192,2560]{3,2,1,0:T(8,128)(2,1)} %refs_1_.5, bf16[1,1,192,2560]{3,2,1,0:T(8,128)(2,1)} %refs_2_.15, bf16[1,2560,1792]{2,1,0:T(8,128)(2,1)} %refs_2_.14, ...), custom_call_target="tpu_custom_call" | custom-call | flops 1020000000 | tf_op jit(solution)/shard_map/partials/pallas_call | solution.py:175
  18.7 12.9 %partials.6 = (f32[3,192,1024]{2,1,0:T(8,128)}, bf16[3,192,1024]{2,1,0:T(8,128)(2,1)}, bf16[2,2,192,2560]{3,2,1,0:T(8,128)(2,1)}, f32[8,128]{1,0:T(8,128)}) custom-call(bf16[1,1,192,2560]{3,2,1,0:T(8,128)(2,1)} %refs_1_.5, bf16[1,1,192,2560]{3,2,1,0:T(8,128)(2,1)} %refs_1_.5, bf16[1,1,192,2560]{3,2,1,0:T(8,128)(2,1)} %refs_2_.15, ...), custom_call_target="tpu_custom_call" | custom-call | flops 1260000000 | tf_op jit(solution)/shard_map/partials/pallas_call | solution.py:175
  31.6 11.6 %all_to_all.40.refs_7_.refs_2_.refs_3_ = bf16[2,2,192,2560]{3,2,1,0:T(8,128)(2,1)} all-to-all(bf16[2,2,192,2560]{3,2,1,0:T(8,128)(2,1)} %get-tuple-element.90), channel_id=1, replica_groups=mesh['groups'=2,'grid'=8,'dp'=2] {'dp'}, dimensions={0} | all-to-all | bytes 7864320 | tf_op jit(solution)/shard_map/all_to_all | solution.py:498
  43.2 3.6 collective-permute-done.3.refs_2_
  46.8 19.4 %partials.7 = (f32[3,192,1792]{2,1,0:T(8,128)}, bf16[3,192,1792]{2,1,0:T(8,128)(2,1)}, bf16[2,2,192,2560]{3,2,1,0:T(8,128)(2,1)}, f32[8,128]{1,0:T(8,128)}) custom-call(bf16[1,1,192,2560]{3,2,1,0:T(8,128)(2,1)} %copy-done.4, bf16[1,1,192,2560]{3,2,1,0:T(8,128)(2,1)} %copy-done.4, bf16[1,1,192,2560]{3,2,1,0:T(8,128)(2,1)} %collective-permute-done.3.refs_2_, ...), custom_call_target="tpu_custom_call" | custom-call | flops 1980000000 | tf_op jit(solution)/shard_map/partials/pallas_call | solution.py:175
  69.1 5.5 %all-to-all-start.1 = ((bf16[2,2,192,2560]{3,2,1,0:T(8,128)(2,1)}), bf16[2,2,192,2560]{3,2,1,0:T(8,128)(2,1)}, u32[]{:S(2)}, u32[]{:S(2)}) async-start(bf16[2,2,192,2560]{3,2,1,0:T(8,128)(2,1)} %get-tuple-element.92), calls=%async_computation.1 | async-start | bytes 7864320 | tf_op jit(solution)/shard_map/all_to_all | solution.py:498
  74.7 4.3 all-to-all-done.1.refs_6_.refs_0_.refs_1_
  78.9 10.7 %hidden_and_back.6 = (bf16[2,3,192,768]{3,2,1,0:T(8,128)(2,1)}, f32[2,192,2560]{2,1,0:T(8,128)}, f32[8,128]{1,0:T(8,128)}) custom-call(f32[3,192,768]{2,1,0:T(8,128)} %get-tuple-element.88.refs_0_, bf16[3,192,768]{2,1,0:T(8,128)(2,1)} %copy-done.5, bf16[1,2560,1792]{2,1,0:T(8,128)(2,1)} %refs_2_.14, bf16[1,2560,1792]{2,1,0:T(8,128)(2,1)} %refs_3_.19, ...), custom_call_target="tpu_custom_call" | custom-call | flops 960000000 | tf_op jit(solution)/shard_map/hidden_and_back/pallas_call | solution.py:175
  89.6 3.7 all-to-all-start.2
  99.8 19.5 %partials.8 = (f32[3,96,1792]{2,1,0:T(8,128)}, bf16[3,96,1792]{2,1,0:T(8,128)(2,1)}, f32[3,96,1792]{2,1,0:T(8,128)}, bf16[3,96,1792]{2,1,0:T(8,128)(2,1)}, bf16[...) custom-call(bf16[1,1,192,2560]{3,2,1,0:T(8,128)(2,1)} %get-tuple-element.94.refs_0_.refs_1_, ...), custom_call_target="tpu_custom_call" | custom-call | flops 1980000000 | tf_op jit(solution)/shard_map/partials/pallas_call | solution.py:175
  119.3 11.6 %all_to_all.41.refs_3_.refs_2_ = bf16[2,2,192,2560]{3,2,1,0:T(8,128)(2,1)} all-to-all(bf16[2,2,192,2560]{3,2,1,0:T(8,128)(2,1)} %get-tuple-element.100), channel_id=1, replica_groups=mesh['groups'=2,'grid'=8,'dp'=2] {'dp'}, dimensions={0} | all-to-all | bytes 7864320 | tf_op jit(solution)/shard_map/all_to_all | solution.py:498
  131.6 10.1 %assemble.2 = (bf16[2560,768]{1,0:T(8,128)(2,1)}, bf16[768,2560]{1,0:T(8,128)(2,1)}, f32[8,128]{1,0:T(8,128)}) custom-call(bf16[2,2,192,2560]{3,2,1,0:T(8,128)(2,1)} %all-to-all-done.1.refs_6_.refs_0_.refs_1_, bf16[2,2,192,2560]{3,2,1,0:T(8,128)(2,1)} %all-to-all-done.1.refs_6_.refs_0_.refs_1_, bf16[2,2,192,2560]{3,2,1,0:T(8,128)(2,1)} %all_to_all.40.refs_7_.refs_2_.refs_3_, ...), custom_call_target="tpu_custom_call" | custom-call | flops 1000000000 | tf_op jit(solution)/shard_map/assemble/pallas_call | solution.py:175
  143.8 19.4 %partials.9 = (f32[3,96,1792]{2,1,0:T(8,128)}, bf16[3,96,1792]{2,1,0:T(8,128)(2,1)}, f32[3,96,1792]{2,1,0:T(8,128)}, bf16[3,96,1792]{2,1,0:T(8,128)(2,1)}, bf16[...) custom-call(bf16[1,1,192,2560]{3,2,1,0:T(8,128)(2,1)} %copy-done.3, bf16[1,1,192,2560]{3,2,1,0:T(8,128)(2,1)} %copy-done.3, ...), custom_call_target="tpu_custom_call" | custom-call | flops 1980000000 | tf_op jit(solution)/shard_map/partials/pallas_call | solution.py:175
  163.2 5.7 %all-to-all-start.4 = ((bf16[2,2,192,2560]{3,2,1,0:T(8,128)(2,1)}), bf16[2,2,192,2560]{3,2,1,0:T(8,128)(2,1)}, u32[]{:S(2)}, u32[]{:S(2)}) async-start(bf16[2,2,192,2560]{3,2,1,0:T(8,128)(2,1)} %get-tuple-element.108), calls=%async_computation.4 | async-start | bytes 7864320 | tf_op jit(solution)/shard_map/all_to_all | solution.py:498
  173.1 10.0 %assemble.3 = (bf16[2560,768]{1,0:T(8,128)(2,1)}, bf16[768,2560]{1,0:T(8,128)(2,1)}, f32[8,128]{1,0:T(8,128)}) custom-call(bf16[2,2,192,2560]{3,2,1,0:T(8,128)(2,1)} %all-to-all-done.4.refs_0_.refs_1_.refs_5_, bf16[2,2,192,2560]{3,2,1,0:T(8,128)(2,1)} %all-to-all-done.4.refs_0_.refs_1_.refs_5_, bf16[2,2,192,2560]{3,2,1,0:T(8,128)(2,1)} %all_to_all.41.refs_3_.refs_2_, ...), custom_call_target="tpu_custom_call" | custom-call | flops 1000000000 | tf_op jit(solution)/shard_map/assemble/pallas_call | solution.py:175
  183.1 23.2 %collective-permute-done.6.refs_1_ = bf16[3,192,1792]{2,1,0:T(8,128)(2,1)} collective-permute-done((bf16[3,192,1792]{2,1,0:T(8,128)(2,1)}, bf16[3,192,1792]{2,1,0:T(8,128)(2,1)}, u32[]{:S(2)}, u32[]{:S(2)}) %collective-permute-start.6) | collective-permute-done | bytes 2064416 | tf_op jit(solution)/shard_map/ppermute | solution.py:24
  206.9 18.7 %hidden_and_back.7 = (bf16[2,3,192,1792]{3,2,1,0:T(8,128)(2,1)}, bf16[2,96,2560]{2,1,0:T(8,128)(2,1)}, bf16[2,96,2560]{2,1,0:T(8,128)(2,1)}, f32[8,128]{1,0:T(8,128)}) custom-call(f32[3,192,1792]{2,1,0:T(8,128)} %get-tuple-element.103.refs_0_, bf16[3,192,1792]{2,1,0:T(8,128)(2,1)} %collective-permute-done.6.refs_1_, bf16[1,2560,1792]{2,1,0:T(8,128)(2,1)} %refs_2_.14, ...), custom_call_target="tpu_custom_call" | custom-call | flops 1840000000 | tf_op jit(solution)/shard_map/hidden_and_back/pallas_call | solution.py:175
  227.8 26.0 %collective-permute-done.5.refs_1_ = bf16[3,192,1024]{2,1,0:T(8,128)(2,1)} collective-permute-done((bf16[3,192,1024]{2,1,0:T(8,128)(2,1)}, bf16[3,192,1024]{2,1,0:T(8,128)(2,1)}, u32[]{:S(2)}, u32[]{:S(2)}) %collective-permute-start.5) | collective-permute-done | bytes 1179680 | tf_op jit(solution)/shard_map/ppermute | solution.py:24
  253.7 14.4 %hidden_and_back.8 = (bf16[2,3,192,1024]{3,2,1,0:T(8,128)(2,1)}, f32[2,192,2560]{2,1,0:T(8,128)}, f32[8,128]{1,0:T(8,128)}) custom-call(f32[3,192,1024]{2,1,0:T(8,128)} %get-tuple-element.85.refs_0_, bf16[3,192,1024]{2,1,0:T(8,128)(2,1)} %collective-permute-done.5.refs_1_, bf16[1,2560,1792]{2,1,0:T(8,128)(2,1)} %refs_2_.14, bf16[1,2560,1792]{2,1,0:T(8,128)(2,1)} %refs_3_.19, ...), custom_call_target="tpu_custom_call" | custom-call | flops 1180000000 | tf_op jit(solution)/shard_map/hidden_and_back/pallas_call | solution.py:175
  268.1 4.9 %all-to-all-start.6 = ((bf16[2,3,192,1024]{3,2,1,0:T(8,128)(2,1)}), bf16[2,3,192,1024]{3,2,1,0:T(8,128)(2,1)}, u32[]{:S(2)}, u32[]{:S(2)}) async-start(bf16[2,3,192,1024]{3,2,1,0:T(8,128)(2,1)} %get-tuple-element.128), calls=%async_computation.6 | async-start | bytes 4718592 | tf_op jit(solution)/shard_map/all_to_all | solution.py:498
  277.3 11.8 %all_to_all.42.refs_3_ = bf16[2,3,192,1792]{3,2,1,0:T(8,128)(2,1)} all-to-all(bf16[2,3,192,1792]{3,2,1,0:T(8,128)(2,1)} %get-tuple-element.127), channel_id=1, replica_groups=mesh['groups'=2,'grid'=8,'dp'=2] {'dp'}, dimensions={0} | all-to-all | bytes 8257536 | tf_op jit(solution)/shard_map/all_to_all | solution.py:498
  289.0 15.2 %weight_grads.3 = (bf16[1,2560,1792]{2,1,0:T(8,128)(2,1)}, bf16[1,2560,1792]{2,1,0:T(8,128)(2,1)}, bf16[1,1792,2560]{2,1,0:T(8,128)(2,1)}, f32[8,128]{1,0:T(8,128)}) custom-call(s32[1]{0:T(128)} %bitcast.refs_0_, bf16[2560,768]{1,0:T(8,128)(2,1)} %get-tuple-element.125.refs_1_, bf16[768,2560]{1,0:T(8,128)(2,1)} %get-tuple-element.126.refs_2_, ...), custom_call_target="tpu_custom_call" | custom-call | flops 1600000000 | tf_op jit(solution)/shard_map/weight_grads/pallas_call | solution.py:175
  304.2 15.8 %collective-permute-done.13.refs_1_.refs_3_ = bf16[3,96,1792]{2,1,0:T(8,128)(2,1)} collective-permute-done((bf16[3,96,1792]{2,1,0:T(8,128)(2,1)}, bf16[3,96,1792]{2,1,0:T(8,128)(2,1)}, u32[]{:S(2)}, u32[]{:S(2)}) %collective-permute-start.13) | collective-permute-done | bytes 1032224 | tf_op jit(solution)/shard_map/ppermute | solution.py:24
  321.7 18.9 %hidden_and_back.9 = (bf16[2,3,192,1792]{3,2,1,0:T(8,128)(2,1)}, bf16[2,96,2560]{2,1,0:T(8,128)(2,1)}, bf16[2,96,2560]{2,1,0:T(8,128)(2,1)}, f32[8,128]{1,0:T(8,128)}) custom-call(f32[3,96,1792]{2,1,0:T(8,128)} %get-tuple-element.121.refs_0_, bf16[3,96,1792]{2,1,0:T(8,128)(2,1)} %copy-done.1, f32[3,96,1792]{2,1,0:T(8,128)} %get-tuple-element.122.refs_2_, ...), custom_call_target="tpu_custom_call" | custom-call | flops 1840000000 | tf_op jit(solution)/shard_map/hidden_and_back/pallas_call | solution.py:175
  342.1 5.9 %all-to-all-start.7 = ((bf16[2,3,192,1792]{3,2,1,0:T(8,128)(2,1)}), bf16[2,3,192,1792]{3,2,1,0:T(8,128)(2,1)}, u32[]{:S(2)}, u32[]{:S(2)}) async-start(bf16[2,3,192,1792]{3,2,1,0:T(8,128)(2,1)} %get-tuple-element.139), calls=%async_computation.7 | async-start | bytes 8257536 | tf_op jit(solution)/shard_map/all_to_all | solution.py:498
  348.1 18.4 %weight_grads.4 = (bf16[1,2560,1792]{2,1,0:T(8,128)(2,1)}, bf16[1,2560,1792]{2,1,0:T(8,128)(2,1)}, bf16[1,1792,2560]{2,1,0:T(8,128)(2,1)}, f32[8,128]{1,0:T(8,128)}) custom-call(s32[1]{0:T(128)} %bitcast.refs_0_, bf16[2560,768]{1,0:T(8,128)(2,1)} %get-tuple-element.125.refs_1_, ...), custom_call_target="tpu_custom_call", output_to_operand_aliasing={{0}: (6, {}), {1}: (7, {}), {2}: (8, {})} | custom-call | flops 2000000000 | tf_op jit(solution)/shard_map/weight_grads/pallas_call | solution.py:175
  368.9 16.8 %hidden_and_back.10 = (bf16[1,3,48,1792]{3,2,1,0:T(8,128)(2,1)}, bf16[1,3,48,1792]{3,2,1,0:T(8,128)(2,1)}, bf16[2,96,2560]{2,1,0:T(8,128)(2,1)}, f32[8,128]{1,0:T(8,128)}) custom-call(f32[3,96,1792]{2,1,0:T(8,128)} %get-tuple-element.116.refs_0_, bf16[3,96,1792]{2,1,0:T(8,128)(2,1)} %copy-done.10, bf16[1,2560,1792]{2,1,0:T(8,128)(2,1)} %refs_2_.14, ...), custom_call_target="tpu_custom_call" | custom-call | flops 1840000000 | tf_op jit(solution)/shard_map/hidden_and_back/pallas_call | solution.py:175
  391.2 5.0 %collective-permute-done.16.refs_1_ = bf16[3,96,1792]{2,1,0:T(8,128)(2,1)} collective-permute-done((bf16[3,96,1792]{2,1,0:T(8,128)(2,1)}, bf16[3,96,1792]{2,1,0:T(8,128)(2,1)}, u32[]{:S(2)}, u32[]{:S(2)}) %collective-permute-start.16) | collective-permute-done | bytes 1032224 | tf_op jit(solution)/shard_map/ppermute | solution.py:24
  397.2 16.8 %hidden_and_back.11 = (bf16[1,3,48,1792]{3,2,1,0:T(8,128)(2,1)}, bf16[1,3,48,1792]{3,2,1,0:T(8,128)(2,1)}, bf16[2,96,2560]{2,1,0:T(8,128)(2,1)}, f32[8,128]{1,0:T(8,128)}) custom-call(f32[3,96,1792]{2,1,0:T(8,128)} %get-tuple-element.142.refs_0_, bf16[3,96,1792]{2,1,0:T(8,128)(2,1)} %collective-permute-done.16.refs_1_, bf16[1,2560,1792]{2,1,0:T(8,128)(2,1)} %refs_2_.14, ...), custom_call_target="tpu_custom_call" | custom-call | flops 1840000000 | tf_op jit(solution)/shard_map/hidden_and_back/pallas_call | solution.py:175
  417.8 30.1 %weight_grads.5 = (bf16[1,2560,1792]{2,1,0:T(8,128)(2,1)}, bf16[1,2560,1792]{2,1,0:T(8,128)(2,1)}, bf16[1,1792,2560]{2,1,0:T(8,128)(2,1)}, f32[8,128]{1,0:T(8,128)}) custom-call(s32[1]{0:T(128)} %bitcast.refs_0_, bf16[2560,768]{1,0:T(8,128)(2,1)} %get-tuple-element.149.refs_1_, bf16[768,2560]{1,0:T(8,128)(2,1)} %get-tuple-element.150.refs_2_, ...), custom_call_target="tpu_custom_call" | custom-call | flops 3200000000 | tf_op jit(solution)/shard_map/weight_grads/pallas_call | solution.py:175
  448.8 5.1 %add_row_sums.1 = (bf16[1,1,192,2560]{3,2,1,0:T(8,128)(2,1)}, bf16[1,1,192,2560]{3,2,1,0:T(8,128)(2,1)}, f32[8,128]{1,0:T(8,128)}) custom-call(f32[2,192,2560]{2,1,0:T(8,128)} %get-tuple-element.113.refs_0_, bf16[1,1,192,2560]{3,2,1,0:T(8,128)(2,1)} %refs_1_.5, bf16[1,1,192,2560]{3,2,1,0:T(8,128)(2,1)} %refs_2_.15, bf16[2,96,2560]{2,1,0:T(8,128)(2,1)} %copy-done.2, ...), custom_call_target="tpu_custom_call" | custom-call | flops 500000000 | tf_op jit(solution)/shard_map/add_row_sums/pallas_call | solution.py:175
  (79 shorter events, 45.1 us)
Async XLA Ops:
  0.6 42.5 %collective-permute-start.2 = (bf16[1,1,192,2560]{3,2,1,0:T(8,128)(2,1)}, bf16[1,1,192,2560]{3,2,1,0:T(8,128)(2,1)S(1)}, u32[]{:S(2)}, u32[]{:S(2)}) collective-permute-start(bf16[1,1,192,2560]{3,2,1,0:T(8,128)(2,1)} %refs_1_.5), channel_id=1, source_target_pairs={{0,2},{2,0},{4,6},{6,4},{8,10},{10,8},{12,14},{14,12},{1,3},{3,1},... | collective-permute-start | bytes 2949128 | tf_op jit(solution)/shard_map/ppermute | solution.py:24
  3.7 43.1 %collective-permute-start.3 = (bf16[1,1,192,2560]{3,2,1,0:T(8,128)(2,1)}, bf16[1,1,192,2560]{3,2,1,0:T(8,128)(2,1)}, u32[]{:S(2)}, u32[]{:S(2)}) collective-permute-start(bf16[1,1,192,2560]{3,2,1,0:T(8,128)(2,1)} %refs_2_.15), channel_id=1, source_target_pairs={{0,2},{2,0},{4,6},{6,4},{8,10},{10,8},{12,14},{14,12},{1,3},{3,1},... | collective-permute-start | bytes 2949128 | tf_op jit(solution)/shard_map/ppermute | solution.py:24
  3.7 89.6 %collective-permute-start.1 = (bf16[1,1,192,2560]{3,2,1,0:T(8,128)(2,1)}, bf16[1,1,192,2560]{3,2,1,0:T(8,128)(2,1)}, u32[]{:S(2)}, u32[]{:S(2)}) collective-permute-start(bf16[1,1,192,2560]{3,2,1,0:T(8,128)(2,1)} %refs_1_.5), channel_id=1, source_target_pairs={{0,4},{4,0},{2,6},{6,2},{8,12},{12,8},{10,14},{14,10},{1,5},{5,1},... | collective-permute-start | bytes 2949128 | tf_op jit(solution)/shard_map/ppermute | solution.py:24
  5.7 88.2 %collective-permute-start.4 = (bf16[1,1,192,2560]{3,2,1,0:T(8,128)(2,1)}, bf16[1,1,192,2560]{3,2,1,0:T(8,128)(2,1)}, u32[]{:S(2)}, u32[]{:S(2)}) collective-permute-start(bf16[1,1,192,2560]{3,2,1,0:T(8,128)(2,1)} %refs_2_.15), channel_id=1, source_target_pairs={{0,4},{4,0},{2,6},{6,2},{8,12},{12,8},{10,14},{14,10},{1,5},{5,1},... | collective-permute-start | bytes 2949128 | tf_op jit(solution)/shard_map/ppermute | solution.py:24
  15.7 58.9 %collective-permute-start = (bf16[3,192,768]{2,1,0:T(8,128)(2,1)}, bf16[3,192,768]{2,1,0:T(8,128)(2,1)S(1)}, u32[]{:S(2)}, u32[]{:S(2)}) collective-permute-start(bf16[3,192,768]{2,1,0:T(8,128)(2,1)} %get-tuple-element.87), channel_id=1, source_target_pairs={{0,8},{8,0},{2,10},{10,2},{4,12},{12,4},{6,14},{14,6},{1,9},{9,1},... | collective-permute-start | bytes 2654216 | tf_op jit(solution)/shard_map/ppermute | solution.py:24
  43.2 3.6 copy-start.4
  66.2 140.1 %collective-permute-start.6 = (bf16[3,192,1792]{2,1,0:T(8,128)(2,1)}, bf16[3,192,1792]{2,1,0:T(8,128)(2,1)}, u32[]{:S(2)}, u32[]{:S(2)}) collective-permute-start(bf16[3,192,1792]{2,1,0:T(8,128)(2,1)} %get-tuple-element.104), channel_id=1, source_target_pairs={{0,8},{8,0},{2,10},{10,2},{4,12},{12,4},{6,14},{14,6},{1,9},{9,1},... | collective-permute-start | bytes 6193160 | tf_op jit(solution)/shard_map/ppermute | solution.py:24
  69.1 9.8 %all-to-all-start.1 = ((bf16[2,2,192,2560]{3,2,1,0:T(8,128)(2,1)}), bf16[2,2,192,2560]{3,2,1,0:T(8,128)(2,1)}, u32[]{:S(2)}, u32[]{:S(2)}) async-start(bf16[2,2,192,2560]{3,2,1,0:T(8,128)(2,1)} %get-tuple-element.92), calls=%async_computation.1 | async-start | bytes 7864320 | tf_op jit(solution)/shard_map/all_to_all | solution.py:498
  74.7 4.3 copy-start.5
  89.6 6.3 %all-to-all-start.2 = ((bf16[2,3,192,768]{3,2,1,0:T(8,128)(2,1)}), bf16[2,3,192,768]{3,2,1,0:T(8,128)(2,1)S(1)}, u32[]{:S(2)}, u32[]{:S(2)}) async-start(bf16[2,3,192,768]{3,2,1,0:T(8,128)(2,1)} %get-tuple-element.96), calls=%async_computation.2 | async-start | bytes 3538944 | tf_op jit(solution)/shard_map/all_to_all | solution.py:498
  96.0 1.2 copy-start
  97.8 43.9 %collective-permute-start.8 = (bf16[1,1,192,2560]{3,2,1,0:T(8,128)(2,1)}, bf16[1,1,192,2560]{3,2,1,0:T(8,128)(2,1)S(1)}, u32[]{:S(2)}, u32[]{:S(2)}) collective-permute-start(bf16[1,1,192,2560]{3,2,1,0:T(8,128)(2,1)} %get-tuple-element.97.refs_2_), channel_id=1, source_target_pairs={{0,2},{2,0},{4,6},{6,4},{8,10},{10,8},{12,14},{14,12},{1,3},{3,1},... | collective-permute-start | bytes 2949128 | tf_op jit(solution)/shard_map/ppermute | solution.py:24
  99.3 43.5 %collective-permute-start.7 = (bf16[1,1,192,2560]{3,2,1,0:T(8,128)(2,1)}, bf16[1,1,192,2560]{3,2,1,0:T(8,128)(2,1)S(1)}, u32[]{:S(2)}, u32[]{:S(2)}) collective-permute-start(bf16[1,1,192,2560]{3,2,1,0:T(8,128)(2,1)} %get-tuple-element.94.refs_0_.refs_1_), channel_id=1, source_target_pairs={{0,2},{2,0},{4,6},{6,4},{8,10},{10,8},{12,14},{14,12},{1,3},{3,1},... | collective-permute-start | bytes 2949128 | tf_op jit(solution)/shard_map/ppermute | solution.py:24
  131.5 122.2 %collective-permute-start.5 = (bf16[3,192,1024]{2,1,0:T(8,128)(2,1)}, bf16[3,192,1024]{2,1,0:T(8,128)(2,1)}, u32[]{:S(2)}, u32[]{:S(2)}) collective-permute-start(bf16[3,192,1024]{2,1,0:T(8,128)(2,1)} %get-tuple-element.101), channel_id=1, source_target_pairs={{0,8},{8,0},{2,10},{10,2},{4,12},{12,4},{6,14},{14,6},{1,9},{9,1},... | collective-permute-start | bytes 3538952 | tf_op jit(solution)/shard_map/ppermute | solution.py:24
  163.2 9.8 %all-to-all-start.4 = ((bf16[2,2,192,2560]{3,2,1,0:T(8,128)(2,1)}), bf16[2,2,192,2560]{3,2,1,0:T(8,128)(2,1)}, u32[]{:S(2)}, u32[]{:S(2)}) async-start(bf16[2,2,192,2560]{3,2,1,0:T(8,128)(2,1)} %get-tuple-element.108), calls=%async_computation.4 | async-start | bytes 7864320 | tf_op jit(solution)/shard_map/all_to_all | solution.py:498
  169.0 106.8 %collective-permute-start.11 = (bf16[3,96,1792]{2,1,0:T(8,128)(2,1)}, bf16[3,96,1792]{2,1,0:T(8,128)(2,1)S(1)}, u32[]{:S(2)}, u32[]{:S(2)}) collective-permute-start(bf16[3,96,1792]{2,1,0:T(8,128)(2,1)} %get-tuple-element.118), channel_id=1, source_target_pairs={{0,8},{8,0},{2,10},{10,2},{4,12},{12,4},{6,14},{14,6},{1,9},{9,1},... | collective-permute-start | bytes 3096584 | tf_op jit(solution)/shard_map/ppermute | solution.py:24
  206.9 113.2 %collective-permute-start.13 = (bf16[3,96,1792]{2,1,0:T(8,128)(2,1)}, bf16[3,96,1792]{2,1,0:T(8,128)(2,1)}, u32[]{:S(2)}, u32[]{:S(2)}) collective-permute-start(bf16[3,96,1792]{2,1,0:T(8,128)(2,1)} %get-tuple-element.123), channel_id=1, source_target_pairs={{0,8},{8,0},{2,10},{10,2},{4,12},{12,4},{6,14},{14,6},{1,9},{9,1},... | collective-permute-start | bytes 3096584 | tf_op jit(solution)/shard_map/ppermute | solution.py:24
  225.7 95.0 %collective-permute-start.9 = (bf16[2,96,2560]{2,1,0:T(8,128)(2,1)}, bf16[2,96,2560]{2,1,0:T(8,128)(2,1)S(1)}, u32[]{:S(2)}, u32[]{:S(2)}) collective-permute-start(bf16[2,96,2560]{2,1,0:T(8,128)(2,1)} %get-tuple-element.114), channel_id=1, source_target_pairs={{0,2},{2,0},{4,6},{6,4},{8,10},{10,8},{12,14},{14,12},{1,3},{3,1},... | collective-permute-start | bytes 2949128 | tf_op jit(solution)/shard_map/ppermute | solution.py:24
  227.3 93.4 %collective-permute-start.10 = (bf16[2,96,2560]{2,1,0:T(8,128)(2,1)}, bf16[2,96,2560]{2,1,0:T(8,128)(2,1)}, u32[]{:S(2)}, u32[]{:S(2)}) collective-permute-start(bf16[2,96,2560]{2,1,0:T(8,128)(2,1)} %get-tuple-element.115), channel_id=1, source_target_pairs={{0,2},{2,0},{4,6},{6,4},{8,10},{10,8},{12,14},{14,12},{1,3},{3,1},... | collective-permute-start | bytes 2949128 | tf_op jit(solution)/shard_map/ppermute | solution.py:24
  268.1 9.2 %all-to-all-start.6 = ((bf16[2,3,192,1024]{3,2,1,0:T(8,128)(2,1)}), bf16[2,3,192,1024]{3,2,1,0:T(8,128)(2,1)}, u32[]{:S(2)}, u32[]{:S(2)}) async-start(bf16[2,3,192,1024]{3,2,1,0:T(8,128)(2,1)} %get-tuple-element.128), calls=%async_computation.6 | async-start | bytes 4718592 | tf_op jit(solution)/shard_map/all_to_all | solution.py:498
  277.3 90.3 %collective-permute-start.12 = (bf16[3,96,1792]{2,1,0:T(8,128)(2,1)}, bf16[3,96,1792]{2,1,0:T(8,128)(2,1)S(1)}, u32[]{:S(2)}, u32[]{:S(2)}) collective-permute-start(bf16[3,96,1792]{2,1,0:T(8,128)(2,1)} %get-tuple-element.120), channel_id=1, source_target_pairs={{0,8},{8,0},{2,10},{10,2},{4,12},{12,4},{6,14},{14,6},{1,9},{9,1},... | collective-permute-start | bytes 3096584 | tf_op jit(solution)/shard_map/ppermute | solution.py:24
  340.5 27.1 %collective-permute-start.14 = (bf16[2,96,2560]{2,1,0:T(8,128)(2,1)}, bf16[2,96,2560]{2,1,0:T(8,128)(2,1)S(1)}, u32[]{:S(2)}, u32[]{:S(2)}) collective-permute-start(bf16[2,96,2560]{2,1,0:T(8,128)(2,1)} %get-tuple-element.132), channel_id=1, source_target_pairs={{0,2},{2,0},{4,6},{6,4},{8,10},{10,8},{12,14},{14,12},{1,3},{3,1},... | collective-permute-start | bytes 2949128 | tf_op jit(solution)/shard_map/ppermute | solution.py:24
  342.1 24.4 %all-to-all-start.7 = ((bf16[2,3,192,1792]{3,2,1,0:T(8,128)(2,1)}), bf16[2,3,192,1792]{3,2,1,0:T(8,128)(2,1)}, u32[]{:S(2)}, u32[]{:S(2)}) async-start(bf16[2,3,192,1792]{3,2,1,0:T(8,128)(2,1)} %get-tuple-element.139), calls=%async_computation.7 | async-start | bytes 8257536 | tf_op jit(solution)/shard_map/all_to_all | solution.py:498
  348.0 48.2 %collective-permute-start.16 = (bf16[3,96,1792]{2,1,0:T(8,128)(2,1)}, bf16[3,96,1792]{2,1,0:T(8,128)(2,1)}, u32[]{:S(2)}, u32[]{:S(2)}) collective-permute-start(bf16[3,96,1792]{2,1,0:T(8,128)(2,1)} %get-tuple-element.143), channel_id=1, source_target_pairs={{0,8},{8,0},{2,10},{10,2},{4,12},{12,4},{6,14},{14,6},{1,9},{9,1},... | collective-permute-start | bytes 3096584 | tf_op jit(solution)/shard_map/ppermute | solution.py:24
  367.1 24.2 %collective-permute-start.17 = (bf16[2,96,2560]{2,1,0:T(8,128)(2,1)}, bf16[2,96,2560]{2,1,0:T(8,128)(2,1)}, u32[]{:S(2)}, u32[]{:S(2)}) collective-permute-start(bf16[2,96,2560]{2,1,0:T(8,128)(2,1)} %get-tuple-element.144), channel_id=1, source_target_pairs={{0,2},{2,0},{4,6},{6,4},{8,10},{10,8},{12,14},{14,12},{1,3},{3,1},... | collective-permute-start | bytes 2949128 | tf_op jit(solution)/shard_map/ppermute | solution.py:24
  367.6 1.3 copy-start.13
  385.7 10.5 %collective-permute-start.18 = (bf16[1,3,48,1792]{3,2,1,0:T(8,128)(2,1)}, bf16[1,3,48,1792]{3,2,1,0:T(8,128)(2,1)S(1)}, u32[]{:S(2)}, u32[]{:S(2)}) collective-permute-start(bf16[1,3,48,1792]{3,2,1,0:T(8,128)(2,1)} %get-tuple-element.146.refs_4_), channel_id=1, source_target_pairs={{0,1},{1,0},{2,3},{3,2},{4,5},{5,4},{6,7},{7,6},{8,9},{9,8},{10,11... | collective-permute-start | bytes 1548296 | tf_op jit(solution)/shard_map/ppermute | solution.py:24
  385.8 10.5 %collective-permute-start.19 = (bf16[1,3,48,1792]{3,2,1,0:T(8,128)(2,1)}, bf16[1,3,48,1792]{3,2,1,0:T(8,128)(2,1)S(1)}, u32[]{:S(2)}, u32[]{:S(2)}) collective-permute-start(bf16[1,3,48,1792]{3,2,1,0:T(8,128)(2,1)} %get-tuple-element.147.refs_6_), channel_id=1, source_target_pairs={{0,1},{1,0},{2,3},{3,2},{4,5},{5,4},{6,7},{7,6},{8,9},{9,8},{10,11... | collective-permute-start | bytes 1548296 | tf_op jit(solution)/shard_map/ppermute | solution.py:24
  386.3 61.6 %collective-permute-start.15 = (bf16[2,96,2560]{2,1,0:T(8,128)(2,1)}, bf16[2,96,2560]{2,1,0:T(8,128)(2,1)}, u32[]{:S(2)}, u32[]{:S(2)}) collective-permute-start(bf16[2,96,2560]{2,1,0:T(8,128)(2,1)} %get-tuple-element.141), channel_id=1, source_target_pairs={{0,4},{4,0},{2,6},{6,2},{8,12},{12,8},{10,14},{14,10},{1,5},{5,1},... | collective-permute-start | bytes 2949128 | tf_op jit(solution)/shard_map/ppermute | solution.py:24
  414.0 33.9 %collective-permute-start.20 = (bf16[2,96,2560]{2,1,0:T(8,128)(2,1)}, bf16[2,96,2560]{2,1,0:T(8,128)(2,1)S(1)}, u32[]{:S(2)}, u32[]{:S(2)}) collective-permute-start(bf16[2,96,2560]{2,1,0:T(8,128)(2,1)} %get-tuple-element.148), channel_id=1, source_target_pairs={{0,4},{4,0},{2,6},{6,2},{8,12},{12,8},{10,14},{14,10},{1,5},{5,1},... | collective-permute-start | bytes 2949128 | tf_op jit(solution)/shard_map/ppermute | solution.py:24
  414.1 2.2 collective-permute-start.21
  414.1 2.8 collective-permute-start.22
  (10 other events, 9.3 us)

commit v3 on v2

--- a/solution.py
+++ b/solution.py
@@ -10,7 +10,7 @@
 
 VMEM_BYTES = 62 * 1024 * 1024
 TILE = 256
-COST_SCALE = 0.1e9
+COST_SCALE = 0.08e9
 G, U, PRE = 0, 1, 2
 
 
@@ -251,7 +251,7 @@
     return pairs, results[-1]
 
 
-def hidden_and_back(order, tiles, parts, weights, out_type, addend=None, cuts=1, twice=True):
+def hidden_and_back(order, tiles, parts, weights, out_type, addend=(), cuts=None, twice=True):
     first, count = tiles
     copies, hqr_cuts = (2, 1) if twice else (1, 2)
     sizes = [kept.shape[1] for kept, _ in parts]
@@ -264,8 +264,8 @@
     n = len(inputs)
     size = rows // hqr_cuts
     inputs += weight_specs(weights, (G, U, PRE), first)
-    if addend is not None:
-        inputs.append((addend, pl.BlockSpec(addend.shape, lambda j: (0, 0, 0))))
+    inputs += [(array, pl.BlockSpec(array.shape, lambda j: (0, 0, 0))) for array in addend]
+    cuts = cuts or [rows]
 
     def body(ins, outs, scratch):
         wg_ref, wu_ref, wd_ref = ins[n : n + 3]
@@ -296,12 +296,14 @@
 
         @pl.when(j == count - 1)
         def _():
-            total = acc_ref[...]
-            if addend is not None:
-                total = total + ins[n + 3][...].astype(jnp.float32)
-            step = rows // cuts
-            for cut, ref in enumerate(outs[hqr_cuts:]):
-                ref[...] = total[:, cut * step : (cut + 1) * step].astype(out_type)
+            at = 0
+            for ref in ins[n + 3 :]:
+                acc_ref[:, at : at + ref.shape[1]] += ref[...].astype(jnp.float32)
+                at += ref.shape[1]
+            at = 0
+            for ref in outs[hqr_cuts:]:
+                ref[...] = acc_ref[:, at : at + ref.shape[1]].astype(out_type)
+                at += ref.shape[1]
 
     outputs = [
         (
@@ -309,9 +311,10 @@
             pl.BlockSpec((copies, 3, size, TILE), lambda j: (0, 0, 0, j)),
         )
     ] * hqr_cuts
-    shape = (2, rows // cuts, depth)
-    sums_spec = pl.BlockSpec(shape, lambda j: (0, 0, 0))
-    outputs += [(jax.ShapeDtypeStruct(shape, out_type), sums_spec)] * cuts
+    for cut in cuts:
+        shape = (2, cut, depth)
+        spec = pl.BlockSpec(shape, lambda j: (0, 0, 0))
+        outputs.append((jax.ShapeDtypeStruct(shape, out_type), spec))
     scratch = [pltpu.VMEM((2, rows, depth), jnp.float32)]
     return order.call(body, "hidden_and_back", 3 + 2.2 * count, count, inputs, outputs, scratch)
 
@@ -497,9 +500,8 @@
     def both_replicas(pair):
         return lax.all_to_all(pair, "dp", 0, 0, tiled=True)
 
-    def finish(name, tiles, parts=None, addend=None, calls=99):
+    def finish(name, tiles, parts=None, addend=(), calls=99, cuts=None):
         parts = [(own[key], got[key]) for key in parts or [name]]
-        cuts = parts[0][0].shape[1] * len(parts) // half if tiles == every else 1
         out_type = jnp.bfloat16 if tiles == every else jnp.float32
         twice = name not in ("fa", "fb")
         found, *rest = hidden_and_back(
@@ -547,19 +549,19 @@
     send("ba")
     late = collect("both", "far")
     send("bb", ["near"])
-    finish("near", every)
-    near_sums = [pass_on(array, near, 4) for array in sums["near"]]
-    finish("c1", chunks["c1"], addend=sums["c0"][0])
-    send("fa", ["ba"])
+    finish("near", every, calls=0, cuts=[half] * 2)
+    near_sums = [pass_on(array, near, 3) for array in sums["near"]]
+    early_pieces = pieces_of([["near"]], [["c0"]])
+    first = weight_grads(order, side, chunks["c0"], early, early_pieces, width)
+    finish("c1", chunks["c1"], addend=sums["c0"], calls=0)
     early_pieces = pieces_of([["near"]], [["c0", "c1"]])
-    mid = n_tiles // 2
-    first = weight_grads(order, side, (0, mid), early, early_pieces, width)
+    send("fa", ["ba", "bb"])
+    finish("both", every, parts=["ba", "bb"], calls=3, cuts=[half // 2] * 2 + [half])
     send("fb", ["bb"])
-    finish("both", every, parts=["ba", "bb"], calls=1)
-    both_sums = [pass_on(sums["both"][0], near, 99)]
-    rest = (mid, n_tiles - mid)
-    first = weight_grads(order, side, rest, early, early_pieces, width, into=first)
-    both_sums.append(pass_on(order.hold(sums["both"][1], []), near, 99))
+    *leading, trailing = sums["both"]
+    both_sums = [[pass_on(array, near, 99) for array in leading]]
+    first = weight_grads(order, side, chunks["c1"], early, early_pieces, width, into=first)
+    both_sums.append([pass_on(order.hold(trailing, []), near, 99)])
     far_sums = []
     for name, addend in zip(("fa", "fb"), both_sums):
         finish(name, every, addend=addend, calls=0)

time: 456 us -> 450 us (0.987)
  waiting for transfers between devices: 90.2 us -> 77.4 us
  blocking collectives: 34.9 us -> 46.6 us
  starting transfers between devices: 49.4 us -> 44.7 us
    ppermute x23 -> x24, waiting for transfers between devices: 81.8 us -> 67.7 us  [from_partner(): return lax.ppermute(block, axis, route)]
    all_to_all x3 -> x4, blocking collectives: 34.9 us -> 46.6 us  [both_replicas(): return lax.all_to_all(pair, 'dp', 0, 0, tiled=True)]
    all_to_all x5 -> x4, starting transfers between devices: 25.8 us -> 19.7 us  [both_replicas(): return lax.all_to_all(pair, 'dp', 0, 0, tiled=True)]
    ppermute x23 -> x24, starting transfers between devices: 23.6 us -> 25 us  [from_partner(): return lax.ppermute(block, axis, route)]
    all_to_all x5 -> x4, waiting for transfers between devices: 8.34 us -> 9.64 us  [both_replicas(): return lax.all_to_all(pair, 'dp', 0, 0, tiled=True)]
  transfers between devices with their start and end apart: 28 -> 28, of which waited for: 13 -> 14; matrix products, arithmetic and copies ran while one was open for 0% -> 0% of each run, Pallas kernels for 58% -> 59%
where the time goes in v3:
time: 450 us; the launch traced here: 448 us
  Pallas kernels  271 us (60%)
  waiting for transfers between devices  77.4 us (17%)
  blocking collectives  46.6 us (10%)
  starting transfers between devices  44.7 us (10%)
  local copies, waits for them, and re-layouts  7.64 us (2%)
    pallas_call x24, Pallas kernels, call(): pl.pallas_call(kernel, name=name, grid=(steps,), in_specs=[spec for _, sp...  271 us
    ppermute x24, waiting for transfers between devices, from_partner(): return lax.ppermute(block, axis, route)  67.7 us
    all_to_all x4, blocking collectives, both_replicas(): return lax.all_to_all(pair, 'dp', 0, 0, tiled=True)  46.6 us
    ppermute x24, starting transfers between devices, from_partner(): return lax.ppermute(block, axis, route)  25 us
    all_to_all x4, starting transfers between devices, both_replicas(): return lax.all_to_all(pair, 'dp', 0, 0, tiled=True)  19.7 us
    all_to_all x4, waiting for transfers between devices, both_replicas(): return lax.all_to_all(pair, 'dp', 0, 0, tiled=True)  9.64 us
  transfers between devices with their start and end apart: 28, of which 14 were waited for; matrix products, arithmetic and copies ran while one was open for 0% of the time, Pallas kernels for 59%

profile of v3, /device:TPU:0, one launch (start us, length us, event | category | flops | bytes accessed | tf_op | source)
XLA Modules:
  0.0 448.2 jit_solution(1223401488009597873)
XLA Ops:
  0.6 3.0 collective-permute-start.2
  5.8 10.1 %partials.5 = (f32[3,192,768]{2,1,0:T(8,128)}, bf16[3,192,768]{2,1,0:T(8,128)(2,1)}, f32[8,128]{1,0:T(8,128)}) custom-call(bf16[1,1,192,2560]{3,2,1,0:T(8,128)(2,1)} %refs_1_.5, bf16[1,1,192,2560]{3,2,1,0:T(8,128)(2,1)} %refs_1_.5, bf16[1,1,192,2560]{3,2,1,0:T(8,128)(2,1)} %refs_2_.15, bf16[1,2560,1792]{2,1,0:T(8,128)(2,1)} %refs_2_.14, ...), custom_call_target="tpu_custom_call" | custom-call | flops 816000000 | tf_op jit(solution)/shard_map/partials/pallas_call | solution.py:175
  15.8 3.0 collective-permute-start
  18.9 13.0 %partials.6 = (f32[3,192,1024]{2,1,0:T(8,128)}, bf16[3,192,1024]{2,1,0:T(8,128)(2,1)}, bf16[2,2,192,2560]{3,2,1,0:T(8,128)(2,1)}, f32[8,128]{1,0:T(8,128)}) custom-call(bf16[1,1,192,2560]{3,2,1,0:T(8,128)(2,1)} %refs_1_.5, bf16[1,1,192,2560]{3,2,1,0:T(8,128)(2,1)} %refs_1_.5, bf16[1,1,192,2560]{3,2,1,0:T(8,128)(2,1)} %refs_2_.15, ...), custom_call_target="tpu_custom_call" | custom-call | flops 1008000000 | tf_op jit(solution)/shard_map/partials/pallas_call | solution.py:175
  31.9 11.6 %all_to_all.40.refs_7_.refs_2_.refs_3_ = bf16[2,2,192,2560]{3,2,1,0:T(8,128)(2,1)} all-to-all(bf16[2,2,192,2560]{3,2,1,0:T(8,128)(2,1)} %get-tuple-element.91), channel_id=1, replica_groups=mesh['groups'=2,'grid'=8,'dp'=2] {'dp'}, dimensions={0} | all-to-all | bytes 7864320 | tf_op jit(solution)/shard_map/all_to_all | solution.py:501
  43.4 3.4 collective-permute-done.3.refs_2_
  46.8 19.5 %partials.7 = (f32[3,192,1792]{2,1,0:T(8,128)}, bf16[3,192,1792]{2,1,0:T(8,128)(2,1)}, bf16[2,2,192,2560]{3,2,1,0:T(8,128)(2,1)}, f32[8,128]{1,0:T(8,128)}) custom-call(bf16[1,1,192,2560]{3,2,1,0:T(8,128)(2,1)} %copy-done.4, bf16[1,1,192,2560]{3,2,1,0:T(8,128)(2,1)} %copy-done.4, bf16[1,1,192,2560]{3,2,1,0:T(8,128)(2,1)} %collective-permute-done.3.refs_2_, ...), custom_call_target="tpu_custom_call" | custom-call | flops 1584000000 | tf_op jit(solution)/shard_map/partials/pallas_call | solution.py:175
  69.2 5.5 %all-to-all-start.1 = ((bf16[2,2,192,2560]{3,2,1,0:T(8,128)(2,1)}), bf16[2,2,192,2560]{3,2,1,0:T(8,128)(2,1)}, u32[]{:S(2)}, u32[]{:S(2)}) async-start(bf16[2,2,192,2560]{3,2,1,0:T(8,128)(2,1)} %get-tuple-element.93), calls=%async_computation.1 | async-start | bytes 7864320 | tf_op jit(solution)/shard_map/all_to_all | solution.py:501
  74.8 4.3 all-to-all-done.1.refs_6_.refs_0_.refs_1_
  79.1 10.7 %hidden_and_back.6 = (bf16[2,3,192,768]{3,2,1,0:T(8,128)(2,1)}, f32[2,192,2560]{2,1,0:T(8,128)}, f32[8,128]{1,0:T(8,128)}) custom-call(f32[3,192,768]{2,1,0:T(8,128)} %get-tuple-element.89.refs_0_, bf16[3,192,768]{2,1,0:T(8,128)(2,1)} %copy-done.5, bf16[1,2560,1792]{2,1,0:T(8,128)(2,1)} %refs_2_.14, bf16[1,2560,1792]{2,1,0:T(8,128)(2,1)} %refs_3_.19, ...), custom_call_target="tpu_custom_call" | custom-call | flops 768000000 | tf_op jit(solution)/shard_map/hidden_and_back/pallas_call | solution.py:175
  89.8 3.7 all-to-all-start.2
  100.0 19.5 %partials.8 = (f32[3,96,1792]{2,1,0:T(8,128)}, bf16[3,96,1792]{2,1,0:T(8,128)(2,1)}, f32[3,96,1792]{2,1,0:T(8,128)}, bf16[3,96,1792]{2,1,0:T(8,128)(2,1)}, bf16[...) custom-call(bf16[1,1,192,2560]{3,2,1,0:T(8,128)(2,1)} %get-tuple-element.95.refs_0_.refs_1_, ...), custom_call_target="tpu_custom_call" | custom-call | flops 1584000000 | tf_op jit(solution)/shard_map/partials/pallas_call | solution.py:175
  119.5 11.6 %all_to_all.41.refs_3_.refs_2_ = bf16[2,2,192,2560]{3,2,1,0:T(8,128)(2,1)} all-to-all(bf16[2,2,192,2560]{3,2,1,0:T(8,128)(2,1)} %get-tuple-element.101), channel_id=1, replica_groups=mesh['groups'=2,'grid'=8,'dp'=2] {'dp'}, dimensions={0} | all-to-all | bytes 7864320 | tf_op jit(solution)/shard_map/all_to_all | solution.py:501
  131.7 10.0 %assemble.2 = (bf16[2560,768]{1,0:T(8,128)(2,1)}, bf16[768,2560]{1,0:T(8,128)(2,1)}, f32[8,128]{1,0:T(8,128)}) custom-call(bf16[2,2,192,2560]{3,2,1,0:T(8,128)(2,1)} %all-to-all-done.1.refs_6_.refs_0_.refs_1_, bf16[2,2,192,2560]{3,2,1,0:T(8,128)(2,1)} %all-to-all-done.1.refs_6_.refs_0_.refs_1_, bf16[2,2,192,2560]{3,2,1,0:T(8,128)(2,1)} %all_to_all.40.refs_7_.refs_2_.refs_3_, ...), custom_call_target="tpu_custom_call" | custom-call | flops 800000000 | tf_op jit(solution)/shard_map/assemble/pallas_call | solution.py:175
  143.9 19.6 %partials.9 = (f32[3,96,1792]{2,1,0:T(8,128)}, bf16[3,96,1792]{2,1,0:T(8,128)(2,1)}, f32[3,96,1792]{2,1,0:T(8,128)}, bf16[3,96,1792]{2,1,0:T(8,128)(2,1)}, bf16[...) custom-call(bf16[1,1,192,2560]{3,2,1,0:T(8,128)(2,1)} %copy-done.3, bf16[1,1,192,2560]{3,2,1,0:T(8,128)(2,1)} %copy-done.3, ...), custom_call_target="tpu_custom_call" | custom-call | flops 1584000000 | tf_op jit(solution)/shard_map/partials/pallas_call | solution.py:175
  163.5 5.5 %all-to-all-start.4 = ((bf16[2,2,192,2560]{3,2,1,0:T(8,128)(2,1)}), bf16[2,2,192,2560]{3,2,1,0:T(8,128)(2,1)}, u32[]{:S(2)}, u32[]{:S(2)}) async-start(bf16[2,2,192,2560]{3,2,1,0:T(8,128)(2,1)} %get-tuple-element.111), calls=%async_computation.4 | async-start | bytes 7864320 | tf_op jit(solution)/shard_map/all_to_all | solution.py:501
  173.4 10.0 %assemble.3 = (bf16[2560,768]{1,0:T(8,128)(2,1)}, bf16[768,2560]{1,0:T(8,128)(2,1)}, f32[8,128]{1,0:T(8,128)}) custom-call(bf16[2,2,192,2560]{3,2,1,0:T(8,128)(2,1)} %all-to-all-done.4.refs_0_.refs_1_.refs_5_, bf16[2,2,192,2560]{3,2,1,0:T(8,128)(2,1)} %all-to-all-done.4.refs_0_.refs_1_.refs_5_, bf16[2,2,192,2560]{3,2,1,0:T(8,128)(2,1)} %all_to_all.41.refs_3_.refs_2_, ...), custom_call_target="tpu_custom_call" | custom-call | flops 800000000 | tf_op jit(solution)/shard_map/assemble/pallas_call | solution.py:175
  183.3 23.1 %collective-permute-done.6.refs_1_ = bf16[3,192,1792]{2,1,0:T(8,128)(2,1)} collective-permute-done((bf16[3,192,1792]{2,1,0:T(8,128)(2,1)}, bf16[3,192,1792]{2,1,0:T(8,128)(2,1)}, u32[]{:S(2)}, u32[]{:S(2)}) %collective-permute-start.6) | collective-permute-done | bytes 2064416 | tf_op jit(solution)/shard_map/ppermute | solution.py:24
  207.1 18.7 %hidden_and_back.7 = (bf16[2,3,192,1792]{3,2,1,0:T(8,128)(2,1)}, bf16[2,96,2560]{2,1,0:T(8,128)(2,1)}, bf16[2,96,2560]{2,1,0:T(8,128)(2,1)}, f32[8,128]{1,0:T(8,128)}) custom-call(f32[3,192,1792]{2,1,0:T(8,128)} %get-tuple-element.107.refs_0_, bf16[3,192,1792]{2,1,0:T(8,128)(2,1)} %collective-permute-done.6.refs_1_, bf16[1,2560,1792]{2,1,0:T(8,128)(2,1)} %refs_2_.14, ...), custom_call_target="tpu_custom_call" | custom-call | flops 1472000000 | tf_op jit(solution)/shard_map/hidden_and_back/pallas_call | solution.py:175
  227.9 11.8 %all_to_all.42.refs_3_.refs_6_ = bf16[2,3,192,1792]{3,2,1,0:T(8,128)(2,1)} all-to-all(bf16[2,3,192,1792]{3,2,1,0:T(8,128)(2,1)} %get-tuple-element.115), channel_id=1, replica_groups=mesh['groups'=2,'grid'=8,'dp'=2] {'dp'}, dimensions={0} | all-to-all | bytes 8257536 | tf_op jit(solution)/shard_map/all_to_all | solution.py:501
  239.6 14.6 %weight_grads.3 = (bf16[1,2560,1792]{2,1,0:T(8,128)(2,1)}, bf16[1,2560,1792]{2,1,0:T(8,128)(2,1)}, bf16[1,1792,2560]{2,1,0:T(8,128)(2,1)}, f32[8,128]{1,0:T(8,128)}) custom-call(s32[1]{0:T(128)} %bitcast.refs_0_, bf16[2560,768]{1,0:T(8,128)(2,1)} %get-tuple-element.105.refs_1_, bf16[768,2560]{1,0:T(8,128)(2,1)} %get-tuple-element.106.refs_2_, ...), custom_call_target="tpu_custom_call" | custom-call | flops 1280000000 | tf_op jit(solution)/shard_map/weight_grads/pallas_call | solution.py:175
  254.2 14.7 %hidden_and_back.8 = (bf16[2,3,192,1024]{3,2,1,0:T(8,128)(2,1)}, f32[2,192,2560]{2,1,0:T(8,128)}, f32[8,128]{1,0:T(8,128)}) custom-call(f32[3,192,1024]{2,1,0:T(8,128)} %get-tuple-element.86.refs_0_, bf16[3,192,1024]{2,1,0:T(8,128)(2,1)} %collective-permute-done.5.refs_1_, bf16[1,2560,1792]{2,1,0:T(8,128)(2,1)} %refs_2_.14, bf16[1,2560,1792]{2,1,0:T(8,128)(2,1)} %refs_3_.19, ...), custom_call_target="tpu_custom_call" | custom-call | flops 944000000 | tf_op jit(solution)/shard_map/hidden_and_back/pallas_call | solution.py:175
  268.9 4.9 %all-to-all-start.6 = ((bf16[2,3,192,1024]{3,2,1,0:T(8,128)(2,1)}), bf16[2,3,192,1024]{3,2,1,0:T(8,128)(2,1)}, u32[]{:S(2)}, u32[]{:S(2)}) async-start(bf16[2,3,192,1024]{3,2,1,0:T(8,128)(2,1)} %get-tuple-element.126), calls=%async_computation.6 | async-start | bytes 4718592 | tf_op jit(solution)/shard_map/all_to_all | solution.py:501
  277.0 19.9 %collective-permute-done.12.refs_2_.refs_3_.refs_1_ = bf16[3,96,1792]{2,1,0:T(8,128)(2,1)S(1)} collective-permute-done((bf16[3,96,1792]{2,1,0:T(8,128)(2,1)}, bf16[3,96,1792]{2,1,0:T(8,128)(2,1)S(1)}, u32[]{:S(2)}, u32[]{:S(2)}) %collective-permute-start.12) | collective-permute-done | bytes 1032224 | tf_op jit(solution)/shard_map/ppermute | solution.py:24
  299.5 18.8 %hidden_and_back.9 = (bf16[2,3,192,1792]{3,2,1,0:T(8,128)(2,1)}, bf16[2,48,2560]{2,1,0:T(8,128)(2,1)}, bf16[2,48,2560]{2,1,0:T(8,128)(2,1)}, bf16[2,96,2560]{2,1,0:T(8,128)(2,1)}, f32[8,128]{1,0:T(8,128)}) custom-call(f32[3,96,1792]{2,1,0:T(8,128)} %get-tuple-element.128.refs_0_, bf16[3,96,1792]{2,1,0:T(8,128)(2,1)} %collective-permute-done.11.refs_1_, ...), custom_call_target="tpu_custom_call" | custom-call | flops 1472000000 | tf_op jit(solution)/shard_map/hidden_and_back/pallas_call | solution.py:175
  323.9 18.3 %weight_grads.4 = (bf16[1,2560,1792]{2,1,0:T(8,128)(2,1)}, bf16[1,2560,1792]{2,1,0:T(8,128)(2,1)}, bf16[1,1792,2560]{2,1,0:T(8,128)(2,1)}, f32[8,128]{1,0:T(8,128)}) custom-call(s32[1]{0:T(128)} %bitcast.refs_0_, bf16[2560,768]{1,0:T(8,128)(2,1)} %get-tuple-element.105.refs_1_, ...), custom_call_target="tpu_custom_call", output_to_operand_aliasing={{0}: (6, {}), {1}: (7, {}), {2}: (8, {})} | custom-call | flops 1600000000 | tf_op jit(solution)/shard_map/weight_grads/pallas_call | solution.py:175
  344.3 11.8 %all_to_all.43.refs_8_.refs_3_ = bf16[2,3,192,1792]{3,2,1,0:T(8,128)(2,1)} all-to-all(bf16[2,3,192,1792]{3,2,1,0:T(8,128)(2,1)} %get-tuple-element.142), channel_id=1, replica_groups=mesh['groups'=2,'grid'=8,'dp'=2] {'dp'}, dimensions={0} | all-to-all | bytes 8257536 | tf_op jit(solution)/shard_map/all_to_all | solution.py:501
  356.1 13.3 %collective-permute-done.13.refs_1_ = bf16[3,96,1792]{2,1,0:T(8,128)(2,1)S(1)} collective-permute-done((bf16[3,96,1792]{2,1,0:T(8,128)(2,1)}, bf16[3,96,1792]{2,1,0:T(8,128)(2,1)S(1)}, u32[]{:S(2)}, u32[]{:S(2)}) %collective-permute-start.13) | collective-permute-done | bytes 1032224 | tf_op jit(solution)/shard_map/ppermute | solution.py:24
  370.4 16.9 %hidden_and_back.10 = (bf16[1,3,48,1792]{3,2,1,0:T(8,128)(2,1)}, bf16[1,3,48,1792]{3,2,1,0:T(8,128)(2,1)}, bf16[2,96,2560]{2,1,0:T(8,128)(2,1)}, f32[8,128]{1,0:T(8,128)}) custom-call(f32[3,96,1792]{2,1,0:T(8,128)} %get-tuple-element.121.refs_0_, bf16[3,96,1792]{2,1,0:T(8,128)(2,1)} %copy-done.10, bf16[1,2560,1792]{2,1,0:T(8,128)(2,1)} %refs_2_.14, ...), custom_call_target="tpu_custom_call" | custom-call | flops 1472000000 | tf_op jit(solution)/shard_map/hidden_and_back/pallas_call | solution.py:175
  391.0 17.0 %hidden_and_back.11 = (bf16[1,3,48,1792]{3,2,1,0:T(8,128)(2,1)}, bf16[1,3,48,1792]{3,2,1,0:T(8,128)(2,1)}, bf16[2,96,2560]{2,1,0:T(8,128)(2,1)}, f32[8,128]{1,0:T(8,128)}) custom-call(f32[3,96,1792]{2,1,0:T(8,128)} %get-tuple-element.144.refs_0_, bf16[3,96,1792]{2,1,0:T(8,128)(2,1)} %collective-permute-done.17.refs_1_, bf16[1,2560,1792]{2,1,0:T(8,128)(2,1)} %refs_2_.14, ...), custom_call_target="tpu_custom_call" | custom-call | flops 1472000000 | tf_op jit(solution)/shard_map/hidden_and_back/pallas_call | solution.py:175
  411.8 30.1 %weight_grads.5 = (bf16[1,2560,1792]{2,1,0:T(8,128)(2,1)}, bf16[1,2560,1792]{2,1,0:T(8,128)(2,1)}, bf16[1,1792,2560]{2,1,0:T(8,128)(2,1)}, f32[8,128]{1,0:T(8,128)}) custom-call(s32[1]{0:T(128)} %bitcast.refs_0_, bf16[2560,768]{1,0:T(8,128)(2,1)} %get-tuple-element.151.refs_1_, bf16[768,2560]{1,0:T(8,128)(2,1)} %get-tuple-element.152.refs_2_, ...), custom_call_target="tpu_custom_call" | custom-call | flops 2560000000 | tf_op jit(solution)/shard_map/weight_grads/pallas_call | solution.py:175
  442.8 5.2 %add_row_sums.1 = (bf16[1,1,192,2560]{3,2,1,0:T(8,128)(2,1)}, bf16[1,1,192,2560]{3,2,1,0:T(8,128)(2,1)}, f32[8,128]{1,0:T(8,128)}) custom-call(f32[2,192,2560]{2,1,0:T(8,128)} %get-tuple-element.118.refs_0_, bf16[1,1,192,2560]{3,2,1,0:T(8,128)(2,1)} %refs_1_.5, bf16[1,1,192,2560]{3,2,1,0:T(8,128)(2,1)} %refs_2_.15, bf16[2,96,2560]{2,1,0:T(8,128)(2,1)} %copy-done.2, ...), custom_call_target="tpu_custom_call" | custom-call | flops 400000000 | tf_op jit(solution)/shard_map/add_row_sums/pallas_call | solution.py:175
  (82 shorter events, 44.1 us)
Async XLA Ops:
  0.6 42.8 %collective-permute-start.2 = (bf16[1,1,192,2560]{3,2,1,0:T(8,128)(2,1)}, bf16[1,1,192,2560]{3,2,1,0:T(8,128)(2,1)S(1)}, u32[]{:S(2)}, u32[]{:S(2)}) collective-permute-start(bf16[1,1,192,2560]{3,2,1,0:T(8,128)(2,1)} %refs_1_.5), channel_id=1, source_target_pairs={{0,2},{2,0},{4,6},{6,4},{8,10},{10,8},{12,14},{14,12},{1,3},{3,1},... | collective-permute-start | bytes 2949128 | tf_op jit(solution)/shard_map/ppermute | solution.py:24
  3.7 43.1 %collective-permute-start.3 = (bf16[1,1,192,2560]{3,2,1,0:T(8,128)(2,1)}, bf16[1,1,192,2560]{3,2,1,0:T(8,128)(2,1)}, u32[]{:S(2)}, u32[]{:S(2)}) collective-permute-start(bf16[1,1,192,2560]{3,2,1,0:T(8,128)(2,1)} %refs_2_.15), channel_id=1, source_target_pairs={{0,2},{2,0},{4,6},{6,4},{8,10},{10,8},{12,14},{14,12},{1,3},{3,1},... | collective-permute-start | bytes 2949128 | tf_op jit(solution)/shard_map/ppermute | solution.py:24
  3.7 89.7 %collective-permute-start.1 = (bf16[1,1,192,2560]{3,2,1,0:T(8,128)(2,1)}, bf16[1,1,192,2560]{3,2,1,0:T(8,128)(2,1)}, u32[]{:S(2)}, u32[]{:S(2)}) collective-permute-start(bf16[1,1,192,2560]{3,2,1,0:T(8,128)(2,1)} %refs_1_.5), channel_id=1, source_target_pairs={{0,4},{4,0},{2,6},{6,2},{8,12},{12,8},{10,14},{14,10},{1,5},{5,1},... | collective-permute-start | bytes 2949128 | tf_op jit(solution)/shard_map/ppermute | solution.py:24
  5.7 88.3 %collective-permute-start.4 = (bf16[1,1,192,2560]{3,2,1,0:T(8,128)(2,1)}, bf16[1,1,192,2560]{3,2,1,0:T(8,128)(2,1)}, u32[]{:S(2)}, u32[]{:S(2)}) collective-permute-start(bf16[1,1,192,2560]{3,2,1,0:T(8,128)(2,1)} %refs_2_.15), channel_id=1, source_target_pairs={{0,4},{4,0},{2,6},{6,2},{8,12},{12,8},{10,14},{14,10},{1,5},{5,1},... | collective-permute-start | bytes 2949128 | tf_op jit(solution)/shard_map/ppermute | solution.py:24
  15.8 58.9 %collective-permute-start = (bf16[3,192,768]{2,1,0:T(8,128)(2,1)}, bf16[3,192,768]{2,1,0:T(8,128)(2,1)S(1)}, u32[]{:S(2)}, u32[]{:S(2)}) collective-permute-start(bf16[3,192,768]{2,1,0:T(8,128)(2,1)} %get-tuple-element.88), channel_id=1, source_target_pairs={{0,8},{8,0},{2,10},{10,2},{4,12},{12,4},{6,14},{14,6},{1,9},{9,1},... | collective-permute-start | bytes 2654216 | tf_op jit(solution)/shard_map/ppermute | solution.py:24
  43.4 3.4 copy-start.4
  66.3 140.1 %collective-permute-start.6 = (bf16[3,192,1792]{2,1,0:T(8,128)(2,1)}, bf16[3,192,1792]{2,1,0:T(8,128)(2,1)}, u32[]{:S(2)}, u32[]{:S(2)}) collective-permute-start(bf16[3,192,1792]{2,1,0:T(8,128)(2,1)} %get-tuple-element.108), channel_id=1, source_target_pairs={{0,8},{8,0},{2,10},{10,2},{4,12},{12,4},{6,14},{14,6},{1,9},{9,1},... | collective-permute-start | bytes 6193160 | tf_op jit(solution)/shard_map/ppermute | solution.py:24
  69.2 9.8 %all-to-all-start.1 = ((bf16[2,2,192,2560]{3,2,1,0:T(8,128)(2,1)}), bf16[2,2,192,2560]{3,2,1,0:T(8,128)(2,1)}, u32[]{:S(2)}, u32[]{:S(2)}) async-start(bf16[2,2,192,2560]{3,2,1,0:T(8,128)(2,1)} %get-tuple-element.93), calls=%async_computation.1 | async-start | bytes 7864320 | tf_op jit(solution)/shard_map/all_to_all | solution.py:501
  74.8 4.3 copy-start.5
  89.8 6.3 %all-to-all-start.2 = ((bf16[2,3,192,768]{3,2,1,0:T(8,128)(2,1)}), bf16[2,3,192,768]{3,2,1,0:T(8,128)(2,1)S(1)}, u32[]{:S(2)}, u32[]{:S(2)}) async-start(bf16[2,3,192,768]{3,2,1,0:T(8,128)(2,1)} %get-tuple-element.97), calls=%async_computation.2 | async-start | bytes 3538944 | tf_op jit(solution)/shard_map/all_to_all | solution.py:501
  97.9 43.8 %collective-permute-start.8 = (bf16[1,1,192,2560]{3,2,1,0:T(8,128)(2,1)}, bf16[1,1,192,2560]{3,2,1,0:T(8,128)(2,1)S(1)}, u32[]{:S(2)}, u32[]{:S(2)}) collective-permute-start(bf16[1,1,192,2560]{3,2,1,0:T(8,128)(2,1)} %get-tuple-element.98.refs_2_), channel_id=1, source_target_pairs={{0,2},{2,0},{4,6},{6,4},{8,10},{10,8},{12,14},{14,12},{1,3},{3,1},... | collective-permute-start | bytes 2949128 | tf_op jit(solution)/shard_map/ppermute | solution.py:24
  99.5 43.5 %collective-permute-start.7 = (bf16[1,1,192,2560]{3,2,1,0:T(8,128)(2,1)}, bf16[1,1,192,2560]{3,2,1,0:T(8,128)(2,1)S(1)}, u32[]{:S(2)}, u32[]{:S(2)}) collective-permute-start(bf16[1,1,192,2560]{3,2,1,0:T(8,128)(2,1)} %get-tuple-element.95.refs_0_.refs_1_), channel_id=1, source_target_pairs={{0,2},{2,0},{4,6},{6,4},{8,10},{10,8},{12,14},{14,12},{1,3},{3,1},... | collective-permute-start | bytes 2949128 | tf_op jit(solution)/shard_map/ppermute | solution.py:24
  131.6 122.6 %collective-permute-start.5 = (bf16[3,192,1024]{2,1,0:T(8,128)(2,1)}, bf16[3,192,1024]{2,1,0:T(8,128)(2,1)}, u32[]{:S(2)}, u32[]{:S(2)}) collective-permute-start(bf16[3,192,1024]{2,1,0:T(8,128)(2,1)} %get-tuple-element.102), channel_id=1, source_target_pairs={{0,8},{8,0},{2,10},{10,2},{4,12},{12,4},{6,14},{14,6},{1,9},{9,1},... | collective-permute-start | bytes 3538952 | tf_op jit(solution)/shard_map/ppermute | solution.py:24
  163.5 9.8 %all-to-all-start.4 = ((bf16[2,2,192,2560]{3,2,1,0:T(8,128)(2,1)}), bf16[2,2,192,2560]{3,2,1,0:T(8,128)(2,1)}, u32[]{:S(2)}, u32[]{:S(2)}) async-start(bf16[2,2,192,2560]{3,2,1,0:T(8,128)(2,1)} %get-tuple-element.111), calls=%async_computation.4 | async-start | bytes 7864320 | tf_op jit(solution)/shard_map/all_to_all | solution.py:501
  169.1 106.9 %collective-permute-start.11 = (bf16[3,96,1792]{2,1,0:T(8,128)(2,1)}, bf16[3,96,1792]{2,1,0:T(8,128)(2,1)}, u32[]{:S(2)}, u32[]{:S(2)}) collective-permute-start(bf16[3,96,1792]{2,1,0:T(8,128)(2,1)} %get-tuple-element.123), channel_id=1, source_target_pairs={{0,8},{8,0},{2,10},{10,2},{4,12},{12,4},{6,14},{14,6},{1,9},{9,1},... | collective-permute-start | bytes 3096584 | tf_op jit(solution)/shard_map/ppermute | solution.py:24
  207.1 89.9 %collective-permute-start.12 = (bf16[3,96,1792]{2,1,0:T(8,128)(2,1)}, bf16[3,96,1792]{2,1,0:T(8,128)(2,1)S(1)}, u32[]{:S(2)}, u32[]{:S(2)}) collective-permute-start(bf16[3,96,1792]{2,1,0:T(8,128)(2,1)} %get-tuple-element.124), channel_id=1, source_target_pairs={{0,8},{8,0},{2,10},{10,2},{4,12},{12,4},{6,14},{14,6},{1,9},{9,1},... | collective-permute-start | bytes 3096584 | tf_op jit(solution)/shard_map/ppermute | solution.py:24
  225.8 72.7 %collective-permute-start.9 = (bf16[2,96,2560]{2,1,0:T(8,128)(2,1)}, bf16[2,96,2560]{2,1,0:T(8,128)(2,1)S(1)}, u32[]{:S(2)}, u32[]{:S(2)}) collective-permute-start(bf16[2,96,2560]{2,1,0:T(8,128)(2,1)} %get-tuple-element.119), channel_id=1, source_target_pairs={{0,2},{2,0},{4,6},{6,4},{8,10},{10,8},{12,14},{14,12},{1,3},{3,1},... | collective-permute-start | bytes 2949128 | tf_op jit(solution)/shard_map/ppermute | solution.py:24
  227.4 71.1 %collective-permute-start.10 = (bf16[2,96,2560]{2,1,0:T(8,128)(2,1)}, bf16[2,96,2560]{2,1,0:T(8,128)(2,1)}, u32[]{:S(2)}, u32[]{:S(2)}) collective-permute-start(bf16[2,96,2560]{2,1,0:T(8,128)(2,1)} %get-tuple-element.120), channel_id=1, source_target_pairs={{0,2},{2,0},{4,6},{6,4},{8,10},{10,8},{12,14},{14,12},{1,3},{3,1},... | collective-permute-start | bytes 2949128 | tf_op jit(solution)/shard_map/ppermute | solution.py:24
  268.9 8.1 %all-to-all-start.6 = ((bf16[2,3,192,1024]{3,2,1,0:T(8,128)(2,1)}), bf16[2,3,192,1024]{3,2,1,0:T(8,128)(2,1)}, u32[]{:S(2)}, u32[]{:S(2)}) async-start(bf16[2,3,192,1024]{3,2,1,0:T(8,128)(2,1)} %get-tuple-element.126), calls=%async_computation.6 | async-start | bytes 4718592 | tf_op jit(solution)/shard_map/all_to_all | solution.py:501
  298.5 71.0 %collective-permute-start.13 = (bf16[3,96,1792]{2,1,0:T(8,128)(2,1)}, bf16[3,96,1792]{2,1,0:T(8,128)(2,1)S(1)}, u32[]{:S(2)}, u32[]{:S(2)}) collective-permute-start(bf16[3,96,1792]{2,1,0:T(8,128)(2,1)} %get-tuple-element.127), channel_id=1, source_target_pairs={{0,8},{8,0},{2,10},{10,2},{4,12},{12,4},{6,14},{14,6},{1,9},{9,1},... | collective-permute-start | bytes 3096584 | tf_op jit(solution)/shard_map/ppermute | solution.py:24
  318.3 37.8 %collective-permute-start.14 = (bf16[2,48,2560]{2,1,0:T(8,128)(2,1)}, bf16[2,48,2560]{2,1,0:T(8,128)(2,1)S(1)}, u32[]{:S(2)}, u32[]{:S(2)}) collective-permute-start(bf16[2,48,2560]{2,1,0:T(8,128)(2,1)} %get-tuple-element.131), channel_id=1, source_target_pairs={{0,2},{2,0},{4,6},{6,4},{8,10},{10,8},{12,14},{14,12},{1,3},{3,1},... | collective-permute-start | bytes 1474568 | tf_op jit(solution)/shard_map/ppermute | solution.py:24
  319.9 36.2 %collective-permute-start.15 = (bf16[2,48,2560]{2,1,0:T(8,128)(2,1)}, bf16[2,48,2560]{2,1,0:T(8,128)(2,1)S(1)}, u32[]{:S(2)}, u32[]{:S(2)}) collective-permute-start(bf16[2,48,2560]{2,1,0:T(8,128)(2,1)} %get-tuple-element.132), channel_id=1, source_target_pairs={{0,2},{2,0},{4,6},{6,4},{8,10},{10,8},{12,14},{14,12},{1,3},{3,1},... | collective-permute-start | bytes 1474568 | tf_op jit(solution)/shard_map/ppermute | solution.py:24
  321.0 68.8 %collective-permute-start.17 = (bf16[3,96,1792]{2,1,0:T(8,128)(2,1)}, bf16[3,96,1792]{2,1,0:T(8,128)(2,1)}, u32[]{:S(2)}, u32[]{:S(2)}) collective-permute-start(bf16[3,96,1792]{2,1,0:T(8,128)(2,1)} %get-tuple-element.145), channel_id=1, source_target_pairs={{0,8},{8,0},{2,10},{10,2},{4,12},{12,4},{6,14},{14,6},{1,9},{9,1},... | collective-permute-start | bytes 3096584 | tf_op jit(solution)/shard_map/ppermute | solution.py:24
  342.8 45.0 %collective-permute-start.18 = (bf16[2,96,2560]{2,1,0:T(8,128)(2,1)}, bf16[2,96,2560]{2,1,0:T(8,128)(2,1)}, u32[]{:S(2)}, u32[]{:S(2)}) collective-permute-start(bf16[2,96,2560]{2,1,0:T(8,128)(2,1)} %get-tuple-element.146), channel_id=1, source_target_pairs={{0,2},{2,0},{4,6},{6,4},{8,10},{10,8},{12,14},{14,12},{1,3},{3,1},... | collective-permute-start | bytes 2949128 | tf_op jit(solution)/shard_map/ppermute | solution.py:24
  356.1 13.4 %copy-start.13 = (bf16[2,48,2560]{2,1,0:T(8,128)(2,1)}, bf16[2,48,2560]{2,1,0:T(8,128)(2,1)S(1)}, u32[]{:S(2)}) copy-start(bf16[2,48,2560]{2,1,0:T(8,128)(2,1)S(1)} %collective-permute-done.14.refs_5_) | copy-start | bytes 1474564
  356.1 13.3 %copy-start.14 = (bf16[2,48,2560]{2,1,0:T(8,128)(2,1)}, bf16[2,48,2560]{2,1,0:T(8,128)(2,1)S(1)}, u32[]{:S(2)}) copy-start(bf16[2,48,2560]{2,1,0:T(8,128)(2,1)S(1)} %collective-permute-done.15.refs_6_) | copy-start | bytes 1474564
  387.3 2.5 collective-permute-start.19
  387.4 2.8 collective-permute-start.20
  387.9 54.0 %collective-permute-start.16 = (bf16[2,96,2560]{2,1,0:T(8,128)(2,1)}, bf16[2,96,2560]{2,1,0:T(8,128)(2,1)}, u32[]{:S(2)}, u32[]{:S(2)}) collective-permute-start(bf16[2,96,2560]{2,1,0:T(8,128)(2,1)} %get-tuple-element.143), channel_id=1, source_target_pairs={{0,4},{4,0},{2,6},{6,2},{8,12},{12,8},{10,14},{14,10},{1,5},{5,1},... | collective-permute-start | bytes 2949128 | tf_op jit(solution)/shard_map/ppermute | solution.py:24
  408.0 33.9 %collective-permute-start.21 = (bf16[2,96,2560]{2,1,0:T(8,128)(2,1)}, bf16[2,96,2560]{2,1,0:T(8,128)(2,1)S(1)}, u32[]{:S(2)}, u32[]{:S(2)}) collective-permute-start(bf16[2,96,2560]{2,1,0:T(8,128)(2,1)} %get-tuple-element.150), channel_id=1, source_target_pairs={{0,4},{4,0},{2,6},{6,2},{8,12},{12,8},{10,14},{14,10},{1,5},{5,1},... | collective-permute-start | bytes 2949128 | tf_op jit(solution)/shard_map/ppermute | solution.py:24
  408.1 2.2 collective-permute-start.22
  408.2 2.7 collective-permute-start.23
  (11 other events, 10.5 us)

commit v4 on v3

--- a/solution.py
+++ b/solution.py
@@ -10,7 +10,7 @@
 
 VMEM_BYTES = 62 * 1024 * 1024
 TILE = 256
-COST_SCALE = 0.08e9
+COST_SCALE = 0.2e9
 G, U, PRE = 0, 1, 2
 
 
@@ -430,7 +430,7 @@
     ]
     scratch = [pltpu.VMEM((3, total, TILE), jnp.bfloat16)]
     return order.call(
-        body, "weight_grads", 4 + 4 * count, count, inputs, outputs, scratch, aliases=aliases.items()
+        body, "weight_grads", 4 + 2 * count, count, inputs, outputs, scratch, aliases=aliases.items()
     )
 
 
@@ -477,7 +477,7 @@
     gather("near", "own", near)
     gather("far", "own", far)
 
-    a = max(1, n_tiles * 3 // 7)
+    a = max(1, n_tiles * 4 // 7)
     every = (0, n_tiles)
     chunks = {"c0": (0, a), "c1": (a, n_tiles - a)}
     own, ready, got, pairs = {}, {}, {}, {}

time: 450 us -> 436 us (0.969)
  waiting for transfers between devices: 77.4 us -> 49.6 us
  blocking collectives: 46.6 us -> 66.4 us
  starting transfers between devices: 44.7 us -> 39.1 us
    all_to_all x4 -> x6, blocking collectives: 46.6 us -> 66.4 us  [both_replicas(): return lax.all_to_all(pair, 'dp', 0, 0, tiled=True)]
    ppermute x24, waiting for transfers between devices: 67.7 us -> 48.3 us  [from_partner(): return lax.ppermute(block, axis, route)]
    all_to_all x4 -> x2, starting transfers between devices: 19.7 us -> 10.4 us  [both_replicas(): return lax.all_to_all(pair, 'dp', 0, 0, tiled=True)]
    all_to_all x4 -> x2, waiting for transfers between devices: 9.64 us -> 1.32 us  [both_replicas(): return lax.all_to_all(pair, 'dp', 0, 0, tiled=True)]
  transfers between devices with their start and end apart: 28 -> 26, of which waited for: 14 -> 9; matrix products, arithmetic and copies ran while one was open for 0% -> 0% of each run, Pallas kernels for 59% -> 61%
where the time goes in v4:
time: 436 us; the launch traced here: 435 us
  Pallas kernels  271 us (62%)
  blocking collectives  66.4 us (15%)
  waiting for transfers between devices  49.6 us (11%)
  starting transfers between devices  39.1 us (9%)
  local copies, waits for them, and re-layouts  7.81 us (2%)
    pallas_call x24, Pallas kernels, call(): pl.pallas_call(kernel, name=name, grid=(steps,), in_specs=[spec for _, sp...  271 us
    all_to_all x6, blocking collectives, both_replicas(): return lax.all_to_all(pair, 'dp', 0, 0, tiled=True)  66.4 us
    ppermute x24, waiting for transfers between devices, from_partner(): return lax.ppermute(block, axis, route)  48.3 us
    ppermute x24, starting transfers between devices, from_partner(): return lax.ppermute(block, axis, route)  28.7 us
    all_to_all x2, starting transfers between devices, both_replicas(): return lax.all_to_all(pair, 'dp', 0, 0, tiled=True)  10.4 us
  transfers between devices with their start and end apart: 26, of which 9 were waited for; matrix products, arithmetic and copies ran while one was open for 0% of the time, Pallas kernels for 61%

profile of v4, /device:TPU:0, one launch (start us, length us, event | category | flops | bytes accessed | tf_op | source)
XLA Modules:
  0.0 434.7 jit_solution(4069906781038819164)
XLA Ops:
  0.6 3.0 collective-permute-start.2
  3.8 11.5 %partials.5 = (f32[3,192,1024]{2,1,0:T(8,128)}, bf16[3,192,1024]{2,1,0:T(8,128)(2,1)}, f32[8,128]{1,0:T(8,128)}) custom-call(bf16[1,1,192,2560]{3,2,1,0:T(8,128)(2,1)} %refs_1_.5, bf16[1,1,192,2560]{3,2,1,0:T(8,128)(2,1)} %refs_1_.5, bf16[1,1,192,2560]{3,2,1,0:T(8,128)(2,1)} %refs_2_.15, bf16[1,2560,1792]{2,1,0:T(8,128)(2,1)} %refs_2_.14, ...), custom_call_target="tpu_custom_call" | custom-call | flops 2520000000 | tf_op jit(solution)/shard_map/partials/pallas_call | solution.py:175
  15.2 3.0 collective-permute-start
  20.3 11.6 %partials.6 = (f32[3,192,768]{2,1,0:T(8,128)}, bf16[3,192,768]{2,1,0:T(8,128)(2,1)}, bf16[2,2,192,2560]{3,2,1,0:T(8,128)(2,1)}, f32[8,128]{1,0:T(8,128)}) custom-call(bf16[1,1,192,2560]{3,2,1,0:T(8,128)(2,1)} %refs_1_.5, bf16[1,1,192,2560]{3,2,1,0:T(8,128)(2,1)} %refs_1_.5, bf16[1,1,192,2560]{3,2,1,0:T(8,128)(2,1)} %refs_2_.15, ...), custom_call_target="tpu_custom_call" | custom-call | flops 2040000000 | tf_op jit(solution)/shard_map/partials/pallas_call | solution.py:175
  31.9 11.5 %all_to_all.40.refs_7_.refs_2_.refs_3_ = bf16[2,2,192,2560]{3,2,1,0:T(8,128)(2,1)} all-to-all(bf16[2,2,192,2560]{3,2,1,0:T(8,128)(2,1)} %get-tuple-element.91), channel_id=1, replica_groups=mesh['groups'=2,'grid'=8,'dp'=2] {'dp'}, dimensions={0} | all-to-all | bytes 7864320 | tf_op jit(solution)/shard_map/all_to_all | solution.py:501
  43.4 3.4 collective-permute-done.3.refs_2_
  46.8 19.6 %partials.7 = (f32[3,192,1792]{2,1,0:T(8,128)}, bf16[3,192,1792]{2,1,0:T(8,128)(2,1)}, bf16[2,2,192,2560]{3,2,1,0:T(8,128)(2,1)}, f32[8,128]{1,0:T(8,128)}) custom-call(bf16[1,1,192,2560]{3,2,1,0:T(8,128)(2,1)} %collective-permute-done.2.refs_0_.refs_1_, bf16[1,1,192,2560]{3,2,1,0:T(8,128)(2,1)} %collective-permute-done.2.refs_0_.refs_1_, ...), custom_call_target="tpu_custom_call" | custom-call | flops 3960000000 | tf_op jit(solution)/shard_map/partials/pallas_call | solution.py:175
  69.3 11.5 %all_to_all.41.refs_6_.refs_0_.refs_1_ = bf16[2,2,192,2560]{3,2,1,0:T(8,128)(2,1)} all-to-all(bf16[2,2,192,2560]{3,2,1,0:T(8,128)(2,1)} %get-tuple-element.93), channel_id=1, replica_groups=mesh['groups'=2,'grid'=8,'dp'=2] {'dp'}, dimensions={0} | all-to-all | bytes 7864320 | tf_op jit(solution)/shard_map/all_to_all | solution.py:501
  80.8 12.6 %hidden_and_back.6 = (bf16[2,3,192,1024]{3,2,1,0:T(8,128)(2,1)}, f32[2,192,2560]{2,1,0:T(8,128)}, f32[8,128]{1,0:T(8,128)}) custom-call(f32[3,192,1024]{2,1,0:T(8,128)} %get-tuple-element.89.refs_0_, bf16[3,192,1024]{2,1,0:T(8,128)(2,1)} %collective-permute-done.refs_1_, bf16[1,2560,1792]{2,1,0:T(8,128)(2,1)} %refs_2_.14, bf16[1,2560,1792]{2,1,0:T(8,128)(2,1)} %refs_3_.19, ...), custom_call_target="tpu_custom_call" | custom-call | flops 2360000000 | tf_op jit(solution)/shard_map/hidden_and_back/pallas_call | solution.py:175
  93.4 4.9 %all-to-all-start.2 = ((bf16[2,3,192,1024]{3,2,1,0:T(8,128)(2,1)}), bf16[2,3,192,1024]{3,2,1,0:T(8,128)(2,1)}, u32[]{:S(2)}, u32[]{:S(2)}) async-start(bf16[2,3,192,1024]{3,2,1,0:T(8,128)(2,1)} %get-tuple-element.97), calls=%async_computation.2 | async-start | bytes 4718592 | tf_op jit(solution)/shard_map/all_to_all | solution.py:501
  99.9 4.0 collective-permute-done.4.refs_0_
  106.5 19.6 %partials.8 = (f32[3,96,1792]{2,1,0:T(8,128)}, bf16[3,96,1792]{2,1,0:T(8,128)(2,1)}, f32[3,96,1792]{2,1,0:T(8,128)}, bf16[3,96,1792]{2,1,0:T(8,128)(2,1)}, bf16[...) custom-call(bf16[1,1,192,2560]{3,2,1,0:T(8,128)(2,1)} %get-tuple-element.95.refs_0_.refs_1_, ...), custom_call_target="tpu_custom_call" | custom-call | flops 3960000000 | tf_op jit(solution)/shard_map/partials/pallas_call | solution.py:175
  126.0 11.6 %all_to_all.42.refs_3_.refs_2_ = bf16[2,2,192,2560]{3,2,1,0:T(8,128)(2,1)} all-to-all(bf16[2,2,192,2560]{3,2,1,0:T(8,128)(2,1)} %get-tuple-element.101), channel_id=1, replica_groups=mesh['groups'=2,'grid'=8,'dp'=2] {'dp'}, dimensions={0} | all-to-all | bytes 7864320 | tf_op jit(solution)/shard_map/all_to_all | solution.py:501
  138.2 10.0 %assemble.2 = (bf16[2560,768]{1,0:T(8,128)(2,1)}, bf16[768,2560]{1,0:T(8,128)(2,1)}, f32[8,128]{1,0:T(8,128)}) custom-call(bf16[2,2,192,2560]{3,2,1,0:T(8,128)(2,1)} %all_to_all.41.refs_6_.refs_0_.refs_1_, bf16[2,2,192,2560]{3,2,1,0:T(8,128)(2,1)} %all_to_all.41.refs_6_.refs_0_.refs_1_, bf16[2,2,192,2560]{3,2,1,0:T(8,128)(2,1)} %all_to_all.40.refs_7_.refs_2_.refs_3_, ...), custom_call_target="tpu_custom_call" | custom-call | flops 2000000000 | tf_op jit(solution)/shard_map/assemble/pallas_call | solution.py:175
  149.5 19.5 %partials.9 = (f32[3,96,1792]{2,1,0:T(8,128)}, bf16[3,96,1792]{2,1,0:T(8,128)(2,1)}, f32[3,96,1792]{2,1,0:T(8,128)}, bf16[3,96,1792]{2,1,0:T(8,128)(2,1)}, bf16[...) custom-call(bf16[1,1,192,2560]{3,2,1,0:T(8,128)(2,1)} %copy-done.4, bf16[1,1,192,2560]{3,2,1,0:T(8,128)(2,1)} %copy-done.4, ...), custom_call_target="tpu_custom_call" | custom-call | flops 3960000000 | tf_op jit(solution)/shard_map/partials/pallas_call | solution.py:175
  169.1 5.5 %all-to-all-start.4 = ((bf16[2,2,192,2560]{3,2,1,0:T(8,128)(2,1)}), bf16[2,2,192,2560]{3,2,1,0:T(8,128)(2,1)}, u32[]{:S(2)}, u32[]{:S(2)}) async-start(bf16[2,2,192,2560]{3,2,1,0:T(8,128)(2,1)} %get-tuple-element.111), calls=%async_computation.4 | async-start | bytes 7864320 | tf_op jit(solution)/shard_map/all_to_all | solution.py:501
  178.9 10.0 %assemble.3 = (bf16[2560,768]{1,0:T(8,128)(2,1)}, bf16[768,2560]{1,0:T(8,128)(2,1)}, f32[8,128]{1,0:T(8,128)}) custom-call(bf16[2,2,192,2560]{3,2,1,0:T(8,128)(2,1)} %all-to-all-done.4.refs_0_.refs_1_.refs_5_, bf16[2,2,192,2560]{3,2,1,0:T(8,128)(2,1)} %all-to-all-done.4.refs_0_.refs_1_.refs_5_, bf16[2,2,192,2560]{3,2,1,0:T(8,128)(2,1)} %all_to_all.42.refs_3_.refs_2_, ...), custom_call_target="tpu_custom_call" | custom-call | flops 2000000000 | tf_op jit(solution)/shard_map/assemble/pallas_call | solution.py:175
  192.4 18.7 %hidden_and_back.7 = (bf16[2,3,192,1792]{3,2,1,0:T(8,128)(2,1)}, bf16[2,96,2560]{2,1,0:T(8,128)(2,1)}, bf16[2,96,2560]{2,1,0:T(8,128)(2,1)}, f32[8,128]{1,0:T(8,128)}) custom-call(f32[3,192,1792]{2,1,0:T(8,128)} %get-tuple-element.107.refs_0_, bf16[3,192,1792]{2,1,0:T(8,128)(2,1)} %collective-permute-done.6.refs_1_, bf16[1,2560,1792]{2,1,0:T(8,128)(2,1)} %refs_2_.14, ...), custom_call_target="tpu_custom_call" | custom-call | flops 3680000000 | tf_op jit(solution)/shard_map/hidden_and_back/pallas_call | solution.py:175
  213.2 11.8 %all_to_all.43.refs_3_.refs_6_ = bf16[2,3,192,1792]{3,2,1,0:T(8,128)(2,1)} all-to-all(bf16[2,3,192,1792]{3,2,1,0:T(8,128)(2,1)} %get-tuple-element.115), channel_id=1, replica_groups=mesh['groups'=2,'grid'=8,'dp'=2] {'dp'}, dimensions={0} | all-to-all | bytes 8257536 | tf_op jit(solution)/shard_map/all_to_all | solution.py:501
  225.0 17.8 %weight_grads.3 = (bf16[1,2560,1792]{2,1,0:T(8,128)(2,1)}, bf16[1,2560,1792]{2,1,0:T(8,128)(2,1)}, bf16[1,1792,2560]{2,1,0:T(8,128)(2,1)}, f32[8,128]{1,0:T(8,128)}) custom-call(s32[1]{0:T(128)} %bitcast.refs_0_, bf16[2560,768]{1,0:T(8,128)(2,1)} %get-tuple-element.105.refs_1_, bf16[768,2560]{1,0:T(8,128)(2,1)} %get-tuple-element.106.refs_2_, ...), custom_call_target="tpu_custom_call" | custom-call | flops 2400000000 | tf_op jit(solution)/shard_map/weight_grads/pallas_call | solution.py:175
  242.8 12.8 %hidden_and_back.8 = (bf16[2,3,192,768]{3,2,1,0:T(8,128)(2,1)}, f32[2,192,2560]{2,1,0:T(8,128)}, f32[8,128]{1,0:T(8,128)}) custom-call(f32[3,192,768]{2,1,0:T(8,128)} %get-tuple-element.86.refs_0_, bf16[3,192,768]{2,1,0:T(8,128)(2,1)} %collective-permute-done.5.refs_1_, bf16[1,2560,1792]{2,1,0:T(8,128)(2,1)} %refs_2_.14, bf16[1,2560,1792]{2,1,0:T(8,128)(2,1)} %refs_3_.19, ...), custom_call_target="tpu_custom_call" | custom-call | flops 1920000000 | tf_op jit(solution)/shard_map/hidden_and_back/pallas_call | solution.py:175
  255.6 8.2 %all_to_all.44.refs_4_.refs_5_ = bf16[2,3,192,768]{3,2,1,0:T(8,128)(2,1)} all-to-all(bf16[2,3,192,768]{3,2,1,0:T(8,128)(2,1)} %get-tuple-element.126), channel_id=1, replica_groups=mesh['groups'=2,'grid'=8,'dp'=2] {'dp'}, dimensions={0} | all-to-all | bytes 3538944 | tf_op jit(solution)/shard_map/all_to_all | solution.py:501
  264.1 20.3 %collective-permute-done.12.refs_2_.refs_3_.refs_1_ = bf16[3,96,1792]{2,1,0:T(8,128)(2,1)S(1)} collective-permute-done((bf16[3,96,1792]{2,1,0:T(8,128)(2,1)}, bf16[3,96,1792]{2,1,0:T(8,128)(2,1)S(1)}, u32[]{:S(2)}, u32[]{:S(2)}) %collective-permute-start.12) | collective-permute-done | bytes 1032224 | tf_op jit(solution)/shard_map/ppermute | solution.py:24
  286.9 18.8 %hidden_and_back.9 = (bf16[2,3,192,1792]{3,2,1,0:T(8,128)(2,1)}, bf16[2,48,2560]{2,1,0:T(8,128)(2,1)}, bf16[2,48,2560]{2,1,0:T(8,128)(2,1)}, bf16[2,96,2560]{2,1,0:T(8,128)(2,1)}, f32[8,128]{1,0:T(8,128)}) custom-call(f32[3,96,1792]{2,1,0:T(8,128)} %get-tuple-element.128.refs_0_, bf16[3,96,1792]{2,1,0:T(8,128)(2,1)} %collective-permute-done.11.refs_1_, ...), custom_call_target="tpu_custom_call" | custom-call | flops 3680000000 | tf_op jit(solution)/shard_map/hidden_and_back/pallas_call | solution.py:175
  311.4 15.0 %weight_grads.4 = (bf16[1,2560,1792]{2,1,0:T(8,128)(2,1)}, bf16[1,2560,1792]{2,1,0:T(8,128)(2,1)}, bf16[1,1792,2560]{2,1,0:T(8,128)(2,1)}, f32[8,128]{1,0:T(8,128)}) custom-call(s32[1]{0:T(128)} %bitcast.refs_0_, bf16[2560,768]{1,0:T(8,128)(2,1)} %get-tuple-element.105.refs_1_, ...), custom_call_target="tpu_custom_call", output_to_operand_aliasing={{0}: (6, {}), {1}: (7, {}), {2}: (8, {})} | custom-call | flops 2000000000 | tf_op jit(solution)/shard_map/weight_grads/pallas_call | solution.py:175
  328.4 11.8 %all_to_all.45.refs_8_.refs_3_ = bf16[2,3,192,1792]{3,2,1,0:T(8,128)(2,1)} all-to-all(bf16[2,3,192,1792]{3,2,1,0:T(8,128)(2,1)} %get-tuple-element.142), channel_id=1, replica_groups=mesh['groups'=2,'grid'=8,'dp'=2] {'dp'}, dimensions={0} | all-to-all | bytes 8257536 | tf_op jit(solution)/shard_map/all_to_all | solution.py:501
  340.1 14.9 %collective-permute-done.13.refs_1_ = bf16[3,96,1792]{2,1,0:T(8,128)(2,1)S(1)} collective-permute-done((bf16[3,96,1792]{2,1,0:T(8,128)(2,1)}, bf16[3,96,1792]{2,1,0:T(8,128)(2,1)S(1)}, u32[]{:S(2)}, u32[]{:S(2)}) %collective-permute-start.13) | collective-permute-done | bytes 1032224 | tf_op jit(solution)/shard_map/ppermute | solution.py:24
  356.0 16.9 %hidden_and_back.10 = (bf16[1,3,48,1792]{3,2,1,0:T(8,128)(2,1)}, bf16[1,3,48,1792]{3,2,1,0:T(8,128)(2,1)}, bf16[2,96,2560]{2,1,0:T(8,128)(2,1)}, f32[8,128]{1,0:T(8,128)}) custom-call(f32[3,96,1792]{2,1,0:T(8,128)} %get-tuple-element.121.refs_0_, bf16[3,96,1792]{2,1,0:T(8,128)(2,1)} %copy-done.9, bf16[1,2560,1792]{2,1,0:T(8,128)(2,1)} %refs_2_.14, ...), custom_call_target="tpu_custom_call" | custom-call | flops 3680000000 | tf_op jit(solution)/shard_map/hidden_and_back/pallas_call | solution.py:175
  373.4 3.1 collective-permute-done.17.refs_1_
  377.6 17.0 %hidden_and_back.11 = (bf16[1,3,48,1792]{3,2,1,0:T(8,128)(2,1)}, bf16[1,3,48,1792]{3,2,1,0:T(8,128)(2,1)}, bf16[2,96,2560]{2,1,0:T(8,128)(2,1)}, f32[8,128]{1,0:T(8,128)}) custom-call(f32[3,96,1792]{2,1,0:T(8,128)} %get-tuple-element.144.refs_0_, bf16[3,96,1792]{2,1,0:T(8,128)(2,1)} %collective-permute-done.17.refs_1_, bf16[1,2560,1792]{2,1,0:T(8,128)(2,1)} %refs_2_.14, ...), custom_call_target="tpu_custom_call" | custom-call | flops 3680000000 | tf_op jit(solution)/shard_map/hidden_and_back/pallas_call | solution.py:175
  398.3 30.1 %weight_grads.5 = (bf16[1,2560,1792]{2,1,0:T(8,128)(2,1)}, bf16[1,2560,1792]{2,1,0:T(8,128)(2,1)}, bf16[1,1792,2560]{2,1,0:T(8,128)(2,1)}, f32[8,128]{1,0:T(8,128)}) custom-call(s32[1]{0:T(128)} %bitcast.refs_0_, bf16[2560,768]{1,0:T(8,128)(2,1)} %get-tuple-element.151.refs_1_, bf16[768,2560]{1,0:T(8,128)(2,1)} %get-tuple-element.152.refs_2_, ...), custom_call_target="tpu_custom_call" | custom-call | flops 3600000000 | tf_op jit(solution)/shard_map/weight_grads/pallas_call | solution.py:175
  429.4 5.1 %add_row_sums.1 = (bf16[1,1,192,2560]{3,2,1,0:T(8,128)(2,1)}, bf16[1,1,192,2560]{3,2,1,0:T(8,128)(2,1)}, f32[8,128]{1,0:T(8,128)}) custom-call(f32[2,192,2560]{2,1,0:T(8,128)} %get-tuple-element.118.refs_0_, bf16[1,1,192,2560]{3,2,1,0:T(8,128)(2,1)} %refs_1_.5, bf16[1,1,192,2560]{3,2,1,0:T(8,128)(2,1)} %refs_2_.15, bf16[2,96,2560]{2,1,0:T(8,128)(2,1)} %copy-done.3, ...), custom_call_target="tpu_custom_call" | custom-call | flops 1000000000 | tf_op jit(solution)/shard_map/add_row_sums/pallas_call | solution.py:175
  (78 shorter events, 38.6 us)
Async XLA Ops:
  0.6 17.6 %copy-start = (bf16[1,1,192,2560]{3,2,1,0:T(8,128)(2,1)S(1)}, bf16[1,1,192,2560]{3,2,1,0:T(8,128)(2,1)}, u32[]{:S(2)}) copy-start(bf16[1,1,192,2560]{3,2,1,0:T(8,128)(2,1)} %refs_1_.5) | copy-start | bytes 2949124
  0.6 42.8 %collective-permute-start.2 = (bf16[1,1,192,2560]{3,2,1,0:T(8,128)(2,1)}, bf16[1,1,192,2560]{3,2,1,0:T(8,128)(2,1)}, u32[]{:S(2)}, u32[]{:S(2)}) collective-permute-start(bf16[1,1,192,2560]{3,2,1,0:T(8,128)(2,1)} %refs_1_.5), channel_id=1, source_target_pairs={{0,2},{2,0},{4,6},{6,4},{8,10},{10,8},{12,14},{14,12},{1,3},{3,1},... | collective-permute-start | bytes 2949128 | tf_op jit(solution)/shard_map/ppermute | solution.py:24
  3.7 43.1 %collective-permute-start.3 = (bf16[1,1,192,2560]{3,2,1,0:T(8,128)(2,1)}, bf16[1,1,192,2560]{3,2,1,0:T(8,128)(2,1)}, u32[]{:S(2)}, u32[]{:S(2)}) collective-permute-start(bf16[1,1,192,2560]{3,2,1,0:T(8,128)(2,1)} %refs_2_.15), channel_id=1, source_target_pairs={{0,2},{2,0},{4,6},{6,4},{8,10},{10,8},{12,14},{14,12},{1,3},{3,1},... | collective-permute-start | bytes 2949128 | tf_op jit(solution)/shard_map/ppermute | solution.py:24
  15.2 65.6 %collective-permute-start = (bf16[3,192,1024]{2,1,0:T(8,128)(2,1)}, bf16[3,192,1024]{2,1,0:T(8,128)(2,1)}, u32[]{:S(2)}, u32[]{:S(2)}) collective-permute-start(bf16[3,192,1024]{2,1,0:T(8,128)(2,1)} %get-tuple-element.88), channel_id=1, source_target_pairs={{0,8},{8,0},{2,10},{10,2},{4,12},{12,4},{6,14},{14,6},{1,9},{9,1},... | collective-permute-start | bytes 3538952 | tf_op jit(solution)/shard_map/ppermute | solution.py:24
  18.2 80.1 %collective-permute-start.1 = (bf16[1,1,192,2560]{3,2,1,0:T(8,128)(2,1)S(1)}, bf16[1,1,192,2560]{3,2,1,0:T(8,128)(2,1)S(1)}, u32[]{:S(2)}, u32[]{:S(2)}) collective-permute-start(bf16[1,1,192,2560]{3,2,1,0:T(8,128)(2,1)S(1)} %copy-done), channel_id=1, source_target_pairs={{0,4},{4,0},{2,6},{6,2},{8,12},{12,8},{10,14},{14,10},{1,5},{5,1},... | collective-permute-start | bytes 2949128 | tf_op jit(solution)/shard_map/ppermute | solution.py:24
  19.8 84.1 %collective-permute-start.4 = (bf16[1,1,192,2560]{3,2,1,0:T(8,128)(2,1)}, bf16[1,1,192,2560]{3,2,1,0:T(8,128)(2,1)}, u32[]{:S(2)}, u32[]{:S(2)}) collective-permute-start(bf16[1,1,192,2560]{3,2,1,0:T(8,128)(2,1)} %refs_2_.15), channel_id=1, source_target_pairs={{0,4},{4,0},{2,6},{6,2},{8,12},{12,8},{10,14},{14,10},{1,5},{5,1},... | collective-permute-start | bytes 2949128 | tf_op jit(solution)/shard_map/ppermute | solution.py:24
  66.4 122.5 %collective-permute-start.6 = (bf16[3,192,1792]{2,1,0:T(8,128)(2,1)}, bf16[3,192,1792]{2,1,0:T(8,128)(2,1)}, u32[]{:S(2)}, u32[]{:S(2)}) collective-permute-start(bf16[3,192,1792]{2,1,0:T(8,128)(2,1)} %get-tuple-element.108), channel_id=1, source_target_pairs={{0,8},{8,0},{2,10},{10,2},{4,12},{12,4},{6,14},{14,6},{1,9},{9,1},... | collective-permute-start | bytes 6193160 | tf_op jit(solution)/shard_map/ppermute | solution.py:24
  93.4 10.4 %all-to-all-start.2 = ((bf16[2,3,192,1024]{3,2,1,0:T(8,128)(2,1)}), bf16[2,3,192,1024]{3,2,1,0:T(8,128)(2,1)}, u32[]{:S(2)}, u32[]{:S(2)}) async-start(bf16[2,3,192,1024]{3,2,1,0:T(8,128)(2,1)} %get-tuple-element.97), calls=%async_computation.2 | async-start | bytes 4718592 | tf_op jit(solution)/shard_map/all_to_all | solution.py:501
  104.5 43.8 %collective-permute-start.8 = (bf16[1,1,192,2560]{3,2,1,0:T(8,128)(2,1)}, bf16[1,1,192,2560]{3,2,1,0:T(8,128)(2,1)S(1)}, u32[]{:S(2)}, u32[]{:S(2)}) collective-permute-start(bf16[1,1,192,2560]{3,2,1,0:T(8,128)(2,1)} %get-tuple-element.98.refs_2_), channel_id=1, source_target_pairs={{0,2},{2,0},{4,6},{6,4},{8,10},{10,8},{12,14},{14,12},{1,3},{3,1},... | collective-permute-start | bytes 2949128 | tf_op jit(solution)/shard_map/ppermute | solution.py:24
  106.1 42.1 %collective-permute-start.7 = (bf16[1,1,192,2560]{3,2,1,0:T(8,128)(2,1)}, bf16[1,1,192,2560]{3,2,1,0:T(8,128)(2,1)S(1)}, u32[]{:S(2)}, u32[]{:S(2)}) collective-permute-start(bf16[1,1,192,2560]{3,2,1,0:T(8,128)(2,1)} %get-tuple-element.95.refs_0_.refs_1_), channel_id=1, source_target_pairs={{0,2},{2,0},{4,6},{6,4},{8,10},{10,8},{12,14},{14,12},{1,3},{3,1},... | collective-permute-start | bytes 2949128 | tf_op jit(solution)/shard_map/ppermute | solution.py:24
  138.2 104.6 %collective-permute-start.5 = (bf16[3,192,768]{2,1,0:T(8,128)(2,1)}, bf16[3,192,768]{2,1,0:T(8,128)(2,1)}, u32[]{:S(2)}, u32[]{:S(2)}) collective-permute-start(bf16[3,192,768]{2,1,0:T(8,128)(2,1)} %get-tuple-element.102), channel_id=1, source_target_pairs={{0,8},{8,0},{2,10},{10,2},{4,12},{12,4},{6,14},{14,6},{1,9},{9,1},... | collective-permute-start | bytes 2654216 | tf_op jit(solution)/shard_map/ppermute | solution.py:24
  148.3 1.2 copy-start.4
  169.1 9.8 %all-to-all-start.4 = ((bf16[2,2,192,2560]{3,2,1,0:T(8,128)(2,1)}), bf16[2,2,192,2560]{3,2,1,0:T(8,128)(2,1)}, u32[]{:S(2)}, u32[]{:S(2)}) async-start(bf16[2,2,192,2560]{3,2,1,0:T(8,128)(2,1)} %get-tuple-element.111), calls=%async_computation.4 | async-start | bytes 7864320 | tf_op jit(solution)/shard_map/all_to_all | solution.py:501
  174.6 89.5 %collective-permute-start.11 = (bf16[3,96,1792]{2,1,0:T(8,128)(2,1)}, bf16[3,96,1792]{2,1,0:T(8,128)(2,1)}, u32[]{:S(2)}, u32[]{:S(2)}) collective-permute-start(bf16[3,96,1792]{2,1,0:T(8,128)(2,1)} %get-tuple-element.123), channel_id=1, source_target_pairs={{0,8},{8,0},{2,10},{10,2},{4,12},{12,4},{6,14},{14,6},{1,9},{9,1},... | collective-permute-start | bytes 3096584 | tf_op jit(solution)/shard_map/ppermute | solution.py:24
  189.5 94.9 %collective-permute-start.12 = (bf16[3,96,1792]{2,1,0:T(8,128)(2,1)}, bf16[3,96,1792]{2,1,0:T(8,128)(2,1)S(1)}, u32[]{:S(2)}, u32[]{:S(2)}) collective-permute-start(bf16[3,96,1792]{2,1,0:T(8,128)(2,1)} %get-tuple-element.124), channel_id=1, source_target_pairs={{0,8},{8,0},{2,10},{10,2},{4,12},{12,4},{6,14},{14,6},{1,9},{9,1},... | collective-permute-start | bytes 3096584 | tf_op jit(solution)/shard_map/ppermute | solution.py:24
  211.1 74.8 %collective-permute-start.9 = (bf16[2,96,2560]{2,1,0:T(8,128)(2,1)}, bf16[2,96,2560]{2,1,0:T(8,128)(2,1)S(1)}, u32[]{:S(2)}, u32[]{:S(2)}) collective-permute-start(bf16[2,96,2560]{2,1,0:T(8,128)(2,1)} %get-tuple-element.119), channel_id=1, source_target_pairs={{0,2},{2,0},{4,6},{6,4},{8,10},{10,8},{12,14},{14,12},{1,3},{3,1},... | collective-permute-start | bytes 2949128 | tf_op jit(solution)/shard_map/ppermute | solution.py:24
  212.9 73.0 %collective-permute-start.10 = (bf16[2,96,2560]{2,1,0:T(8,128)(2,1)}, bf16[2,96,2560]{2,1,0:T(8,128)(2,1)}, u32[]{:S(2)}, u32[]{:S(2)}) collective-permute-start(bf16[2,96,2560]{2,1,0:T(8,128)(2,1)} %get-tuple-element.120), channel_id=1, source_target_pairs={{0,2},{2,0},{4,6},{6,4},{8,10},{10,8},{12,14},{14,12},{1,3},{3,1},... | collective-permute-start | bytes 2949128 | tf_op jit(solution)/shard_map/ppermute | solution.py:24
  285.9 69.1 %collective-permute-start.13 = (bf16[3,96,1792]{2,1,0:T(8,128)(2,1)}, bf16[3,96,1792]{2,1,0:T(8,128)(2,1)S(1)}, u32[]{:S(2)}, u32[]{:S(2)}) collective-permute-start(bf16[3,96,1792]{2,1,0:T(8,128)(2,1)} %get-tuple-element.127), channel_id=1, source_target_pairs={{0,8},{8,0},{2,10},{10,2},{4,12},{12,4},{6,14},{14,6},{1,9},{9,1},... | collective-permute-start | bytes 3096584 | tf_op jit(solution)/shard_map/ppermute | solution.py:24
  285.9 1.0 copy-start.3
  305.7 34.4 %collective-permute-start.14 = (bf16[2,48,2560]{2,1,0:T(8,128)(2,1)}, bf16[2,48,2560]{2,1,0:T(8,128)(2,1)S(1)}, u32[]{:S(2)}, u32[]{:S(2)}) collective-permute-start(bf16[2,48,2560]{2,1,0:T(8,128)(2,1)} %get-tuple-element.131), channel_id=1, source_target_pairs={{0,2},{2,0},{4,6},{6,4},{8,10},{10,8},{12,14},{14,12},{1,3},{3,1},... | collective-permute-start | bytes 1474568 | tf_op jit(solution)/shard_map/ppermute | solution.py:24
  307.2 32.9 %collective-permute-start.15 = (bf16[2,48,2560]{2,1,0:T(8,128)(2,1)}, bf16[2,48,2560]{2,1,0:T(8,128)(2,1)S(1)}, u32[]{:S(2)}, u32[]{:S(2)}) collective-permute-start(bf16[2,48,2560]{2,1,0:T(8,128)(2,1)} %get-tuple-element.132), channel_id=1, source_target_pairs={{0,2},{2,0},{4,6},{6,4},{8,10},{10,8},{12,14},{14,12},{1,3},{3,1},... | collective-permute-start | bytes 1474568 | tf_op jit(solution)/shard_map/ppermute | solution.py:24
  308.4 68.2 %collective-permute-start.17 = (bf16[3,96,1792]{2,1,0:T(8,128)(2,1)}, bf16[3,96,1792]{2,1,0:T(8,128)(2,1)}, u32[]{:S(2)}, u32[]{:S(2)}) collective-permute-start(bf16[3,96,1792]{2,1,0:T(8,128)(2,1)} %get-tuple-element.145), channel_id=1, source_target_pairs={{0,8},{8,0},{2,10},{10,2},{4,12},{12,4},{6,14},{14,6},{1,9},{9,1},... | collective-permute-start | bytes 3096584 | tf_op jit(solution)/shard_map/ppermute | solution.py:24
  326.9 46.5 %collective-permute-start.18 = (bf16[2,96,2560]{2,1,0:T(8,128)(2,1)}, bf16[2,96,2560]{2,1,0:T(8,128)(2,1)}, u32[]{:S(2)}, u32[]{:S(2)}) collective-permute-start(bf16[2,96,2560]{2,1,0:T(8,128)(2,1)} %get-tuple-element.146), channel_id=1, source_target_pairs={{0,2},{2,0},{4,6},{6,4},{8,10},{10,8},{12,14},{14,12},{1,3},{3,1},... | collective-permute-start | bytes 2949128 | tf_op jit(solution)/shard_map/ppermute | solution.py:24
  340.1 14.9 %copy-start.12 = (bf16[2,48,2560]{2,1,0:T(8,128)(2,1)}, bf16[2,48,2560]{2,1,0:T(8,128)(2,1)S(1)}, u32[]{:S(2)}) copy-start(bf16[2,48,2560]{2,1,0:T(8,128)(2,1)S(1)} %collective-permute-done.14.refs_5_) | copy-start | bytes 1474564
  340.1 14.9 %copy-start.13 = (bf16[2,48,2560]{2,1,0:T(8,128)(2,1)}, bf16[2,48,2560]{2,1,0:T(8,128)(2,1)S(1)}, u32[]{:S(2)}) copy-start(bf16[2,48,2560]{2,1,0:T(8,128)(2,1)S(1)} %collective-permute-done.15.refs_6_) | copy-start | bytes 1474564
  372.9 3.7 collective-permute-start.19
  372.9 3.6 collective-permute-start.20
  373.4 55.0 %collective-permute-start.16 = (bf16[2,96,2560]{2,1,0:T(8,128)(2,1)}, bf16[2,96,2560]{2,1,0:T(8,128)(2,1)}, u32[]{:S(2)}, u32[]{:S(2)}) collective-permute-start(bf16[2,96,2560]{2,1,0:T(8,128)(2,1)} %get-tuple-element.143), channel_id=1, source_target_pairs={{0,4},{4,0},{2,6},{6,2},{8,12},{12,8},{10,14},{14,10},{1,5},{5,1},... | collective-permute-start | bytes 2949128 | tf_op jit(solution)/shard_map/ppermute | solution.py:24
  376.6 1.0 copy-start.8
  394.5 33.9 %collective-permute-start.21 = (bf16[2,96,2560]{2,1,0:T(8,128)(2,1)}, bf16[2,96,2560]{2,1,0:T(8,128)(2,1)S(1)}, u32[]{:S(2)}, u32[]{:S(2)}) collective-permute-start(bf16[2,96,2560]{2,1,0:T(8,128)(2,1)} %get-tuple-element.150), channel_id=1, source_target_pairs={{0,4},{4,0},{2,6},{6,2},{8,12},{12,8},{10,14},{14,10},{1,5},{5,1},... | collective-permute-start | bytes 2949128 | tf_op jit(solution)/shard_map/ppermute | solution.py:24
  394.6 2.2 collective-permute-start.22
  394.7 2.8 collective-permute-start.23
  (8 other events, 7.2 us)

commit v5 on v4

--- a/solution.py
+++ b/solution.py
@@ -198,11 +198,11 @@
         )[0]
 
 
-def weight_specs(weights, kinds, first):
+def weight_specs(weights, kinds, first, tile=TILE):
     gate, up, down = weights
     depth = gate.shape[1]
-    wide = pl.BlockSpec((1, depth, TILE), lambda j: (0, 0, first + j))
-    tall = pl.BlockSpec((1, TILE, depth), lambda j: (0, first + j, 0))
+    wide = pl.BlockSpec((1, depth, tile), lambda j: (0, 0, first + j))
+    tall = pl.BlockSpec((1, tile, depth), lambda j: (0, first + j, 0))
     return [((gate, up, down)[kind], tall if kind == PRE else wide) for kind in kinds]
 
 
@@ -254,16 +254,19 @@
 def hidden_and_back(order, tiles, parts, weights, out_type, addend=(), cuts=None, twice=True):
     first, count = tiles
     copies, hqr_cuts = (2, 1) if twice else (1, 2)
+    tile = TILE
+    if not twice and count % 2 == 1 and count * TILE % 256 == 0:
+        tile, count = count * TILE // 2, 2
     sizes = [kept.shape[1] for kept, _ in parts]
     rows = sum(sizes)
     depth = weights[0].shape[1]
     inputs = []
     for pair, size in zip(parts, sizes):
-        spec = pl.BlockSpec((3, size, TILE), lambda j: (0, 0, j))
+        spec = pl.BlockSpec((3, size, tile), lambda j: (0, 0, j))
         inputs += [(array, spec) for array in pair]
     n = len(inputs)
     size = rows // hqr_cuts
-    inputs += weight_specs(weights, (G, U, PRE), first)
+    inputs += weight_specs(weights, (G, U, PRE), first, tile)
     inputs += [(array, pl.BlockSpec(array.shape, lambda j: (0, 0, 0))) for array in addend]
     cuts = cuts or [rows]
 
@@ -307,8 +310,8 @@
 
     outputs = [
         (
-            jax.ShapeDtypeStruct((copies, 3, size, count * TILE), jnp.bfloat16),
-            pl.BlockSpec((copies, 3, size, TILE), lambda j: (0, 0, 0, j)),
+            jax.ShapeDtypeStruct((copies, 3, size, count * tile), jnp.bfloat16),
+            pl.BlockSpec((copies, 3, size, tile), lambda j: (0, 0, 0, j)),
         )
     ] * hqr_cuts
     for cut in cuts:
@@ -316,7 +319,7 @@
         spec = pl.BlockSpec(shape, lambda j: (0, 0, 0))
         outputs.append((jax.ShapeDtypeStruct(shape, out_type), spec))
     scratch = [pltpu.VMEM((2, rows, depth), jnp.float32)]
-    return order.call(body, "hidden_and_back", 3 + 2.2 * count, count, inputs, outputs, scratch)
+    return order.call(body, "hidden_and_back", 3 + 2.2 * count * tile // TILE, count, inputs, outputs, scratch)
 
 
 def assemble(order, blocks):
@@ -557,10 +560,10 @@
     early_pieces = pieces_of([["near"]], [["c0", "c1"]])
     send("fa", ["ba", "bb"])
     finish("both", every, parts=["ba", "bb"], calls=3, cuts=[half // 2] * 2 + [half])
-    send("fb", ["bb"])
     *leading, trailing = sums["both"]
     both_sums = [[pass_on(array, near, 99) for array in leading]]
     first = weight_grads(order, side, chunks["c1"], early, early_pieces, width, into=first)
+    send("fb", ["bb"])
     both_sums.append([pass_on(order.hold(trailing, []), near, 99)])
     far_sums = []
     for name, addend in zip(("fa", "fb"), both_sums):

time: 436 us -> 436 us (level)
  no operation moved by 1% of the time
where the time goes in v5:
time: 436 us; the launch traced here: 434 us
  Pallas kernels  269 us (62%)
  blocking collectives  66.4 us (15%)
  waiting for transfers between devices  50.4 us (12%)
  starting transfers between devices  39.1 us (9%)
  local copies, waits for them, and re-layouts  7.81 us (2%)
    pallas_call x24, Pallas kernels, call(): pl.pallas_call(kernel, name=name, grid=(steps,), in_specs=[spec for _, sp...  269 us
    all_to_all x6, blocking collectives, both_replicas(): return lax.all_to_all(pair, 'dp', 0, 0, tiled=True)  66.4 us
    ppermute x24, waiting for transfers between devices, from_partner(): return lax.ppermute(block, axis, route)  49 us
    ppermute x24, starting transfers between devices, from_partner(): return lax.ppermute(block, axis, route)  28.7 us
    all_to_all x2, starting transfers between devices, both_replicas(): return lax.all_to_all(pair, 'dp', 0, 0, tiled=True)  10.4 us
  transfers between devices with their start and end apart: 26, of which 9 were waited for; matrix products, arithmetic and copies ran while one was open for 0% of the time, Pallas kernels for 61%

profile of v5, /device:TPU:0, one launch (start us, length us, event | category | flops | bytes accessed | tf_op | source)
XLA Modules:
  0.0 434.1 jit_solution(14081655678935140207)
XLA Ops:
  0.6 3.0 collective-permute-start.2
  3.8 11.5 %partials.5 = (f32[3,192,1024]{2,1,0:T(8,128)}, bf16[3,192,1024]{2,1,0:T(8,128)(2,1)}, f32[8,128]{1,0:T(8,128)}) custom-call(bf16[1,1,192,2560]{3,2,1,0:T(8,128)(2,1)} %refs_1_.5, bf16[1,1,192,2560]{3,2,1,0:T(8,128)(2,1)} %refs_1_.5, bf16[1,1,192,2560]{3,2,1,0:T(8,128)(2,1)} %refs_2_.15, bf16[1,2560,1792]{2,1,0:T(8,128)(2,1)} %refs_2_.14, ...), custom_call_target="tpu_custom_call" | custom-call | flops 2520000000 | tf_op jit(solution)/shard_map/partials/pallas_call | solution.py:175
  15.2 3.0 collective-permute-start
  20.3 11.6 %partials.6 = (f32[3,192,768]{2,1,0:T(8,128)}, bf16[3,192,768]{2,1,0:T(8,128)(2,1)}, bf16[2,2,192,2560]{3,2,1,0:T(8,128)(2,1)}, f32[8,128]{1,0:T(8,128)}) custom-call(bf16[1,1,192,2560]{3,2,1,0:T(8,128)(2,1)} %refs_1_.5, bf16[1,1,192,2560]{3,2,1,0:T(8,128)(2,1)} %refs_1_.5, bf16[1,1,192,2560]{3,2,1,0:T(8,128)(2,1)} %refs_2_.15, ...), custom_call_target="tpu_custom_call" | custom-call | flops 2040000000 | tf_op jit(solution)/shard_map/partials/pallas_call | solution.py:175
  31.9 11.5 %all_to_all.40.refs_7_.refs_2_.refs_3_ = bf16[2,2,192,2560]{3,2,1,0:T(8,128)(2,1)} all-to-all(bf16[2,2,192,2560]{3,2,1,0:T(8,128)(2,1)} %get-tuple-element.91), channel_id=1, replica_groups=mesh['groups'=2,'grid'=8,'dp'=2] {'dp'}, dimensions={0} | all-to-all | bytes 7864320 | tf_op jit(solution)/shard_map/all_to_all | solution.py:504
  43.4 3.4 collective-permute-done.3.refs_2_
  46.8 19.6 %partials.7 = (f32[3,192,1792]{2,1,0:T(8,128)}, bf16[3,192,1792]{2,1,0:T(8,128)(2,1)}, bf16[2,2,192,2560]{3,2,1,0:T(8,128)(2,1)}, f32[8,128]{1,0:T(8,128)}) custom-call(bf16[1,1,192,2560]{3,2,1,0:T(8,128)(2,1)} %collective-permute-done.2.refs_0_.refs_1_, bf16[1,1,192,2560]{3,2,1,0:T(8,128)(2,1)} %collective-permute-done.2.refs_0_.refs_1_, ...), custom_call_target="tpu_custom_call" | custom-call | flops 3960000000 | tf_op jit(solution)/shard_map/partials/pallas_call | solution.py:175
  69.3 11.5 %all_to_all.41.refs_6_.refs_0_.refs_1_ = bf16[2,2,192,2560]{3,2,1,0:T(8,128)(2,1)} all-to-all(bf16[2,2,192,2560]{3,2,1,0:T(8,128)(2,1)} %get-tuple-element.93), channel_id=1, replica_groups=mesh['groups'=2,'grid'=8,'dp'=2] {'dp'}, dimensions={0} | all-to-all | bytes 7864320 | tf_op jit(solution)/shard_map/all_to_all | solution.py:504
  80.8 12.6 %hidden_and_back.6 = (bf16[2,3,192,1024]{3,2,1,0:T(8,128)(2,1)}, f32[2,192,2560]{2,1,0:T(8,128)}, f32[8,128]{1,0:T(8,128)}) custom-call(f32[3,192,1024]{2,1,0:T(8,128)} %get-tuple-element.89.refs_0_, bf16[3,192,1024]{2,1,0:T(8,128)(2,1)} %collective-permute-done.refs_1_, bf16[1,2560,1792]{2,1,0:T(8,128)(2,1)} %refs_2_.14, bf16[1,2560,1792]{2,1,0:T(8,128)(2,1)} %refs_3_.19, ...), custom_call_target="tpu_custom_call" | custom-call | flops 2200000000 | tf_op jit(solution)/shard_map/hidden_and_back/pallas_call | solution.py:175
  93.4 4.9 %all-to-all-start.2 = ((bf16[2,3,192,1024]{3,2,1,0:T(8,128)(2,1)}), bf16[2,3,192,1024]{3,2,1,0:T(8,128)(2,1)}, u32[]{:S(2)}, u32[]{:S(2)}) async-start(bf16[2,3,192,1024]{3,2,1,0:T(8,128)(2,1)} %get-tuple-element.97), calls=%async_computation.2 | async-start | bytes 4718592 | tf_op jit(solution)/shard_map/all_to_all | solution.py:504
  99.9 4.0 collective-permute-done.4.refs_0_
  106.5 19.6 %partials.8 = (f32[3,96,1792]{2,1,0:T(8,128)}, bf16[3,96,1792]{2,1,0:T(8,128)(2,1)}, f32[3,96,1792]{2,1,0:T(8,128)}, bf16[3,96,1792]{2,1,0:T(8,128)(2,1)}, bf16[...) custom-call(bf16[1,1,192,2560]{3,2,1,0:T(8,128)(2,1)} %get-tuple-element.95.refs_0_.refs_1_, ...), custom_call_target="tpu_custom_call" | custom-call | flops 3960000000 | tf_op jit(solution)/shard_map/partials/pallas_call | solution.py:175
  126.0 11.6 %all_to_all.42.refs_3_.refs_2_ = bf16[2,2,192,2560]{3,2,1,0:T(8,128)(2,1)} all-to-all(bf16[2,2,192,2560]{3,2,1,0:T(8,128)(2,1)} %get-tuple-element.101), channel_id=1, replica_groups=mesh['groups'=2,'grid'=8,'dp'=2] {'dp'}, dimensions={0} | all-to-all | bytes 7864320 | tf_op jit(solution)/shard_map/all_to_all | solution.py:504
  138.2 10.0 %assemble.2 = (bf16[2560,768]{1,0:T(8,128)(2,1)}, bf16[768,2560]{1,0:T(8,128)(2,1)}, f32[8,128]{1,0:T(8,128)}) custom-call(bf16[2,2,192,2560]{3,2,1,0:T(8,128)(2,1)} %all_to_all.41.refs_6_.refs_0_.refs_1_, bf16[2,2,192,2560]{3,2,1,0:T(8,128)(2,1)} %all_to_all.41.refs_6_.refs_0_.refs_1_, bf16[2,2,192,2560]{3,2,1,0:T(8,128)(2,1)} %all_to_all.40.refs_7_.refs_2_.refs_3_, ...), custom_call_target="tpu_custom_call" | custom-call | flops 2000000000 | tf_op jit(solution)/shard_map/assemble/pallas_call | solution.py:175
  149.5 19.5 %partials.9 = (f32[3,96,1792]{2,1,0:T(8,128)}, bf16[3,96,1792]{2,1,0:T(8,128)(2,1)}, f32[3,96,1792]{2,1,0:T(8,128)}, bf16[3,96,1792]{2,1,0:T(8,128)(2,1)}, bf16[...) custom-call(bf16[1,1,192,2560]{3,2,1,0:T(8,128)(2,1)} %copy-done.4, bf16[1,1,192,2560]{3,2,1,0:T(8,128)(2,1)} %copy-done.4, ...), custom_call_target="tpu_custom_call" | custom-call | flops 3960000000 | tf_op jit(solution)/shard_map/partials/pallas_call | solution.py:175
  169.1 5.5 %all-to-all-start.4 = ((bf16[2,2,192,2560]{3,2,1,0:T(8,128)(2,1)}), bf16[2,2,192,2560]{3,2,1,0:T(8,128)(2,1)}, u32[]{:S(2)}, u32[]{:S(2)}) async-start(bf16[2,2,192,2560]{3,2,1,0:T(8,128)(2,1)} %get-tuple-element.111), calls=%async_computation.4 | async-start | bytes 7864320 | tf_op jit(solution)/shard_map/all_to_all | solution.py:504
  178.9 10.0 %assemble.3 = (bf16[2560,768]{1,0:T(8,128)(2,1)}, bf16[768,2560]{1,0:T(8,128)(2,1)}, f32[8,128]{1,0:T(8,128)}) custom-call(bf16[2,2,192,2560]{3,2,1,0:T(8,128)(2,1)} %all-to-all-done.4.refs_0_.refs_1_.refs_5_, bf16[2,2,192,2560]{3,2,1,0:T(8,128)(2,1)} %all-to-all-done.4.refs_0_.refs_1_.refs_5_, bf16[2,2,192,2560]{3,2,1,0:T(8,128)(2,1)} %all_to_all.42.refs_3_.refs_2_, ...), custom_call_target="tpu_custom_call" | custom-call | flops 2000000000 | tf_op jit(solution)/shard_map/assemble/pallas_call | solution.py:175
  192.4 18.7 %hidden_and_back.7 = (bf16[2,3,192,1792]{3,2,1,0:T(8,128)(2,1)}, bf16[2,96,2560]{2,1,0:T(8,128)(2,1)}, bf16[2,96,2560]{2,1,0:T(8,128)(2,1)}, f32[8,128]{1,0:T(8,128)}) custom-call(f32[3,192,1792]{2,1,0:T(8,128)} %get-tuple-element.107.refs_0_, bf16[3,192,1792]{2,1,0:T(8,128)(2,1)} %collective-permute-done.6.refs_1_, bf16[1,2560,1792]{2,1,0:T(8,128)(2,1)} %refs_2_.14, ...), custom_call_target="tpu_custom_call" | custom-call | flops 3600000000 | tf_op jit(solution)/shard_map/hidden_and_back/pallas_call | solution.py:175
  213.2 11.8 %all_to_all.43.refs_3_.refs_6_ = bf16[2,3,192,1792]{3,2,1,0:T(8,128)(2,1)} all-to-all(bf16[2,3,192,1792]{3,2,1,0:T(8,128)(2,1)} %get-tuple-element.115), channel_id=1, replica_groups=mesh['groups'=2,'grid'=8,'dp'=2] {'dp'}, dimensions={0} | all-to-all | bytes 8257536 | tf_op jit(solution)/shard_map/all_to_all | solution.py:504
  225.0 17.8 %weight_grads.3 = (bf16[1,2560,1792]{2,1,0:T(8,128)(2,1)}, bf16[1,2560,1792]{2,1,0:T(8,128)(2,1)}, bf16[1,1792,2560]{2,1,0:T(8,128)(2,1)}, f32[8,128]{1,0:T(8,128)}) custom-call(s32[1]{0:T(128)} %bitcast.refs_0_, bf16[2560,768]{1,0:T(8,128)(2,1)} %get-tuple-element.105.refs_1_, bf16[768,2560]{1,0:T(8,128)(2,1)} %get-tuple-element.106.refs_2_, ...), custom_call_target="tpu_custom_call" | custom-call | flops 2400000000 | tf_op jit(solution)/shard_map/weight_grads/pallas_call | solution.py:175
  242.8 12.8 %hidden_and_back.8 = (bf16[2,3,192,768]{3,2,1,0:T(8,128)(2,1)}, f32[2,192,2560]{2,1,0:T(8,128)}, f32[8,128]{1,0:T(8,128)}) custom-call(f32[3,192,768]{2,1,0:T(8,128)} %get-tuple-element.86.refs_0_, bf16[3,192,768]{2,1,0:T(8,128)(2,1)} %collective-permute-done.5.refs_1_, bf16[1,2560,1792]{2,1,0:T(8,128)(2,1)} %refs_2_.14, bf16[1,2560,1792]{2,1,0:T(8,128)(2,1)} %refs_3_.19, ...), custom_call_target="tpu_custom_call" | custom-call | flops 1800000000 | tf_op jit(solution)/shard_map/hidden_and_back/pallas_call | solution.py:175
  255.6 8.2 %all_to_all.44.refs_4_.refs_5_ = bf16[2,3,192,768]{3,2,1,0:T(8,128)(2,1)} all-to-all(bf16[2,3,192,768]{3,2,1,0:T(8,128)(2,1)} %get-tuple-element.126), channel_id=1, replica_groups=mesh['groups'=2,'grid'=8,'dp'=2] {'dp'}, dimensions={0} | all-to-all | bytes 3538944 | tf_op jit(solution)/shard_map/all_to_all | solution.py:504
  264.1 20.3 %collective-permute-done.12.refs_2_.refs_3_.refs_1_ = bf16[3,96,1792]{2,1,0:T(8,128)(2,1)S(1)} collective-permute-done((bf16[3,96,1792]{2,1,0:T(8,128)(2,1)}, bf16[3,96,1792]{2,1,0:T(8,128)(2,1)S(1)}, u32[]{:S(2)}, u32[]{:S(2)}) %collective-permute-start.12) | collective-permute-done | bytes 1032224 | tf_op jit(solution)/shard_map/ppermute | solution.py:24
  286.9 18.8 %hidden_and_back.9 = (bf16[2,3,192,1792]{3,2,1,0:T(8,128)(2,1)}, bf16[2,48,2560]{2,1,0:T(8,128)(2,1)}, bf16[2,48,2560]{2,1,0:T(8,128)(2,1)}, bf16[2,96,2560]{2,1,0:T(8,128)(2,1)}, f32[8,128]{1,0:T(8,128)}) custom-call(f32[3,96,1792]{2,1,0:T(8,128)} %get-tuple-element.128.refs_0_, bf16[3,96,1792]{2,1,0:T(8,128)(2,1)} %collective-permute-done.11.refs_1_, ...), custom_call_target="tpu_custom_call" | custom-call | flops 3600000000 | tf_op jit(solution)/shard_map/hidden_and_back/pallas_call | solution.py:175
  307.8 15.0 %weight_grads.4 = (bf16[1,2560,1792]{2,1,0:T(8,128)(2,1)}, bf16[1,2560,1792]{2,1,0:T(8,128)(2,1)}, bf16[1,1792,2560]{2,1,0:T(8,128)(2,1)}, f32[8,128]{1,0:T(8,128)}) custom-call(s32[1]{0:T(128)} %bitcast.refs_0_, bf16[2560,768]{1,0:T(8,128)(2,1)} %get-tuple-element.105.refs_1_, ...), custom_call_target="tpu_custom_call", output_to_operand_aliasing={{0}: (6, {}), {1}: (7, {}), {2}: (8, {})} | custom-call | flops 2000000000 | tf_op jit(solution)/shard_map/weight_grads/pallas_call | solution.py:175
  328.4 11.8 %all_to_all.45.refs_8_.refs_3_ = bf16[2,3,192,1792]{3,2,1,0:T(8,128)(2,1)} all-to-all(bf16[2,3,192,1792]{3,2,1,0:T(8,128)(2,1)} %get-tuple-element.142), channel_id=1, replica_groups=mesh['groups'=2,'grid'=8,'dp'=2] {'dp'}, dimensions={0} | all-to-all | bytes 8257536 | tf_op jit(solution)/shard_map/all_to_all | solution.py:504
  340.1 14.9 %collective-permute-done.13.refs_1_ = bf16[3,96,1792]{2,1,0:T(8,128)(2,1)S(1)} collective-permute-done((bf16[3,96,1792]{2,1,0:T(8,128)(2,1)}, bf16[3,96,1792]{2,1,0:T(8,128)(2,1)S(1)}, u32[]{:S(2)}, u32[]{:S(2)}) %collective-permute-start.13) | collective-permute-done | bytes 1032224 | tf_op jit(solution)/shard_map/ppermute | solution.py:24
  356.0 16.2 %hidden_and_back.10 = (bf16[1,3,48,1792]{3,2,1,0:T(8,128)(2,1)}, bf16[1,3,48,1792]{3,2,1,0:T(8,128)(2,1)}, bf16[2,96,2560]{2,1,0:T(8,128)(2,1)}, f32[8,128]{1,0:T(8,128)}) custom-call(f32[3,96,1792]{2,1,0:T(8,128)} %get-tuple-element.121.refs_0_, bf16[3,96,1792]{2,1,0:T(8,128)(2,1)} %copy-done.9, bf16[1,2560,1792]{2,1,0:T(8,128)(2,1)} %refs_2_.14, ...), custom_call_target="tpu_custom_call" | custom-call | flops 3600000000 | tf_op jit(solution)/shard_map/hidden_and_back/pallas_call | solution.py:175
  372.8 3.9 collective-permute-done.17.refs_1_
  377.6 16.3 %hidden_and_back.11 = (bf16[1,3,48,1792]{3,2,1,0:T(8,128)(2,1)}, bf16[1,3,48,1792]{3,2,1,0:T(8,128)(2,1)}, bf16[2,96,2560]{2,1,0:T(8,128)(2,1)}, f32[8,128]{1,0:T(8,128)}) custom-call(f32[3,96,1792]{2,1,0:T(8,128)} %get-tuple-element.144.refs_0_, bf16[3,96,1792]{2,1,0:T(8,128)(2,1)} %collective-permute-done.17.refs_1_, bf16[1,2560,1792]{2,1,0:T(8,128)(2,1)} %refs_2_.14, ...), custom_call_target="tpu_custom_call" | custom-call | flops 3600000000 | tf_op jit(solution)/shard_map/hidden_and_back/pallas_call | solution.py:175
  397.7 30.1 %weight_grads.5 = (bf16[1,2560,1792]{2,1,0:T(8,128)(2,1)}, bf16[1,2560,1792]{2,1,0:T(8,128)(2,1)}, bf16[1,1792,2560]{2,1,0:T(8,128)(2,1)}, f32[8,128]{1,0:T(8,128)}) custom-call(s32[1]{0:T(128)} %bitcast.refs_0_, bf16[2560,768]{1,0:T(8,128)(2,1)} %get-tuple-element.151.refs_1_, bf16[768,2560]{1,0:T(8,128)(2,1)} %get-tuple-element.152.refs_2_, ...), custom_call_target="tpu_custom_call" | custom-call | flops 3600000000 | tf_op jit(solution)/shard_map/weight_grads/pallas_call | solution.py:175
  428.8 5.1 %add_row_sums.1 = (bf16[1,1,192,2560]{3,2,1,0:T(8,128)(2,1)}, bf16[1,1,192,2560]{3,2,1,0:T(8,128)(2,1)}, f32[8,128]{1,0:T(8,128)}) custom-call(f32[2,192,2560]{2,1,0:T(8,128)} %get-tuple-element.118.refs_0_, bf16[1,1,192,2560]{3,2,1,0:T(8,128)(2,1)} %refs_1_.5, bf16[1,1,192,2560]{3,2,1,0:T(8,128)(2,1)} %refs_2_.15, bf16[2,96,2560]{2,1,0:T(8,128)(2,1)} %copy-done.3, ...), custom_call_target="tpu_custom_call" | custom-call | flops 1000000000 | tf_op jit(solution)/shard_map/add_row_sums/pallas_call | solution.py:175
  (78 shorter events, 38.6 us)
Async XLA Ops:
  0.6 17.6 %copy-start = (bf16[1,1,192,2560]{3,2,1,0:T(8,128)(2,1)S(1)}, bf16[1,1,192,2560]{3,2,1,0:T(8,128)(2,1)}, u32[]{:S(2)}) copy-start(bf16[1,1,192,2560]{3,2,1,0:T(8,128)(2,1)} %refs_1_.5) | copy-start | bytes 2949124
  0.6 42.8 %collective-permute-start.2 = (bf16[1,1,192,2560]{3,2,1,0:T(8,128)(2,1)}, bf16[1,1,192,2560]{3,2,1,0:T(8,128)(2,1)}, u32[]{:S(2)}, u32[]{:S(2)}) collective-permute-start(bf16[1,1,192,2560]{3,2,1,0:T(8,128)(2,1)} %refs_1_.5), channel_id=1, source_target_pairs={{0,2},{2,0},{4,6},{6,4},{8,10},{10,8},{12,14},{14,12},{1,3},{3,1},... | collective-permute-start | bytes 2949128 | tf_op jit(solution)/shard_map/ppermute | solution.py:24
  3.7 43.1 %collective-permute-start.3 = (bf16[1,1,192,2560]{3,2,1,0:T(8,128)(2,1)}, bf16[1,1,192,2560]{3,2,1,0:T(8,128)(2,1)}, u32[]{:S(2)}, u32[]{:S(2)}) collective-permute-start(bf16[1,1,192,2560]{3,2,1,0:T(8,128)(2,1)} %refs_2_.15), channel_id=1, source_target_pairs={{0,2},{2,0},{4,6},{6,4},{8,10},{10,8},{12,14},{14,12},{1,3},{3,1},... | collective-permute-start | bytes 2949128 | tf_op jit(solution)/shard_map/ppermute | solution.py:24
  15.2 65.6 %collective-permute-start = (bf16[3,192,1024]{2,1,0:T(8,128)(2,1)}, bf16[3,192,1024]{2,1,0:T(8,128)(2,1)}, u32[]{:S(2)}, u32[]{:S(2)}) collective-permute-start(bf16[3,192,1024]{2,1,0:T(8,128)(2,1)} %get-tuple-element.88), channel_id=1, source_target_pairs={{0,8},{8,0},{2,10},{10,2},{4,12},{12,4},{6,14},{14,6},{1,9},{9,1},... | collective-permute-start | bytes 3538952 | tf_op jit(solution)/shard_map/ppermute | solution.py:24
  18.2 80.1 %collective-permute-start.1 = (bf16[1,1,192,2560]{3,2,1,0:T(8,128)(2,1)S(1)}, bf16[1,1,192,2560]{3,2,1,0:T(8,128)(2,1)S(1)}, u32[]{:S(2)}, u32[]{:S(2)}) collective-permute-start(bf16[1,1,192,2560]{3,2,1,0:T(8,128)(2,1)S(1)} %copy-done), channel_id=1, source_target_pairs={{0,4},{4,0},{2,6},{6,2},{8,12},{12,8},{10,14},{14,10},{1,5},{5,1},... | collective-permute-start | bytes 2949128 | tf_op jit(solution)/shard_map/ppermute | solution.py:24
  19.8 84.1 %collective-permute-start.4 = (bf16[1,1,192,2560]{3,2,1,0:T(8,128)(2,1)}, bf16[1,1,192,2560]{3,2,1,0:T(8,128)(2,1)}, u32[]{:S(2)}, u32[]{:S(2)}) collective-permute-start(bf16[1,1,192,2560]{3,2,1,0:T(8,128)(2,1)} %refs_2_.15), channel_id=1, source_target_pairs={{0,4},{4,0},{2,6},{6,2},{8,12},{12,8},{10,14},{14,10},{1,5},{5,1},... | collective-permute-start | bytes 2949128 | tf_op jit(solution)/shard_map/ppermute | solution.py:24
  66.4 122.5 %collective-permute-start.6 = (bf16[3,192,1792]{2,1,0:T(8,128)(2,1)}, bf16[3,192,1792]{2,1,0:T(8,128)(2,1)}, u32[]{:S(2)}, u32[]{:S(2)}) collective-permute-start(bf16[3,192,1792]{2,1,0:T(8,128)(2,1)} %get-tuple-element.108), channel_id=1, source_target_pairs={{0,8},{8,0},{2,10},{10,2},{4,12},{12,4},{6,14},{14,6},{1,9},{9,1},... | collective-permute-start | bytes 6193160 | tf_op jit(solution)/shard_map/ppermute | solution.py:24
  93.4 10.4 %all-to-all-start.2 = ((bf16[2,3,192,1024]{3,2,1,0:T(8,128)(2,1)}), bf16[2,3,192,1024]{3,2,1,0:T(8,128)(2,1)}, u32[]{:S(2)}, u32[]{:S(2)}) async-start(bf16[2,3,192,1024]{3,2,1,0:T(8,128)(2,1)} %get-tuple-element.97), calls=%async_computation.2 | async-start | bytes 4718592 | tf_op jit(solution)/shard_map/all_to_all | solution.py:504
  104.5 43.8 %collective-permute-start.8 = (bf16[1,1,192,2560]{3,2,1,0:T(8,128)(2,1)}, bf16[1,1,192,2560]{3,2,1,0:T(8,128)(2,1)S(1)}, u32[]{:S(2)}, u32[]{:S(2)}) collective-permute-start(bf16[1,1,192,2560]{3,2,1,0:T(8,128)(2,1)} %get-tuple-element.98.refs_2_), channel_id=1, source_target_pairs={{0,2},{2,0},{4,6},{6,4},{8,10},{10,8},{12,14},{14,12},{1,3},{3,1},... | collective-permute-start | bytes 2949128 | tf_op jit(solution)/shard_map/ppermute | solution.py:24
  106.1 42.1 %collective-permute-start.7 = (bf16[1,1,192,2560]{3,2,1,0:T(8,128)(2,1)}, bf16[1,1,192,2560]{3,2,1,0:T(8,128)(2,1)S(1)}, u32[]{:S(2)}, u32[]{:S(2)}) collective-permute-start(bf16[1,1,192,2560]{3,2,1,0:T(8,128)(2,1)} %get-tuple-element.95.refs_0_.refs_1_), channel_id=1, source_target_pairs={{0,2},{2,0},{4,6},{6,4},{8,10},{10,8},{12,14},{14,12},{1,3},{3,1},... | collective-permute-start | bytes 2949128 | tf_op jit(solution)/shard_map/ppermute | solution.py:24
  138.2 104.6 %collective-permute-start.5 = (bf16[3,192,768]{2,1,0:T(8,128)(2,1)}, bf16[3,192,768]{2,1,0:T(8,128)(2,1)}, u32[]{:S(2)}, u32[]{:S(2)}) collective-permute-start(bf16[3,192,768]{2,1,0:T(8,128)(2,1)} %get-tuple-element.102), channel_id=1, source_target_pairs={{0,8},{8,0},{2,10},{10,2},{4,12},{12,4},{6,14},{14,6},{1,9},{9,1},... | collective-permute-start | bytes 2654216 | tf_op jit(solution)/shard_map/ppermute | solution.py:24
  148.3 1.2 copy-start.4
  169.1 9.8 %all-to-all-start.4 = ((bf16[2,2,192,2560]{3,2,1,0:T(8,128)(2,1)}), bf16[2,2,192,2560]{3,2,1,0:T(8,128)(2,1)}, u32[]{:S(2)}, u32[]{:S(2)}) async-start(bf16[2,2,192,2560]{3,2,1,0:T(8,128)(2,1)} %get-tuple-element.111), calls=%async_computation.4 | async-start | bytes 7864320 | tf_op jit(solution)/shard_map/all_to_all | solution.py:504
  174.6 89.5 %collective-permute-start.11 = (bf16[3,96,1792]{2,1,0:T(8,128)(2,1)}, bf16[3,96,1792]{2,1,0:T(8,128)(2,1)}, u32[]{:S(2)}, u32[]{:S(2)}) collective-permute-start(bf16[3,96,1792]{2,1,0:T(8,128)(2,1)} %get-tuple-element.123), channel_id=1, source_target_pairs={{0,8},{8,0},{2,10},{10,2},{4,12},{12,4},{6,14},{14,6},{1,9},{9,1},... | collective-permute-start | bytes 3096584 | tf_op jit(solution)/shard_map/ppermute | solution.py:24
  189.5 94.9 %collective-permute-start.12 = (bf16[3,96,1792]{2,1,0:T(8,128)(2,1)}, bf16[3,96,1792]{2,1,0:T(8,128)(2,1)S(1)}, u32[]{:S(2)}, u32[]{:S(2)}) collective-permute-start(bf16[3,96,1792]{2,1,0:T(8,128)(2,1)} %get-tuple-element.124), channel_id=1, source_target_pairs={{0,8},{8,0},{2,10},{10,2},{4,12},{12,4},{6,14},{14,6},{1,9},{9,1},... | collective-permute-start | bytes 3096584 | tf_op jit(solution)/shard_map/ppermute | solution.py:24
  211.1 74.8 %collective-permute-start.9 = (bf16[2,96,2560]{2,1,0:T(8,128)(2,1)}, bf16[2,96,2560]{2,1,0:T(8,128)(2,1)S(1)}, u32[]{:S(2)}, u32[]{:S(2)}) collective-permute-start(bf16[2,96,2560]{2,1,0:T(8,128)(2,1)} %get-tuple-element.119), channel_id=1, source_target_pairs={{0,2},{2,0},{4,6},{6,4},{8,10},{10,8},{12,14},{14,12},{1,3},{3,1},... | collective-permute-start | bytes 2949128 | tf_op jit(solution)/shard_map/ppermute | solution.py:24
  212.9 73.0 %collective-permute-start.10 = (bf16[2,96,2560]{2,1,0:T(8,128)(2,1)}, bf16[2,96,2560]{2,1,0:T(8,128)(2,1)}, u32[]{:S(2)}, u32[]{:S(2)}) collective-permute-start(bf16[2,96,2560]{2,1,0:T(8,128)(2,1)} %get-tuple-element.120), channel_id=1, source_target_pairs={{0,2},{2,0},{4,6},{6,4},{8,10},{10,8},{12,14},{14,12},{1,3},{3,1},... | collective-permute-start | bytes 2949128 | tf_op jit(solution)/shard_map/ppermute | solution.py:24
  285.9 69.1 %collective-permute-start.13 = (bf16[3,96,1792]{2,1,0:T(8,128)(2,1)}, bf16[3,96,1792]{2,1,0:T(8,128)(2,1)S(1)}, u32[]{:S(2)}, u32[]{:S(2)}) collective-permute-start(bf16[3,96,1792]{2,1,0:T(8,128)(2,1)} %get-tuple-element.127), channel_id=1, source_target_pairs={{0,8},{8,0},{2,10},{10,2},{4,12},{12,4},{6,14},{14,6},{1,9},{9,1},... | collective-permute-start | bytes 3096584 | tf_op jit(solution)/shard_map/ppermute | solution.py:24
  285.9 1.0 copy-start.3
  305.7 34.4 %collective-permute-start.14 = (bf16[2,48,2560]{2,1,0:T(8,128)(2,1)}, bf16[2,48,2560]{2,1,0:T(8,128)(2,1)S(1)}, u32[]{:S(2)}, u32[]{:S(2)}) collective-permute-start(bf16[2,48,2560]{2,1,0:T(8,128)(2,1)} %get-tuple-element.131), channel_id=1, source_target_pairs={{0,2},{2,0},{4,6},{6,4},{8,10},{10,8},{12,14},{14,12},{1,3},{3,1},... | collective-permute-start | bytes 1474568 | tf_op jit(solution)/shard_map/ppermute | solution.py:24
  307.2 32.9 %collective-permute-start.15 = (bf16[2,48,2560]{2,1,0:T(8,128)(2,1)}, bf16[2,48,2560]{2,1,0:T(8,128)(2,1)S(1)}, u32[]{:S(2)}, u32[]{:S(2)}) collective-permute-start(bf16[2,48,2560]{2,1,0:T(8,128)(2,1)} %get-tuple-element.132), channel_id=1, source_target_pairs={{0,2},{2,0},{4,6},{6,4},{8,10},{10,8},{12,14},{14,12},{1,3},{3,1},... | collective-permute-start | bytes 1474568 | tf_op jit(solution)/shard_map/ppermute | solution.py:24
  323.4 53.2 %collective-permute-start.17 = (bf16[3,96,1792]{2,1,0:T(8,128)(2,1)}, bf16[3,96,1792]{2,1,0:T(8,128)(2,1)}, u32[]{:S(2)}, u32[]{:S(2)}) collective-permute-start(bf16[3,96,1792]{2,1,0:T(8,128)(2,1)} %get-tuple-element.145), channel_id=1, source_target_pairs={{0,8},{8,0},{2,10},{10,2},{4,12},{12,4},{6,14},{14,6},{1,9},{9,1},... | collective-permute-start | bytes 3096584 | tf_op jit(solution)/shard_map/ppermute | solution.py:24
  326.9 45.8 %collective-permute-start.18 = (bf16[2,96,2560]{2,1,0:T(8,128)(2,1)}, bf16[2,96,2560]{2,1,0:T(8,128)(2,1)}, u32[]{:S(2)}, u32[]{:S(2)}) collective-permute-start(bf16[2,96,2560]{2,1,0:T(8,128)(2,1)} %get-tuple-element.146), channel_id=1, source_target_pairs={{0,2},{2,0},{4,6},{6,4},{8,10},{10,8},{12,14},{14,12},{1,3},{3,1},... | collective-permute-start | bytes 2949128 | tf_op jit(solution)/shard_map/ppermute | solution.py:24
  340.1 14.9 %copy-start.12 = (bf16[2,48,2560]{2,1,0:T(8,128)(2,1)}, bf16[2,48,2560]{2,1,0:T(8,128)(2,1)S(1)}, u32[]{:S(2)}) copy-start(bf16[2,48,2560]{2,1,0:T(8,128)(2,1)S(1)} %collective-permute-done.14.refs_5_) | copy-start | bytes 1474564
  340.1 14.9 %copy-start.13 = (bf16[2,48,2560]{2,1,0:T(8,128)(2,1)}, bf16[2,48,2560]{2,1,0:T(8,128)(2,1)S(1)}, u32[]{:S(2)}) copy-start(bf16[2,48,2560]{2,1,0:T(8,128)(2,1)S(1)} %collective-permute-done.15.refs_6_) | copy-start | bytes 1474564
  372.2 4.5 %collective-permute-start.19 = (bf16[1,3,48,1792]{3,2,1,0:T(8,128)(2,1)}, bf16[1,3,48,1792]{3,2,1,0:T(8,128)(2,1)S(1)}, u32[]{:S(2)}, u32[]{:S(2)}) collective-permute-start(bf16[1,3,48,1792]{3,2,1,0:T(8,128)(2,1)} %get-tuple-element.148.refs_4_), channel_id=1, source_target_pairs={{0,1},{1,0},{2,3},{3,2},{4,5},{5,4},{6,7},{7,6},{8,9},{9,8},{10,11... | collective-permute-start | bytes 1548296 | tf_op jit(solution)/shard_map/ppermute | solution.py:24
  372.3 4.4 %collective-permute-start.20 = (bf16[1,3,48,1792]{3,2,1,0:T(8,128)(2,1)}, bf16[1,3,48,1792]{3,2,1,0:T(8,128)(2,1)S(1)}, u32[]{:S(2)}, u32[]{:S(2)}) collective-permute-start(bf16[1,3,48,1792]{3,2,1,0:T(8,128)(2,1)} %get-tuple-element.149.refs_6_), channel_id=1, source_target_pairs={{0,1},{1,0},{2,3},{3,2},{4,5},{5,4},{6,7},{7,6},{8,9},{9,8},{10,11... | collective-permute-start | bytes 1548296 | tf_op jit(solution)/shard_map/ppermute | solution.py:24
  372.8 55.1 %collective-permute-start.16 = (bf16[2,96,2560]{2,1,0:T(8,128)(2,1)}, bf16[2,96,2560]{2,1,0:T(8,128)(2,1)}, u32[]{:S(2)}, u32[]{:S(2)}) collective-permute-start(bf16[2,96,2560]{2,1,0:T(8,128)(2,1)} %get-tuple-element.143), channel_id=1, source_target_pairs={{0,4},{4,0},{2,6},{6,2},{8,12},{12,8},{10,14},{14,10},{1,5},{5,1},... | collective-permute-start | bytes 2949128 | tf_op jit(solution)/shard_map/ppermute | solution.py:24
  376.7 1.0 copy-start.8
  393.9 33.9 %collective-permute-start.21 = (bf16[2,96,2560]{2,1,0:T(8,128)(2,1)}, bf16[2,96,2560]{2,1,0:T(8,128)(2,1)S(1)}, u32[]{:S(2)}, u32[]{:S(2)}) collective-permute-start(bf16[2,96,2560]{2,1,0:T(8,128)(2,1)} %get-tuple-element.150), channel_id=1, source_target_pairs={{0,4},{4,0},{2,6},{6,2},{8,12},{12,8},{10,14},{14,10},{1,5},{5,1},... | collective-permute-start | bytes 2949128 | tf_op jit(solution)/shard_map/ppermute | solution.py:24
  394.0 2.2 collective-permute-start.22
  394.1 2.8 collective-permute-start.23
  (8 other events, 7.2 us)
